TPU v7x, 32 devices: a whole 2x2x4 slice. The times are simulated.
32 devices in a mesh: rep: 2 (over x), adp: 16 (over z, y, core).
Axes of the slice: x: 2, y: 2, z: 4, core: 2. Of those that a mesh axis runs over, the one named last changes fastest.
Arguments:
- tokens: bfloat16 [768, 8192], P('rep', 'adp'), parts along dimension 0, may hold values from -6 to 6
- request_adapter: int32 [768, 1], P('rep'), parts along dimension 0, may hold values from 0 to 15
- adapter_storage_slot: int32 [16], replicated, may hold values from 0 to 15, each once
- cache_length: int32 [768], P(('rep', 'adp')), parts along dimension 0, may hold values from 2 to 128, as said below
- query_weight: bfloat16 [8192, 8192], P(None, 'adp'), may hold values from -0.0625 to 0.0625
- adapter_down_maps: bfloat16 [16, 8192, 64], P('adp'), may hold values from -0.0625 to 0.0625
- adapter_up_maps: bfloat16 [16, 8192, 64], P('adp'), may hold values from -0.75 to 0.75
- key_cache: bfloat16 [8, 768, 128, 128], P(None, ('rep', 'adp')), parts along dimension 1, may hold values from -250 to 250
- value_cache: bfloat16 [8, 768, 128, 128], P(None, ('rep', 'adp')), parts along dimension 1, may hold values from -6 to 6
- new_token_key: bfloat16 [768, 1024], P(('rep', 'adp')), parts along dimension 0, may hold values from -6 to 6
- new_token_value: bfloat16 [768, 1024], P(('rep', 'adp')), parts along dimension 0, may hold values from -6 to 6
- output_weight: bfloat16 [8192, 8192], P('adp'), may hold values from -0.09375 to 0.09375
Outputs:
- attn_out: bfloat16 [768, 8192], P('rep', 'adp'), parts along dimension 0
There are 2 independent parts, one for each index of `rep`. A program takes and returns all parts, laid end to end along the dimension named above; an argument that names none is the same for every part. Nothing has to cross between parts.
Inputs may be any that keep to these rules, and one draw needn't show every extreme that they name: `request_adapter`: every adapter is named by some request of a group. `adapter_storage_slot`: each adapter id has its own slot. `cache_length`: some request holds exactly 128 positions.
All inputs are finite; a program needn't handle non-finite values.
Results may differ from a plain program's by a relative error of at most 0.011.
Values may be sent and summed in bfloat16 or wider, within the bound.
No kernel may reach another device: no remote copies, remote signals or barrier semaphores. Data moves between devices by JAX's collectives and lax.ppermute only.
A program may use at most 128 MiB of HBM per device.

v0:
```python
import jax
import jax.numpy as jnp
from jax import lax
from jax.experimental import pallas as pl
from jax.experimental.pallas import tpu as pltpu
from jax.sharding import Mesh
from jax.sharding import PartitionSpec as P

HEADS = 64
HEAD_DIM = 128
ADP = ("z", "y", "core")
NT = (((1,), (1,)), ((), ()))
VMEM_LIMIT = 56 << 20


def slices_kernel(core, query_weight, down, output_weight, query_out, down_out, out_out, sems):
    chips, width = query_out.shape[0], query_out.shape[1]
    copies = []
    for k in range(chips):
        span = pl.ds(pl.multiple_of((2 * k + 1 - core[0]) * width, width), width)
        copies += [
            pltpu.make_async_copy(query_weight.at[span, :], query_out.at[k], sems.at[0, k]),
            pltpu.make_async_copy(down.at[0, :, span], down_out.at[k], sems.at[1, k]),
            pltpu.make_async_copy(output_weight.at[:, span], out_out.at[k], sems.at[2, k]),
        ]
    for copy in copies:
        copy.start()
    for copy in copies:
        copy.wait()


def other_slices(core, query_weight, down, output_weight, chips, width):
    cols, rank, depth = query_weight.shape[1], down.shape[1], output_weight.shape[0]
    shapes = [(chips, width, cols), (chips, rank, width), (chips, depth, width)]
    hbm = pl.BlockSpec(memory_space=pl.ANY)
    return pl.pallas_call(
        slices_kernel,
        in_specs=[pl.BlockSpec(memory_space=pltpu.SMEM), hbm, hbm, hbm],
        out_specs=[hbm] * 3,
        out_shape=[jax.ShapeDtypeStruct(shape, query_weight.dtype) for shape in shapes],
        scratch_shapes=[pltpu.SemaphoreType.DMA((3, chips))],
        cost_estimate=pl.CostEstimate(
            flops=0,
            bytes_accessed=4 * chips * width * (cols + rank + depth),
            transcendentals=0,
        ),
    )(core, query_weight, down, output_weight)


def project_kernel(places, *refs):
    count = places.shape[0] // 2
    blocks, w_own, w_other, a_own, a_other = (refs[i * count : (i + 1) * count] for i in range(5))
    own_out, sent_out = refs[-2:]
    cols = own_out.shape[1]
    first_core = places[0] % 2 == 0
    own = other = low = None
    if len(refs) > 5 * count + 2:
        own = refs[5 * count][...]
        other = refs[5 * count + 1][:, :cols]
        low = refs[5 * count + 1][:, cols:]
    for i in range(count):
        x = blocks[i][...]
        d_own, d_other = a_own[i][0], a_other[i][0]
        pair = jnp.concatenate(
            [jnp.where(first_core, d_own, d_other), jnp.where(first_core, d_other, d_own)], axis=0
        )
        parts = (
            jnp.dot(x, w_own[i][...], preferred_element_type=jnp.float32),
            jnp.dot(x, w_other[i][0], preferred_element_type=jnp.float32),
            lax.dot_general(x, pair, NT, preferred_element_type=jnp.float32),
        )
        own, other, low = parts if own is None else (own + parts[0], other + parts[1], low + parts[2])
    own_out[...] = own
    sent_out[:, :cols] = other
    sent_out[:, cols:] = low


def project(chips, core, blocks, weight, weight_other, down, down_other, sums):
    count = len(blocks)
    rows, width = blocks[0].shape
    cols, rank = weight.shape[1], down.shape[1]
    places = jnp.stack([2 * chip + core for chip in chips] + chips).astype(jnp.int32)
    flat = lambda shape: pl.BlockSpec(shape, lambda j, p: (0, 0))
    sum_shapes = [(rows, cols), (rows, cols + 2 * rank)]
    each = range(count)
    return pl.pallas_call(
        project_kernel,
        grid_spec=pltpu.PrefetchScalarGridSpec(
            num_scalar_prefetch=1,
            grid=(1,),
            in_specs=[flat((rows, width))] * count
            + [pl.BlockSpec((width, cols), lambda j, p, i=i: (p[i], 0)) for i in each]
            + [pl.BlockSpec((1, width, cols), lambda j, p, i=i: (p[count + i], 0, 0)) for i in each]
            + [pl.BlockSpec((1, rank, width), lambda j, p, i=i: (0, 0, p[i])) for i in each]
            + [pl.BlockSpec((1, rank, width), lambda j, p, i=i: (p[count + i], 0, 0)) for i in each]
            + [flat(shape) for shape in sum_shapes[: len(sums)]],
            out_specs=[flat(shape) for shape in sum_shapes],
        ),
        out_shape=[jax.ShapeDtypeStruct(shape, jnp.float32) for shape in sum_shapes],
        compiler_params=pltpu.CompilerParams(vmem_limit_bytes=VMEM_LIMIT),
        cost_estimate=pl.CostEstimate(
            flops=4 * count * rows * width * (cols + rank),
            bytes_accessed=2 * count * width * (rows + 2 * cols) + 8 * rows * cols,
            transcendentals=0,
        ),
    )(
        places,
        *blocks,
        *[weight] * count,
        *[weight_other] * count,
        *[down] * count,
        *[down_other] * count,
        *sums,
    )


def query_kernel(half, own, received, low, slot, up_own, up_other, out):
    step = pl.program_id(0)
    cols, lanes = own.shape[1], low.shape[1]
    rank = lanes // 2
    part = rank // 2
    depth = up_own.shape[0]
    shape = (lanes, depth)
    lane = lax.broadcasted_iota(jnp.int32, shape, 1) % part
    row = lax.broadcasted_iota(jnp.int32, shape, 0)
    owner = lax.broadcasted_iota(jnp.int32, (own.shape[0], depth), 1) // part
    live = slot[...] == owner
    total = own[...] + received[:, :cols]
    for h, up in ((half[0], up_own), (1 - half[0], up_other)):
        copies = (row == lane + rank * step + part * h).astype(jnp.bfloat16)
        spread = jnp.dot(low[...], copies, preferred_element_type=jnp.float32)
        spread = jnp.where(live, spread, 0.0).astype(jnp.bfloat16)
        total += jnp.dot(spread, up[...], preferred_element_type=jnp.float32)
    out[...] = (total * HEAD_DIM ** (-0.5)).astype(out.dtype)


def make_query(half, own, received, low, slot, up_own, up_other):
    rows, cols = own.shape
    tile = rows // 2
    depth = up_own.shape[0]
    by_rows = lambda width: pl.BlockSpec((tile, width), lambda j, h: (j, 0))
    whole = lambda array: pl.BlockSpec(array.shape, lambda j, h: (0, 0))
    return pl.pallas_call(
        query_kernel,
        grid_spec=pltpu.PrefetchScalarGridSpec(
            num_scalar_prefetch=1,
            grid=(2,),
            in_specs=[
                by_rows(cols),
                by_rows(received.shape[1]),
                whole(low),
                by_rows(1),
                whole(up_own),
                whole(up_other),
            ],
            out_specs=by_rows(cols),
        ),
        out_shape=jax.ShapeDtypeStruct((rows, cols), jnp.bfloat16),
        compiler_params=pltpu.CompilerParams(vmem_limit_bytes=VMEM_LIMIT),
        cost_estimate=pl.CostEstimate(
            flops=4 * rows * cols * depth,
            bytes_accessed=rows * cols * 10 + 4 * depth * cols,
            transcendentals=0,
        ),
    )(half, own, received, low, slot, up_own, up_other)


def output_kernel(places, own, other, *refs):
    count = places.shape[0] // 2
    for w_own, w_other, out in zip(refs[:count], refs[count : 2 * count], refs[2 * count :]):
        total = jnp.dot(own[...], w_own[...], preferred_element_type=jnp.float32)
        total += jnp.dot(other[...], w_other[0], preferred_element_type=jnp.float32)
        out[...] = total.astype(out.dtype)


def output_partial(chips, core, own, other, weight, weight_other):
    rows, depth = own.shape
    width = weight_other.shape[2]
    count = len(chips)
    places = jnp.stack([2 * chip + core for chip in chips] + chips).astype(jnp.int32)
    whole = pl.BlockSpec((rows, depth), lambda j, p: (0, 0))
    return pl.pallas_call(
        output_kernel,
        grid_spec=pltpu.PrefetchScalarGridSpec(
            num_scalar_prefetch=1,
            grid=(1,),
            in_specs=[whole, whole]
            + [pl.BlockSpec((depth, width), lambda j, p, i=i: (0, p[i])) for i in range(count)]
            + [
                pl.BlockSpec((1, depth, width), lambda j, p, i=i: (p[count + i], 0, 0))
                for i in range(count)
            ],
            out_specs=[pl.BlockSpec((rows, width), lambda j, p: (0, 0))] * count,
        ),
        out_shape=[jax.ShapeDtypeStruct((rows, width), jnp.bfloat16)] * count,
        compiler_params=pltpu.CompilerParams(vmem_limit_bytes=VMEM_LIMIT),
        cost_estimate=pl.CostEstimate(
            flops=4 * count * rows * width * depth,
            bytes_accessed=2 * count * width * (rows + 2 * depth) + 4 * rows * depth,
            transcendentals=0,
        ),
    )(places, own, other, *[weight] * count, *[weight_other] * count)


def attention(query, cache_length, key_cache, value_cache, k_new, v_new):
    local_reqs = query.shape[0]
    kv_count, _, span, dim = key_cache.shape
    group = HEADS // kv_count
    query = query.reshape(local_reqs, kv_count, group, dim)
    k_new = k_new.reshape(local_reqs, kv_count, dim)
    v_new = v_new.reshape(local_reqs, kv_count, dim)
    live = (jnp.arange(span)[None, :] < cache_length[:, None])[None, :, None, :]
    scores = jnp.einsum("rkge,krje->krgj", query, key_cache, preferred_element_type=jnp.float32)
    fresh = jnp.einsum("rkge,rke->krg", query, k_new, preferred_element_type=jnp.float32)
    scores = jnp.where(live, scores, -jnp.inf)
    top = jnp.maximum(jnp.max(scores, axis=3), fresh)
    expd = jnp.where(live, jnp.exp(scores - top[:, :, :, None]), 0.0)
    expf = jnp.exp(fresh - top)
    total = jnp.sum(expd, axis=3) + expf
    probs = (expd / total[:, :, :, None]).astype(jnp.bfloat16)
    probf = (expf / total).astype(jnp.bfloat16)
    context = jnp.einsum("krgj,krje->rkge", probs, value_cache, preferred_element_type=jnp.float32)
    fresh_part = jnp.einsum("krg,rke->rkge", probf.astype(jnp.float32), v_new.astype(jnp.float32))
    return (context + fresh_part).astype(jnp.bfloat16).reshape(local_reqs, HEADS * dim)


def shift(value, axis, by):
    size = lax.axis_size(axis)
    return lax.ppermute(value, axis, [(i, (i + by) % size) for i in range(size)])


def after(value, *others):
    return lax.optimization_barrier((value, *others))[0]


def gather_layers(tokens):
    layers = lax.axis_size("z")
    if layers != 4:
        return [shift(tokens, "z", k) if k else tokens for k in range(layers)]
    below, above = shift(tokens, "z", 1), shift(tokens, "z", 3)
    two = lax.ppermute(below, "z", [(1, 2), (2, 3)]), lax.ppermute(above, "z", [(2, 1), (1, 0)])
    return [tokens, below, jnp.where(lax.axis_index("z") >= 2, *two), above]


def scatter_layers(parts):
    layers = lax.axis_size("z")
    wide = lambda value: value.astype(jnp.float32)
    narrow = lambda value: value.astype(jnp.bfloat16)
    if layers != 4:
        return sum([wide(shift(narrow(parts[k]), "z", k)) for k in range(1, layers)], parts[0])
    two = narrow(parts[2])
    up = lax.ppermute(two, "z", [(0, 1), (1, 2)])
    down = lax.ppermute(two, "z", [(3, 2), (2, 1)])
    above = shift(narrow(parts[1] + wide(up)), "z", 1)
    below = shift(narrow(parts[3] + wide(down)), "z", 3)
    return parts[0] + wide(above) + wide(below)


def shards(
    tokens,
    request_adapter,
    adapter_storage_slot,
    cache_length,
    query_weight,
    adapter_down_maps,
    adapter_up_maps,
    key_cache,
    value_cache,
    new_token_key,
    new_token_value,
    output_weight,
):
    layers, sides = lax.axis_size("z"), lax.axis_size("y")
    z, y, core = lax.axis_index("z"), lax.axis_index("y"), lax.axis_index("core")
    core_arg = core.astype(jnp.int32).reshape(1)
    rows, width = tokens.shape
    cols = query_weight.shape[1]
    total_adapters = adapter_storage_slot.shape[0]
    rank = adapter_down_maps.shape[2]
    chips_of = lambda layer: [
        (layer % layers) * sides + (y + side) % sides for side in range(sides)
    ]

    blocks = gather_layers(tokens)
    blocks = [
        [block, shift(block, "y", 1)] if sides == 2 else [block] for block in blocks
    ]

    down = jnp.swapaxes(adapter_down_maps, 1, 2)
    sent = other_slices(core_arg, query_weight, down, output_weight, layers * sides, width)
    query_weight_other, down_other, output_weight_other = [shift(s, "core", 1) for s in sent]

    reps = lax.axis_size("rep")
    half = lax.axis_index("rep") % 2
    up = jnp.swapaxes(adapter_up_maps, 1, 2)[0]
    up = lax.dynamic_slice_in_dim(up, half * (rank // 2), rank // 2, 0)
    up = after(up, blocks[1][0], blocks[layers - 1][0])
    up = lax.all_to_all(up, ADP, split_axis=1, concat_axis=0, tiled=True)
    up_other = lax.ppermute(up, "rep", [(i, i ^ 1) for i in range(reps)])

    ids = request_adapter[:, 0]
    numbers = jnp.arange(total_adapters, dtype=jnp.int32)
    slot = jnp.sum(
        jnp.where(ids[:, None] == numbers[None, :], adapter_storage_slot[None, :], 0), axis=1
    )[:, None]

    order = [0, 1, 3, 2] if layers == 4 else list(range(layers))
    sums = []
    for group in (order[:-1], order[-1:]):
        sums = project(
            [chip for k in group for chip in chips_of(z - k)],
            core,
            [block for k in group for block in blocks[k]],
            query_weight,
            query_weight_other,
            down,
            down_other,
            sums,
        )
    own, sent = sums
    received = shift(sent, "core", 1)

    low = sent[:, cols:] + received[:, cols:]
    chip = z * sides + y
    low = jnp.where(slot == 2 * chip, low[:, :rank], 0.0) + jnp.where(
        slot == 2 * chip + 1, low[:, rank:], 0.0
    )
    low = low.astype(jnp.bfloat16)
    low = jnp.concatenate([low[: rows // 2], low[rows // 2 :]], axis=1)
    if sides == 2:
        low = low + shift(low, "y", 1)
    low = sum([shift(low, "z", k) for k in range(1, layers)], low)

    query = make_query(half.astype(jnp.int32).reshape(1), own, received, low, slot, up, up_other)
    query_local = lax.all_to_all(query, ADP, split_axis=0, concat_axis=1, tiled=True)

    context = attention(
        query_local, cache_length, key_cache, value_cache, new_token_key, new_token_value
    )
    context = lax.all_to_all(context, ADP, split_axis=1, concat_axis=0, tiled=True)
    context_other = shift(context, "core", 1)

    parts = [None] * layers
    for k in [2, 1, 3, 0] if layers == 4 else list(range(1, layers)) + [0]:
        made = output_partial(
            chips_of(z + k), core, context, context_other, output_weight, output_weight_other
        )
        parts[k] = made[0].astype(jnp.float32)
        if sides == 2:
            parts[k] = parts[k] + shift(made[1], "y", 1).astype(jnp.float32)
    return scatter_layers(parts).astype(jnp.bfloat16)


def solution(mesh):
    reps, adp = mesh.shape["rep"], mesh.shape["adp"]
    sides = 2 if adp == 16 else 1
    mesh = Mesh(mesh.devices.reshape(reps, adp // (2 * sides), sides, 2), ("rep",) + ADP)
    in_specs = (
        P("rep", ADP),
        P("rep", None),
        P(),
        P(("rep",) + ADP),
        P(None, ADP),
        P(ADP, None, None),
        P(ADP, None, None),
        P(None, ("rep",) + ADP, None, None),
        P(None, ("rep",) + ADP, None, None),
        P(("rep",) + ADP, None),
        P(("rep",) + ADP, None),
        P(ADP, None),
    )
    return jax.shard_map(
        shards, mesh=mesh, in_specs=in_specs, out_specs=P("rep", ADP), check_vma=False
    )
```

profile of v0, /device:TPU:0, one launch (start us, length us, event | category | flops | bytes accessed | tf_op | source)
XLA Modules:
  0.0 482.3 jit_solution(1861860293357434551)
XLA Ops:
  0.0 271.3 %shard_map.118 = (bf16[8,512,512]{2,1,0:T(8,128)(2,1)}, bf16[8,64,512]{2,1,0:T(8,128)(2,1)}, bf16[8,512,512]{2,1,0:T(8,128)(2,1)}) custom-call(s32[1]{0:T(128)} %bitcast.9.core, bf16[8192,512]{1,0:T(8,128)(2,1)} %refs_3_.1, bf16[1,64,8192]{2,1,0:T(8,128)(2,1)} %bitcast.61, bf16[512,8192]{1,0:T(8,128)(2,1)} %refs_1_.7), custom_call_target="tpu_custom_call" | custom-call | bytes 17825792 | tf_op jit(solution)/shard_map/pallas_call | solution.py:36
  271.9 2.6 collective-permute-start
  274.5 2.1 collective-permute-start.2
  276.6 9.9 %collective-permute-done.refs_2_ = bf16[384,512]{1,0:T(8,128)(2,1)S(1)} collective-permute-done((bf16[384,512]{1,0:T(8,128)(2,1)S(1)}, bf16[384,512]{1,0:T(8,128)(2,1)S(1)}, u32[]{:S(2)}, u32[]{:S(2)}) %collective-permute-start) | collective-permute-done | bytes 393248 | tf_op jit(solution)/shard_map/ppermute | solution.py:229
  286.5 0.7 collective-permute-start.1
  287.2 6.9 %collective-permute-done.2.refs_4_ = bf16[384,512]{1,0:T(8,128)(2,1)S(1)} collective-permute-done((bf16[384,512]{1,0:T(8,128)(2,1)S(1)}, bf16[384,512]{1,0:T(8,128)(2,1)S(1)}, u32[]{:S(2)}, u32[]{:S(2)}) %collective-permute-start.2) | collective-permute-done | bytes 393248 | tf_op jit(solution)/shard_map/ppermute | solution.py:229
  294.1 1.3 collective-permute-start.3
  295.4 1.6 collective-permute-start.7
  297.0 0.6 collective-permute-start.8
  297.6 9.0 %collective-permute-done.3 = bf16[384,512]{1,0:T(8,128)(2,1)} collective-permute-done((bf16[384,512]{1,0:T(8,128)(2,1)S(1)}, bf16[384,512]{1,0:T(8,128)(2,1)}, u32[]{:S(2)}, u32[]{:S(2)}) %collective-permute-start.3) | collective-permute-done | bytes 393248 | tf_op jit(solution)/shard_map/ppermute | solution.py:241
  306.6 1.5 collective-permute-start.9
  308.1 1.0 broadcast_select_fusion.refs_0_
  309.2 0.6 collective-permute-start.4
  309.8 0.7 pad_add_fusion.1.places
  310.5 0.7 stack.124.places
  311.3 4.7 collective-permute-done.8.refs_3_
  316.1 8.4 %collective-permute-done.9.refs_5_ = bf16[384,512]{1,0:T(8,128)(2,1)} collective-permute-done((bf16[384,512]{1,0:T(8,128)(2,1)S(1)}, bf16[384,512]{1,0:T(8,128)(2,1)}, u32[]{:S(2)}, u32[]{:S(2)}) %collective-permute-start.9) | collective-permute-done | bytes 393248 | tf_op jit(solution)/shard_map/ppermute | solution.py:229
  324.5 8.5 %shard_map.119 = (f32[384,512]{1,0:T(8,128)}, f32[384,640]{1,0:T(8,128)}) custom-call(s32[12]{0:T(128)} %stack.124.places, bf16[384,512]{1,0:T(8,128)(2,1)} %refs_0_.5, bf16[384,512]{1,0:T(8,128)(2,1)} %copy-done.12, bf16[384,512]{1,0:T(8,128)(2,1)} %copy-done.10, bf16[384,512]{1,0:T(8,128)(2,1)} %collective-permute-done.8.refs_3_, ...), custom_call_target="tpu_custom_call" | custom-call | flops 2717908992 | bytes 10223616 | tf_op jit(solution)/shard_map/pallas_call | solution.py:86
  333.1 0.7 copy-done.13
  333.8 5.2 %shard_map.120 = (f32[384,512]{1,0:T(8,128)}, f32[384,640]{1,0:T(8,128)}) custom-call(s32[4]{0:T(128)} %pad_add_fusion.1.places, bf16[384,512]{1,0:T(8,128)(2,1)} %copy-done.6, bf16[384,512]{1,0:T(8,128)(2,1)} %copy-done.13, bf16[8192,512]{1,0:T(8,128)(2,1)} %refs_3_.1, bf16[8192,512]{1,0:T(8,128)(2,1)} %refs_3_.1, ...), custom_call_target="tpu_custom_call" | custom-call | flops 905969664 | bytes 4456448 | tf_op jit(solution)/shard_map/pallas_call | solution.py:86
  339.2 0.9 copy.64
  340.1 9.0 %all-to-all-start = ((bf16[32,16,512]{2,0,1:T(8,128)(2,1)}), bf16[32,16,512]{2,0,1:T(8,128)(2,1)S(1)}, u32[]{:S(2)}, u32[]{:S(2)}) async-start(bf16[32,16,512]{2,0,1:T(8,128)(2,1)} %bitcast.60), calls=%async_computation | async-start | bytes 1048576 | tf_op jit(solution)/shard_map/all_to_all | solution.py:298
  349.2 1.2 slice_add_fusion
  350.7 2.0 collective-permute-start.11
  352.7 10.9 %all-to-all-done = bf16[32,16,512]{2,0,1:T(8,128)(2,1)S(1)} async-done(((bf16[32,16,512]{2,0,1:T(8,128)(2,1)}), bf16[32,16,512]{2,0,1:T(8,128)(2,1)S(1)}, u32[]{:S(2)}, u32[]{:S(2)}) %all-to-all-start) | async-done | bytes 524320 | tf_op jit(solution)/shard_map/all_to_all | solution.py:298
  363.6 1.5 collective-permute-start.15
  365.2 1.2 collective-permute-start.12
  366.4 1.2 collective-permute-start.13
  367.6 2.8 collective-permute-start.14
  370.4 0.8 reduce_sum.23.slot
  371.2 1.5 collective-permute-done.13
  372.7 0.6 add_add_fusion.low
  373.3 4.1 collective-permute-done.15.up_other
  377.5 0.8 copy-done.8
  378.2 3.6 shard_map.121
  381.9 4.4 all-to-all-start.1
  386.4 12.0 %all-to-all-done.1 = bf16[16,24,512]{2,1,0:T(8,128)(2,1)S(1)} async-done(((bf16[16,24,512]{2,1,0:T(8,128)(2,1)}), bf16[16,24,512]{2,1,0:T(8,128)(2,1)S(1)}, u32[]{:S(2)}, u32[]{:S(2)}) %all-to-all-start.1) | async-done | bytes 393248 | tf_op jit(solution)/shard_map/all_to_all | solution.py:335
  399.2 5.5 %fusion.18 = (f32[8,24,8]{2,1,0:T(8,128)S(1)}, f32[8,24,8,128]{3,2,1,0:T(8,128)S(1)}) fusion(bf16[8,24,128,128]{3,2,1,0:T(8,128)(2,1)} %param.19, bf16[24,8,8,128]{3,2,1,0:T(8,128)(2,1)S(1)} %reshape.61, pred[24,128]{1,0:T(8,128)(4,1)S(1)} %iota_compare_fusion.1), kind=kOutput, calls=%fused_computation.43 | convolution fusion | flops 50723328 | bytes 7480320 | tf_op jit(solution)/shard_map/rkge,krje->krgj/dot_general | solution.py:213
  404.7 0.5 fusion.8
  405.4 4.6 fusion.5
  410.4 15.5 %all_to_all.54 = bf16[24,16,512]{2,0,1:T(8,128)(2,1)S(1)} all-to-all(bf16[24,16,512]{2,0,1:T(8,128)(2,1)S(1)} %copy.41), channel_id=1, replica_groups=mesh['rep'=2,'z'=4,'y'=2,'core'=2] {'z','y','core'}, dimensions={1} | all-to-all | bytes 786432 | tf_op jit(solution)/shard_map/all_to_all | solution.py:340
  426.1 0.6 pad_add_fusion.3.places
  426.7 1.0 collective-permute-done.16.other
  427.7 0.8 copy-done.4
  428.4 4.2 shard_map.124
  432.6 0.6 collective-permute-start.20
  433.2 0.6 pad_add_fusion.2.places
  433.8 4.3 shard_map.123
  438.1 1.4 collective-permute-start.19
  439.5 5.3 %collective-permute-done.20 = bf16[384,512]{1,0:T(8,128)(2,1)S(1)} collective-permute-done((bf16[384,512]{1,0:T(8,128)(2,1)}, bf16[384,512]{1,0:T(8,128)(2,1)S(1)}, u32[]{:S(2)}, u32[]{:S(2)}) %collective-permute-start.20) | collective-permute-done | bytes 393248 | tf_op jit(solution)/shard_map/ppermute | solution.py:229
  444.9 2.8 collective-permute-start.21
  447.7 0.6 pad_add_fusion.4.places
  448.3 4.2 shard_map.125
  452.5 0.9 collective-permute-start.23
  453.4 0.7 collective-permute-start.24
  454.0 0.7 pad_add_fusion.places
  454.7 4.3 shard_map.122
  459.0 1.1 collective-permute-start.18
  460.3 2.0 collective-permute-start.22
  462.3 2.4 collective-permute-done.23
  465.0 5.9 %collective-permute-done.18 = bf16[384,512]{1,0:T(8,128)(2,1)S(1)} collective-permute-done((bf16[384,512]{1,0:T(8,128)(2,1)}, bf16[384,512]{1,0:T(8,128)(2,1)S(1)}, u32[]{:S(2)}, u32[]{:S(2)}) %collective-permute-start.18) | collective-permute-done | bytes 393248 | tf_op jit(solution)/shard_map/ppermute | solution.py:229
  470.8 3.3 collective-permute-done.22
  474.2 6.1 %collective-permute-done.25 = bf16[384,512]{1,0:T(8,128)(2,1)S(1)} collective-permute-done((bf16[384,512]{1,0:T(8,128)(2,1)S(1)}, bf16[384,512]{1,0:T(8,128)(2,1)S(1)}, u32[]{:S(2)}, u32[]{:S(2)}) %collective-permute-start.25) | collective-permute-done | bytes 393248 | tf_op jit(solution)/shard_map/ppermute | solution.py:229
  480.3 1.9 add_convert_fusion
  (85 shorter events, 3.3 us)
Async XLA Ops:
  0.0 339.2 %copy-start = (bf16[1,8192,64]{1,2,0:T(8,128)(2,1)S(1)}, bf16[1,8192,64]{1,2,0:T(8,128)(2,1)}, u32[]{:S(2)}) copy-start(bf16[1,8192,64]{1,2,0:T(8,128)(2,1)} %param.18) | copy-start | bytes 3145732
  0.0 271.9 %copy-start.9 = (bf16[384,512]{1,0:T(8,128)(2,1)S(1)}, bf16[384,512]{1,0:T(8,128)(2,1)}, u32[]{:S(2)}) copy-start(bf16[384,512]{1,0:T(8,128)(2,1)} %refs_0_.5) | copy-start | bytes 1179652
  0.0 310.4 %copy-start.20 = (s32[384,1]{0,1:T(1,128)S(1)}, s32[384,1]{0,1:T(1,128)}, u32[]{:S(2)}) copy-start(s32[384,1]{0,1:T(1,128)} %param.13) | copy-start | bytes 4612
  0.0 311.1 %copy-start.21 = (s32[16]{0:T(128)S(1)}, s32[16]{0:T(128)}, u32[]{:S(2)}) copy-start(s32[16]{0:T(128)} %param.14) | copy-start | bytes 196
  271.3 53.1 %collective-permute-start.5 = (bf16[8,512,512]{2,1,0:T(8,128)(2,1)}, bf16[8,512,512]{2,1,0:T(8,128)(2,1)}, u32[]{:S(2)}, u32[]{:S(2)}) collective-permute-start(bf16[8,512,512]{2,1,0:T(8,128)(2,1)} %get-tuple-element.21), channel_id=1, source_target_pairs={{0,1},{1,0},{2,3},{3,2},{4,5},{5,4},{6,7},{7,6},{8,9},{9,8},{10,11... | collective-permute-start | bytes 12582920 | tf_op jit(solution)/shard_map/ppermute | solution.py:229
  271.9 14.7 %collective-permute-start = (bf16[384,512]{1,0:T(8,128)(2,1)S(1)}, bf16[384,512]{1,0:T(8,128)(2,1)S(1)}, u32[]{:S(2)}, u32[]{:S(2)}) collective-permute-start(bf16[384,512]{1,0:T(8,128)(2,1)S(1)} %copy-done.9), channel_id=1, source_target_pairs={{0,4},{4,8},{8,12},{12,0},{1,5},{5,9},{9,13},{13,1},{2,6},{6,10},{... | collective-permute-start | bytes 1179656 | tf_op jit(solution)/shard_map/ppermute | solution.py:229
  274.5 19.6 %collective-permute-start.2 = (bf16[384,512]{1,0:T(8,128)(2,1)S(1)}, bf16[384,512]{1,0:T(8,128)(2,1)S(1)}, u32[]{:S(2)}, u32[]{:S(2)}) collective-permute-start(bf16[384,512]{1,0:T(8,128)(2,1)S(1)} %copy-done.9), channel_id=1, source_target_pairs={{0,12},{4,0},{8,4},{12,8},{1,13},{5,1},{9,5},{13,9},{2,14},{6,2},{... | collective-permute-start | bytes 1179656 | tf_op jit(solution)/shard_map/ppermute | solution.py:229
  286.5 37.9 %copy-start.10 = (bf16[384,512]{1,0:T(8,128)(2,1)}, bf16[384,512]{1,0:T(8,128)(2,1)S(1)}, u32[]{:S(2)}) copy-start(bf16[384,512]{1,0:T(8,128)(2,1)S(1)} %collective-permute-done.refs_2_) | copy-start | bytes 1179652
  286.5 10.4 %collective-permute-start.1 = (bf16[384,512]{1,0:T(8,128)(2,1)S(1)}, bf16[384,512]{1,0:T(8,128)(2,1)S(1)}, u32[]{:S(2)}, u32[]{:S(2)}) collective-permute-start(bf16[384,512]{1,0:T(8,128)(2,1)S(1)} %collective-permute-done.refs_2_), channel_id=1, source_target_pairs={{4,8},{8,12},{5,9},{9,13},{6,10},{10,14},{7,11},{11,15},{20,24},{2... | collective-permute-start | bytes 1179656 | tf_op jit(solution)/shard_map/ppermute | solution.py:241
  294.1 30.4 %copy-start.11 = (bf16[384,512]{1,0:T(8,128)(2,1)}, bf16[384,512]{1,0:T(8,128)(2,1)S(1)}, u32[]{:S(2)}) copy-start(bf16[384,512]{1,0:T(8,128)(2,1)S(1)} %collective-permute-done.2.refs_4_) | copy-start | bytes 1179652
  294.1 12.5 %collective-permute-start.3 = (bf16[384,512]{1,0:T(8,128)(2,1)S(1)}, bf16[384,512]{1,0:T(8,128)(2,1)}, u32[]{:S(2)}, u32[]{:S(2)}) collective-permute-start(bf16[384,512]{1,0:T(8,128)(2,1)S(1)} %collective-permute-done.2.refs_4_), channel_id=1, source_target_pairs={{8,4},{4,0},{9,5},{5,1},{10,6},{6,2},{11,7},{7,3},{24,20},{20,16},... | collective-permute-start | bytes 1179656 | tf_op jit(solution)/shard_map/ppermute | solution.py:241
  295.4 13.8 %collective-permute-start.7 = (bf16[384,512]{1,0:T(8,128)(2,1)S(1)}, bf16[384,512]{1,0:T(8,128)(2,1)S(1)}, u32[]{:S(2)}, u32[]{:S(2)}) collective-permute-start(bf16[384,512]{1,0:T(8,128)(2,1)S(1)} %copy-done.9), channel_id=1, source_target_pairs={{0,2},{2,0},{1,3},{3,1},{4,6},{6,4},{5,7},{7,5},{8,10},{10,8},{9,1... | collective-permute-start | bytes 1179656 | tf_op jit(solution)/shard_map/ppermute | solution.py:229
  297.0 14.2 %collective-permute-start.6 = (bf16[8,64,512]{2,1,0:T(8,128)(2,1)}, bf16[8,64,512]{2,1,0:T(8,128)(2,1)S(1)}, u32[]{:S(2)}, u32[]{:S(2)}) collective-permute-start(bf16[8,64,512]{2,1,0:T(8,128)(2,1)} %get-tuple-element.22), channel_id=1, source_target_pairs={{0,1},{1,0},{2,3},{3,2},{4,5},{5,4},{6,7},{7,6},{8,9},{9,8},{10,11... | collective-permute-start | bytes 1572872 | tf_op jit(solution)/shard_map/ppermute | solution.py:229
  297.0 9.6 %copy-start.14 = (bf16[384,512]{1,0:T(8,128)(2,1)}, bf16[384,512]{1,0:T(8,128)(2,1)S(1)}, u32[]{:S(2)}) copy-start(bf16[384,512]{1,0:T(8,128)(2,1)S(1)} %collective-permute-done.1) | copy-start | bytes 1179652
  297.0 19.1 %collective-permute-start.8 = (bf16[384,512]{1,0:T(8,128)(2,1)S(1)}, bf16[384,512]{1,0:T(8,128)(2,1)}, u32[]{:S(2)}, u32[]{:S(2)}) collective-permute-start(bf16[384,512]{1,0:T(8,128)(2,1)S(1)} %collective-permute-done.refs_2_), channel_id=1, source_target_pairs={{0,2},{2,0},{1,3},{3,1},{4,6},{6,4},{5,7},{7,5},{8,10},{10,8},{9,1... | collective-permute-start | bytes 1179656 | tf_op jit(solution)/shard_map/ppermute | solution.py:229
  306.6 17.9 %collective-permute-start.9 = (bf16[384,512]{1,0:T(8,128)(2,1)S(1)}, bf16[384,512]{1,0:T(8,128)(2,1)}, u32[]{:S(2)}, u32[]{:S(2)}) collective-permute-start(bf16[384,512]{1,0:T(8,128)(2,1)S(1)} %collective-permute-done.2.refs_4_), channel_id=1, source_target_pairs={{0,2},{2,0},{1,3},{3,1},{4,6},{6,4},{5,7},{7,5},{8,10},{10,8},{9,1... | collective-permute-start | bytes 1179656 | tf_op jit(solution)/shard_map/ppermute | solution.py:229
  309.2 23.9 %copy-start.6 = (bf16[384,512]{1,0:T(8,128)(2,1)}, bf16[384,512]{1,0:T(8,128)(2,1)S(1)}, u32[]{:S(2)}) copy-start(bf16[384,512]{1,0:T(8,128)(2,1)S(1)} %broadcast_select_fusion.refs_0_) | copy-start | bytes 1179652
  309.2 15.3 %copy-start.12 = (bf16[384,512]{1,0:T(8,128)(2,1)}, bf16[384,512]{1,0:T(8,128)(2,1)S(1)}, u32[]{:S(2)}) copy-start(bf16[384,512]{1,0:T(8,128)(2,1)S(1)} %collective-permute-done.7.refs_1_) | copy-start | bytes 1179652
  309.2 23.9 %collective-permute-start.4 = (bf16[384,512]{1,0:T(8,128)(2,1)S(1)}, bf16[384,512]{1,0:T(8,128)(2,1)S(1)}, u32[]{:S(2)}, u32[]{:S(2)}) collective-permute-start(bf16[384,512]{1,0:T(8,128)(2,1)S(1)} %broadcast_select_fusion.refs_0_), channel_id=1, source_target_pairs={{0,2},{2,0},{1,3},{3,1},{4,6},{6,4},{5,7},{7,5},{8,10},{10,8},{9,1... | collective-permute-start | bytes 1179656 | tf_op jit(solution)/shard_map/ppermute | solution.py:229
  311.2 13.3 %copy-start.2 = (bf16[8,64,512]{2,1,0:T(8,128)(2,1)}, bf16[8,64,512]{2,1,0:T(8,128)(2,1)S(1)}, u32[]{:S(2)}) copy-start(bf16[8,64,512]{2,1,0:T(8,128)(2,1)S(1)} %collective-permute-done.6.refs_24_.refs_25_.refs_26_.refs_27_.refs_28_.refs_29_.refs_8_.refs_9_) | copy-start | bytes 1572868
  311.2 115.4 %collective-permute-start.17 = (bf16[8,512,512]{2,1,0:T(8,128)(2,1)}, bf16[8,512,512]{2,1,0:T(8,128)(2,1)}, u32[]{:S(2)}, u32[]{:S(2)}) collective-permute-start(bf16[8,512,512]{2,1,0:T(8,128)(2,1)} %get-tuple-element.28), channel_id=1, source_target_pairs={{0,1},{1,0},{2,3},{3,2},{4,5},{5,4},{6,7},{7,6},{8,9},{9,8},{10,11... | collective-permute-start | bytes 12582920 | tf_op jit(solution)/shard_map/ppermute | solution.py:229
  333.1 0.8 copy-start.13
  339.1 47.2 %copy-start.18 = (bf16[24,1024]{1,0:T(8,128)(2,1)S(1)}, bf16[24,1024]{1,0:T(8,128)(2,1)}, u32[]{:S(2)}) copy-start(bf16[24,1024]{1,0:T(8,128)(2,1)} %param.21) | copy-start | bytes 147460
  339.1 47.2 %copy-start.19 = (bf16[24,1024]{1,0:T(8,128)(2,1)S(1)}, bf16[24,1024]{1,0:T(8,128)(2,1)}, u32[]{:S(2)}) copy-start(bf16[24,1024]{1,0:T(8,128)(2,1)} %param.22) | copy-start | bytes 147460
  339.1 47.3 %copy-start.22 = (s32[24]{0:T(128)S(1)}, s32[24]{0:T(128)}, u32[]{:S(2)}) copy-start(s32[24]{0:T(128)} %param.15) | copy-start | bytes 292
  339.1 10.1 %collective-permute-start.10 = (f32[384,640]{1,0:T(8,128)}, f32[384,640]{1,0:T(8,128)S(1)}, u32[]{:S(2)}, u32[]{:S(2)}) collective-permute-start(f32[384,640]{1,0:T(8,128)} %get-tuple-element.26), channel_id=1, source_target_pairs={{0,1},{1,0},{2,3},{3,2},{4,5},{5,4},{6,7},{7,6},{8,9},{9,8},{10,11... | collective-permute-start | bytes 2949128 | tf_op jit(solution)/shard_map/ppermute | solution.py:229
  340.1 23.5 %all-to-all-start = ((bf16[32,16,512]{2,0,1:T(8,128)(2,1)}), bf16[32,16,512]{2,0,1:T(8,128)(2,1)S(1)}, u32[]{:S(2)}, u32[]{:S(2)}) async-start(bf16[32,16,512]{2,0,1:T(8,128)(2,1)} %bitcast.60), calls=%async_computation | async-start | bytes 1048576 | tf_op jit(solution)/shard_map/all_to_all | solution.py:298
  349.2 28.3 %copy-start.7 = (f32[384,640]{1,0:T(8,128)}, f32[384,640]{1,0:T(8,128)S(1)}, u32[]{:S(2)}) copy-start(f32[384,640]{1,0:T(8,128)S(1)} %collective-permute-done.10.received) | copy-start | bytes 2949124
  350.7 14.4 %collective-permute-start.11 = (bf16[192,128]{1,0:T(8,128)(2,1)S(1)}, bf16[192,128]{1,0:T(8,128)(2,1)S(1)}, u32[]{:S(2)}, u32[]{:S(2)}) collective-permute-start(bf16[192,128]{1,0:T(8,128)(2,1)S(1)} %pad_maximum_fusion), channel_id=1, source_target_pairs={{0,2},{2,0},{1,3},{3,1},{4,6},{6,4},{5,7},{7,5},{8,10},{10,8},{9,1... | collective-permute-start | bytes 147464 | tf_op jit(solution)/shard_map/ppermute | solution.py:229
  363.6 13.9 %copy-start.5 = (bf16[32,16,512]{2,0,1:T(8,128)(2,1)}, bf16[32,16,512]{2,0,1:T(8,128)(2,1)S(1)}, u32[]{:S(2)}) copy-start(bf16[32,16,512]{2,0,1:T(8,128)(2,1)S(1)} %all-to-all-done) | copy-start | bytes 1572868
  363.6 13.8 %collective-permute-start.15 = (bf16[512,512]{1,0:T(8,128)(2,1)S(1)}, bf16[512,512]{1,0:T(8,128)(2,1)S(1)}, u32[]{:S(2)}, u32[]{:S(2)}) collective-permute-start(bf16[512,512]{1,0:T(8,128)(2,1)S(1)} %bitcast.76), channel_id=1, source_target_pairs={{0,16},{16,0},{1,17},{17,1},{2,18},{18,2},{3,19},{19,3},{4,20},{20... | collective-permute-start | bytes 1572872 | tf_op jit(solution)/shard_map/ppermute | solution.py:299
  365.2 6.0 %collective-permute-start.12 = (bf16[192,128]{1,0:T(8,128)(2,1)S(1)}, bf16[192,128]{1,0:T(8,128)(2,1)S(1)}, u32[]{:S(2)}, u32[]{:S(2)}) collective-permute-start(bf16[192,128]{1,0:T(8,128)(2,1)S(1)} %fusion.20), channel_id=1, source_target_pairs={{0,4},{4,8},{8,12},{12,0},{1,5},{5,9},{9,13},{13,1},{2,6},{6,10},{... | collective-permute-start | bytes 147464 | tf_op jit(solution)/shard_map/ppermute | solution.py:229
  366.4 6.3 %collective-permute-start.13 = (bf16[192,128]{1,0:T(8,128)(2,1)S(1)}, bf16[192,128]{1,0:T(8,128)(2,1)S(1)}, u32[]{:S(2)}, u32[]{:S(2)}) collective-permute-start(bf16[192,128]{1,0:T(8,128)(2,1)S(1)} %fusion.20), channel_id=1, source_target_pairs={{0,8},{4,12},{8,0},{12,4},{1,9},{5,13},{9,1},{13,5},{2,10},{6,14},... | collective-permute-start | bytes 147464 | tf_op jit(solution)/shard_map/ppermute | solution.py:229
  367.6 5.1 %collective-permute-start.14 = (bf16[192,128]{1,0:T(8,128)(2,1)S(1)}, bf16[192,128]{1,0:T(8,128)(2,1)S(1)}, u32[]{:S(2)}, u32[]{:S(2)}) collective-permute-start(bf16[192,128]{1,0:T(8,128)(2,1)S(1)} %fusion.20), channel_id=1, source_target_pairs={{0,12},{4,0},{8,4},{12,8},{1,13},{5,1},{9,5},{13,9},{2,14},{6,2},{... | collective-permute-start | bytes 147464 | tf_op jit(solution)/shard_map/ppermute | solution.py:229
  377.4 0.8 copy-start.8
  381.9 16.6 %all-to-all-start.1 = ((bf16[16,24,512]{2,1,0:T(8,128)(2,1)}), bf16[16,24,512]{2,1,0:T(8,128)(2,1)S(1)}, u32[]{:S(2)}, u32[]{:S(2)}) async-start(bf16[16,24,512]{2,1,0:T(8,128)(2,1)} %bitcast.79), calls=%async_computation.1 | async-start | bytes 786432 | tf_op jit(solution)/shard_map/all_to_all | solution.py:335
  425.9 1.7 copy-start.3
  425.9 1.7 collective-permute-start.16
  427.7 0.8 copy-start.4
  432.6 12.2 %collective-permute-start.20 = (bf16[384,512]{1,0:T(8,128)(2,1)}, bf16[384,512]{1,0:T(8,128)(2,1)S(1)}, u32[]{:S(2)}, u32[]{:S(2)}) collective-permute-start(bf16[384,512]{1,0:T(8,128)(2,1)} %get-tuple-element.34), channel_id=1, source_target_pairs={{0,2},{2,0},{1,3},{3,1},{4,6},{6,4},{5,7},{7,5},{8,10},{10,8},{9,1... | collective-permute-start | bytes 1179656 | tf_op jit(solution)/shard_map/ppermute | solution.py:229
  433.8 11.0 %copy-start.16 = (bf16[384,512]{1,0:T(8,128)(2,1)S(1)}, bf16[384,512]{1,0:T(8,128)(2,1)}, u32[]{:S(2)}) copy-start(bf16[384,512]{1,0:T(8,128)(2,1)} %get-tuple-element.33) | copy-start | bytes 1179652
  438.1 22.1 %collective-permute-start.19 = (bf16[384,512]{1,0:T(8,128)(2,1)}, bf16[384,512]{1,0:T(8,128)(2,1)S(1)}, u32[]{:S(2)}, u32[]{:S(2)}) collective-permute-start(bf16[384,512]{1,0:T(8,128)(2,1)} %get-tuple-element.32), channel_id=1, source_target_pairs={{0,2},{2,0},{1,3},{3,1},{4,6},{6,4},{5,7},{7,5},{8,10},{10,8},{9,1... | collective-permute-start | bytes 1179656 | tf_op jit(solution)/shard_map/ppermute | solution.py:229
  444.9 15.3 %collective-permute-start.21 = (bf16[384,512]{1,0:T(8,128)(2,1)S(1)}, bf16[384,512]{1,0:T(8,128)(2,1)S(1)}, u32[]{:S(2)}, u32[]{:S(2)}) collective-permute-start(bf16[384,512]{1,0:T(8,128)(2,1)S(1)} %add_convert_fusion.3), channel_id=1, source_target_pairs={{0,4},{4,8},{1,5},{5,9},{2,6},{6,10},{3,7},{7,11},{16,20},{20,24},... | collective-permute-start | bytes 1179656 | tf_op jit(solution)/shard_map/ppermute | solution.py:252
  452.5 12.3 %collective-permute-start.23 = (bf16[384,512]{1,0:T(8,128)(2,1)}, bf16[384,512]{1,0:T(8,128)(2,1)S(1)}, u32[]{:S(2)}, u32[]{:S(2)}) collective-permute-start(bf16[384,512]{1,0:T(8,128)(2,1)} %get-tuple-element.36), channel_id=1, source_target_pairs={{0,2},{2,0},{1,3},{3,1},{4,6},{6,4},{5,7},{7,5},{8,10},{10,8},{9,1... | collective-permute-start | bytes 1179656 | tf_op jit(solution)/shard_map/ppermute | solution.py:229
  453.4 11.4 %collective-permute-start.24 = (bf16[384,512]{1,0:T(8,128)(2,1)S(1)}, bf16[384,512]{1,0:T(8,128)(2,1)S(1)}, u32[]{:S(2)}, u32[]{:S(2)}) collective-permute-start(bf16[384,512]{1,0:T(8,128)(2,1)S(1)} %add_convert_fusion.3), channel_id=1, source_target_pairs={{12,8},{8,4},{13,9},{9,5},{14,10},{10,6},{15,11},{11,7},{28,24},{2... | collective-permute-start | bytes 1179656 | tf_op jit(solution)/shard_map/ppermute | solution.py:253
  454.7 5.4 %copy-start.15 = (bf16[384,512]{1,0:T(8,128)(2,1)S(1)}, bf16[384,512]{1,0:T(8,128)(2,1)}, u32[]{:S(2)}) copy-start(bf16[384,512]{1,0:T(8,128)(2,1)} %get-tuple-element.31) | copy-start | bytes 1179652
  454.7 10.0 %copy-start.17 = (bf16[384,512]{1,0:T(8,128)(2,1)S(1)}, bf16[384,512]{1,0:T(8,128)(2,1)}, u32[]{:S(2)}) copy-start(bf16[384,512]{1,0:T(8,128)(2,1)} %get-tuple-element.35) | copy-start | bytes 1179652
  454.7 27.6 %copy-start.1 = (bf16[1,8192,64]{1,2,0:T(8,128)(2,1)S(1)}, bf16[1,8192,64]{1,2,0:T(8,128)(2,1)}, u32[]{:S(2)}) copy-start(bf16[1,8192,64]{1,2,0:T(8,128)(2,1)} %param.18) | copy-start | bytes 3145732
  459.0 11.9 %collective-permute-start.18 = (bf16[384,512]{1,0:T(8,128)(2,1)}, bf16[384,512]{1,0:T(8,128)(2,1)S(1)}, u32[]{:S(2)}, u32[]{:S(2)}) collective-permute-start(bf16[384,512]{1,0:T(8,128)(2,1)} %get-tuple-element.30), channel_id=1, source_target_pairs={{0,2},{2,0},{1,3},{3,1},{4,6},{6,4},{5,7},{7,5},{8,10},{10,8},{9,1... | collective-permute-start | bytes 1179656 | tf_op jit(solution)/shard_map/ppermute | solution.py:229
  460.3 13.9 %collective-permute-start.22 = (bf16[384,512]{1,0:T(8,128)(2,1)S(1)}, bf16[384,512]{1,0:T(8,128)(2,1)S(1)}, u32[]{:S(2)}, u32[]{:S(2)}) collective-permute-start(bf16[384,512]{1,0:T(8,128)(2,1)S(1)} %add_convert_fusion.2), channel_id=1, source_target_pairs={{0,4},{4,8},{8,12},{12,0},{1,5},{5,9},{9,13},{13,1},{2,6},{6,10},{... | collective-permute-start | bytes 1179656 | tf_op jit(solution)/shard_map/ppermute | solution.py:229
  464.9 15.4 %collective-permute-start.25 = (bf16[384,512]{1,0:T(8,128)(2,1)S(1)}, bf16[384,512]{1,0:T(8,128)(2,1)S(1)}, u32[]{:S(2)}, u32[]{:S(2)}) collective-permute-start(bf16[384,512]{1,0:T(8,128)(2,1)S(1)} %add_convert_fusion.1), channel_id=1, source_target_pairs={{0,12},{4,0},{8,4},{12,8},{1,13},{5,1},{9,5},{13,9},{2,14},{6,2},{... | collective-permute-start | bytes 1179656 | tf_op jit(solution)/shard_map/ppermute | solution.py:229
where the time goes:
time: 483 us; the launch traced here: 482 us
  Pallas kernels  306 us (63%)
  waiting for transfers between devices  91.6 us (19%)
  starting transfers between devices  43.5 us (9%)
  blocking collectives  15.5 us (3%)
  matrix products  10.5 us (2%)
  other arithmetic  9.46 us (2%)
  local copies, waits for them, and re-layouts  5.65 us (1%)
    pallas_call x1, Pallas kernels, other_slices(): pl.pallas_call(slices_kernel, in_specs=[pl.BlockSpec(memory_space=pltpu.S...  271 us
    ppermute x21, waiting for transfers between devices, shift(): lax.ppermute(value, axis, [(i, (i + by) % size) for i in range(size)])  55.5 us
    ppermute x21, starting transfers between devices, shift(): lax.ppermute(value, axis, [(i, (i + by) % size) for i in range(size)])  23.1 us
    pallas_call x4, Pallas kernels, output_partial(): pl.pallas_call(output_kernel, grid_spec=pltpu.PrefetchScalarGridSpec(num_...  16.9 us
    all_to_all x1, blocking collectives, shards(): lax.all_to_all(context, ADP, split_axis=1, concat_axis=0, tiled=True)  15.5 us
    pallas_call x2, Pallas kernels, project(): pl.pallas_call(project_kernel, grid_spec=pltpu.PrefetchScalarGridSpec(num...  13.8 us
    all_to_all x1, waiting for transfers between devices, shards(): lax.all_to_all(query, ADP, split_axis=0, concat_axis=1, tiled=True)  12 us
    all_to_all x1, waiting for transfers between devices, shards(): up = lax.all_to_all(up, ADP, split_axis=1, concat_axis=0, tiled=True)  10.9 us
  transfers between devices with their start and end apart: 28, of which 15 were waited for; matrix products, arithmetic and copies ran while one was open for 4% of the time, Pallas kernels for 6%

commit v1 on v0

v1 whole, which is shorter than its diff:
```python
import jax
import jax.numpy as jnp
from jax import lax
from jax.experimental import pallas as pl
from jax.experimental.pallas import tpu as pltpu
from jax.sharding import Mesh
from jax.sharding import PartitionSpec as P

HEADS = 64
HEAD_DIM = 128
ADP = ("z", "y", "core")
NT = (((1,), (1,)), ((), ()))
VMEM_LIMIT = 56 << 20


def low_kernel(places, *refs):
    count = places.shape[0] // 2
    blocks, a_own, a_other = (refs[i * count : (i + 1) * count] for i in range(3))
    out = refs[-1]
    out[...] = refs[-2][...] if len(refs) > 3 * count + 1 else jnp.zeros_like(out)
    first_core = places[0] % 2 == 0
    for i in range(count):

        @pl.when(places[count + i] > 0)
        def _():
            own, other = a_own[i][0], a_other[i][0]
            pair = jnp.concatenate(
                [jnp.where(first_core, own, other), jnp.where(first_core, other, own)], axis=0
            )
            out[...] += lax.dot_general(
                blocks[i][...], pair, NT, preferred_element_type=jnp.float32
            )


def add_low(places, blocks, down, down_other, sums):
    count = len(blocks)
    rows, width = blocks[0].shape
    rank = down.shape[1]
    flat = lambda shape: pl.BlockSpec(shape, lambda j, p: (0, 0))
    shape = (rows, 2 * rank)
    maps = [pl.BlockSpec((1, rank, width), lambda j, p, i=i: (0, 0, p[i])) for i in range(count)]
    return pl.pallas_call(
        low_kernel,
        grid_spec=pltpu.PrefetchScalarGridSpec(
            num_scalar_prefetch=1,
            grid=(1,),
            in_specs=[flat((rows, width))] * count + maps * 2 + [flat(shape)] * len(sums),
            out_specs=flat(shape),
        ),
        out_shape=jax.ShapeDtypeStruct(shape, jnp.float32),
        compiler_params=pltpu.CompilerParams(vmem_limit_bytes=VMEM_LIMIT),
        cost_estimate=pl.CostEstimate(
            flops=4 * count * rows * width * rank,
            bytes_accessed=2 * count * width * (rows + 2 * rank),
            transcendentals=0,
        ),
    )(places, *blocks, *[down] * count, *[down_other] * count, *sums)


def project_kernel(places, *refs):
    count = places.shape[0] // 2
    blocks, w_own, w_other = (refs[i * count : (i + 1) * count] for i in range(3))
    outs = refs[-2:]
    for j, (out, weights) in enumerate(zip(outs, (w_own, w_other))):
        out[...] = refs[3 * count + j][...] if len(refs) > 3 * count + 2 else jnp.zeros_like(out)
        for i in range(count):

            @pl.when(places[count + i] > 0)
            def _():
                out[...] += jnp.dot(
                    blocks[i][...], weights[i][...], preferred_element_type=jnp.float32
                )


def project(places, blocks, weight, weight_other, sums):
    count = len(blocks)
    rows, width = blocks[0].shape
    cols = weight.shape[1]
    tile = cols // 2 if cols % 256 == 0 else cols
    sum_spec = pl.BlockSpec((rows, tile), lambda j, p: (0, j))
    weights = [pl.BlockSpec((width, tile), lambda j, p, i=i: (p[i], j)) for i in range(count)]
    return pl.pallas_call(
        project_kernel,
        grid_spec=pltpu.PrefetchScalarGridSpec(
            num_scalar_prefetch=1,
            grid=(cols // tile,),
            in_specs=[pl.BlockSpec((rows, width), lambda j, p: (0, 0))] * count
            + weights * 2
            + [sum_spec] * len(sums),
            out_specs=[sum_spec] * 2,
        ),
        out_shape=[jax.ShapeDtypeStruct((rows, cols), jnp.float32)] * 2,
        compiler_params=pltpu.CompilerParams(vmem_limit_bytes=VMEM_LIMIT),
        cost_estimate=pl.CostEstimate(
            flops=4 * count * rows * width * cols,
            bytes_accessed=2 * count * width * (rows + 2 * cols) + 8 * rows * cols,
            transcendentals=0,
        ),
    )(places, *blocks, *[weight] * count, *[weight_other] * count, *sums)


def query_kernel(half, own, received, low, slot, up_own, up_other, out):
    step = pl.program_id(0)
    cols, lanes = own.shape[1], low.shape[1]
    rank = lanes // 2
    part = rank // 2
    depth = up_own.shape[0]
    shape = (lanes, depth)
    lane = lax.broadcasted_iota(jnp.int32, shape, 1) % part
    row = lax.broadcasted_iota(jnp.int32, shape, 0)
    owner = lax.broadcasted_iota(jnp.int32, (own.shape[0], depth), 1) // part
    live = slot[...] == owner
    total = own[...] + received[:, :cols]
    for h, up in ((half[0], up_own), (1 - half[0], up_other)):
        copies = (row == lane + rank * step + part * h).astype(jnp.bfloat16)
        spread = jnp.dot(low[...], copies, preferred_element_type=jnp.float32)
        spread = jnp.where(live, spread, 0.0).astype(jnp.bfloat16)
        total += jnp.dot(spread, up[...], preferred_element_type=jnp.float32)
    out[...] = (total * HEAD_DIM ** (-0.5)).astype(out.dtype)


def make_query(half, own, received, low, slot, up_own, up_other):
    rows, cols = own.shape
    tile = rows // 2
    depth = up_own.shape[0]
    by_rows = lambda width: pl.BlockSpec((tile, width), lambda j, h: (j, 0))
    whole = lambda array: pl.BlockSpec(array.shape, lambda j, h: (0, 0))
    return pl.pallas_call(
        query_kernel,
        grid_spec=pltpu.PrefetchScalarGridSpec(
            num_scalar_prefetch=1,
            grid=(2,),
            in_specs=[
                by_rows(cols),
                by_rows(received.shape[1]),
                whole(low),
                by_rows(1),
                whole(up_own),
                whole(up_other),
            ],
            out_specs=by_rows(cols),
        ),
        out_shape=jax.ShapeDtypeStruct((rows, cols), jnp.bfloat16),
        compiler_params=pltpu.CompilerParams(vmem_limit_bytes=VMEM_LIMIT),
        cost_estimate=pl.CostEstimate(
            flops=4 * rows * cols * depth,
            bytes_accessed=rows * cols * 10 + 4 * depth * cols,
            transcendentals=0,
        ),
    )(half, own, received, low, slot, up_own, up_other)


def output_kernel(places, own, other, *refs):
    count = places.shape[0]
    for w_own, w_other, out in zip(refs[:count], refs[count : 2 * count], refs[2 * count :]):
        total = jnp.dot(own[...], w_own[...], preferred_element_type=jnp.float32)
        total += jnp.dot(other[...], w_other[...], preferred_element_type=jnp.float32)
        out[...] = total.astype(out.dtype)


def output_partial(chips, core, own, other, weight, weight_other, width):
    rows, depth = own.shape
    count = len(chips)
    tile = width // 2 if width % 256 == 0 else width
    steps = width // tile
    places = jnp.stack([2 * chip + core for chip in chips]).astype(jnp.int32)
    whole = pl.BlockSpec((rows, depth), lambda j, p: (0, 0))
    weights = [
        pl.BlockSpec((depth, tile), lambda j, p, i=i: (0, p[i] * steps + j)) for i in range(count)
    ]
    return pl.pallas_call(
        output_kernel,
        grid_spec=pltpu.PrefetchScalarGridSpec(
            num_scalar_prefetch=1,
            grid=(steps,),
            in_specs=[whole, whole] + weights * 2,
            out_specs=[pl.BlockSpec((rows, tile), lambda j, p: (0, j))] * count,
        ),
        out_shape=[jax.ShapeDtypeStruct((rows, width), jnp.bfloat16)] * count,
        compiler_params=pltpu.CompilerParams(vmem_limit_bytes=VMEM_LIMIT),
        cost_estimate=pl.CostEstimate(
            flops=4 * count * rows * width * depth,
            bytes_accessed=2 * count * width * (rows + 2 * depth) + 4 * rows * depth,
            transcendentals=0,
        ),
    )(places, own, other, *[weight] * count, *[weight_other] * count)


def attention(query, cache_length, key_cache, value_cache, k_new, v_new):
    local_reqs = query.shape[0]
    kv_count, _, span, dim = key_cache.shape
    group = HEADS // kv_count
    query = query.reshape(local_reqs, kv_count, group, dim)
    k_new = k_new.reshape(local_reqs, kv_count, dim)
    v_new = v_new.reshape(local_reqs, kv_count, dim)
    live = (jnp.arange(span)[None, :] < cache_length[:, None])[None, :, None, :]
    scores = jnp.einsum("rkge,krje->krgj", query, key_cache, preferred_element_type=jnp.float32)
    fresh = jnp.einsum("rkge,rke->krg", query, k_new, preferred_element_type=jnp.float32)
    scores = jnp.where(live, scores, -jnp.inf)
    top = jnp.maximum(jnp.max(scores, axis=3), fresh)
    expd = jnp.where(live, jnp.exp(scores - top[:, :, :, None]), 0.0)
    expf = jnp.exp(fresh - top)
    total = jnp.sum(expd, axis=3) + expf
    probs = (expd / total[:, :, :, None]).astype(jnp.bfloat16)
    probf = (expf / total).astype(jnp.bfloat16)
    context = jnp.einsum("krgj,krje->rkge", probs, value_cache, preferred_element_type=jnp.float32)
    fresh_part = jnp.einsum("krg,rke->rkge", probf.astype(jnp.float32), v_new.astype(jnp.float32))
    return (context + fresh_part).astype(jnp.bfloat16).reshape(local_reqs, HEADS * dim)


def shift(value, axis, by):
    size = lax.axis_size(axis)
    return lax.ppermute(value, axis, [(i, (i + by) % size) for i in range(size)])


def after(value, *others):
    return lax.optimization_barrier((value, *others))[0]


def swap_sides(value, layers):
    return lax.ppermute(value, ("z", "y"), [(2 * i + j, 2 * i + 1 - j) for i in layers for j in (0, 1)])


def gather_features(tokens):
    layers, sides = lax.axis_size("z"), lax.axis_size("y")
    z = lax.axis_index("z")
    if layers != 4 or sides != 2:
        entries = []
        for k in range(layers):
            block = shift(tokens, "z", k) if k else tokens
            pair = [block, shift(block, "y", 1)] if sides == 2 else [block]
            entries.append(((z - k) % layers, True, pair))
        return [entries[:-1], entries[-1:]]
    own_side = swap_sides(tokens, range(4))
    below = lax.ppermute(tokens, "z", [(0, 1), (1, 2), (2, 3)])
    above = lax.ppermute(tokens, "z", [(1, 0), (2, 1), (3, 2)])
    below_side = swap_sides(after(below, own_side), (1, 2, 3))
    above_side = swap_sides(above, (0, 1, 2))
    two = lax.ppermute(below, "z", [(1, 2), (2, 3)]), lax.ppermute(above, "z", [(2, 1), (1, 0)])
    far = lax.ppermute(after(tokens, below, above), "z", [(0, 3), (3, 0)])
    two = jnp.where(z >= 2, *two)
    two_side = swap_sides(two, range(4))
    far_side = swap_sides(far, (0, 3))
    return [
        [
            (z, True, [tokens, own_side]),
            ((z - 1) % 4, z >= 1, [below, below_side]),
            ((z + 1) % 4, z <= 2, [above, above_side]),
        ],
        [((z + 2) % 4, True, [two, two_side]), (3 - z, (z == 0) | (z == 3), [far, far_side])],
    ]


def scatter_layers(parts):
    layers = lax.axis_size("z")
    wide = lambda value: value.astype(jnp.float32)
    narrow = lambda value: value.astype(jnp.bfloat16)
    if layers != 4:
        return sum([wide(shift(narrow(parts[k]), "z", k)) for k in range(1, layers)], parts[0])
    two = narrow(parts[2])
    up = lax.ppermute(two, "z", [(0, 1), (1, 2)])
    down = lax.ppermute(two, "z", [(3, 2), (2, 1)])
    above = shift(narrow(parts[1] + wide(up)), "z", 1)
    below = shift(narrow(parts[3] + wide(down)), "z", 3)
    return parts[0] + wide(above) + wide(below)


def shards(
    tokens,
    request_adapter,
    adapter_storage_slot,
    cache_length,
    query_weight,
    adapter_down_maps,
    adapter_up_maps,
    key_cache,
    value_cache,
    new_token_key,
    new_token_value,
    output_weight,
):
    layers, sides = lax.axis_size("z"), lax.axis_size("y")
    z, y, core = lax.axis_index("z"), lax.axis_index("y"), lax.axis_index("core")
    rows, width = tokens.shape
    total_adapters = adapter_storage_slot.shape[0]
    rank = adapter_down_maps.shape[2]
    chips_of = lambda layer: [
        (layer % layers) * sides + (y + side) % sides for side in range(sides)
    ]

    down = jnp.swapaxes(adapter_down_maps, 1, 2)
    down_other = shift(down, "core", 1)
    query_weight_other = shift(query_weight, "core", 1)
    output_weight_other = shift(output_weight, "core", 1)

    ids = request_adapter[:, 0]
    numbers = jnp.arange(total_adapters, dtype=jnp.int32)
    slot = jnp.sum(
        jnp.where(ids[:, None] == numbers[None, :], adapter_storage_slot[None, :], 0), axis=1
    )[:, None]

    groups = []
    for entries in gather_features(tokens):
        chips = [chip for layer, _, _ in entries for chip in chips_of(layer)]
        valid = [flag for _, flag, pair in entries for _ in pair]
        places = [2 * chip + core for chip in chips] + valid
        places = jnp.stack([jnp.asarray(place, jnp.int32) for place in places])
        groups.append((places, [block for _, _, pair in entries for block in pair]))

    reps = lax.axis_size("rep")
    half = lax.axis_index("rep") % 2
    up = jnp.swapaxes(adapter_up_maps, 1, 2)[0]
    up = lax.dynamic_slice_in_dim(up, half * (rank // 2), rank // 2, 0)
    up = after(up, groups[0][1][2])
    up = lax.all_to_all(up, ADP, split_axis=1, concat_axis=0, tiled=True)
    up_other = lax.ppermute(up, "rep", [(i, i ^ 1) for i in range(reps)])

    sums, low = [], []
    for index, (places, blocks) in enumerate(groups):
        if index == 0:
            places = after(places, up)
        low = [add_low(places, blocks, down, down_other, low)]
        if index:
            low_other = shift(low[0], "core", 1)
        sums = project(places, blocks, query_weight, query_weight_other, sums)
    own, sent = sums
    received = shift(sent, "core", 1)

    low = low[0] + low_other
    chip = z * sides + y
    low = jnp.where(slot == 2 * chip, low[:, :rank], 0.0) + jnp.where(
        slot == 2 * chip + 1, low[:, rank:], 0.0
    )
    low = low.astype(jnp.bfloat16)
    low = jnp.concatenate([low[: rows // 2], low[rows // 2 :]], axis=1)
    if sides == 2:
        low = low + shift(low, "y", 1)
    low = sum([shift(low, "z", k) for k in range(1, layers)], low)

    query = make_query(half.astype(jnp.int32).reshape(1), own, received, low, slot, up, up_other)
    query_local = lax.all_to_all(query, ADP, split_axis=0, concat_axis=1, tiled=True)

    context = attention(
        query_local, cache_length, key_cache, value_cache, new_token_key, new_token_value
    )
    context = lax.all_to_all(context, ADP, split_axis=1, concat_axis=0, tiled=True)
    context_other = shift(context, "core", 1)

    made = {}
    order = [2, 1, 3, 0] if layers == 4 else list(range(1, layers)) + [0]
    for group in (order[:1], order[1:]):
        outs = output_partial(
            [chip for k in group for chip in chips_of(z + k)],
            core,
            context,
            context_other,
            output_weight,
            output_weight_other,
            width,
        )
        for index, k in enumerate(group):
            made[k] = outs[index * sides : (index + 1) * sides]
    other_side = {k: shift(made[k][1], "y", 1) for k in order if sides == 2}
    parts = [None] * layers
    for k in order:
        parts[k] = after(made[k][0], made[order[-1]][0]).astype(jnp.float32)
        if sides == 2:
            parts[k] = parts[k] + other_side[k].astype(jnp.float32)
    return scatter_layers(parts).astype(jnp.bfloat16)


def solution(mesh):
    reps, adp = mesh.shape["rep"], mesh.shape["adp"]
    sides = 2 if adp == 16 else 1
    mesh = Mesh(mesh.devices.reshape(reps, adp // (2 * sides), sides, 2), ("rep",) + ADP)
    in_specs = (
        P("rep", ADP),
        P("rep", None),
        P(),
        P(("rep",) + ADP),
        P(None, ADP),
        P(ADP, None, None),
        P(ADP, None, None),
        P(None, ("rep",) + ADP, None, None),
        P(None, ("rep",) + ADP, None, None),
        P(("rep",) + ADP, None),
        P(("rep",) + ADP, None),
        P(ADP, None),
    )
    return jax.shard_map(
        shards, mesh=mesh, in_specs=in_specs, out_specs=P("rep", ADP), check_vma=False
    )
```

time: 483 us -> 215 us (0.45)
  Pallas kernels: 306 us -> 40.3 us
  waiting for transfers between devices: 91.6 us -> 72.2 us
  starting transfers between devices: 43.5 us -> 57.4 us
    pallas_call x1 -> x2, Pallas kernels: 271 us -> 8.27 us  [add_low(): pl.pallas_call(low_kernel, grid_spec=pltpu.PrefetchScalarGridSpec(num_sca...]
    ppermute x21 -> x16, waiting for transfers between devices: 55.5 us -> 32.1 us  [shift(): lax.ppermute(value, axis, [(i, (i + by) % size) for i in range(size)])]
    ppermute x2 -> x10, starting transfers between devices: 1.95 us -> 23.3 us  [the longest x5 11.2 us: swap_sides(): lax.ppermute(value, ('z', 'y'), [(2 * i + j, 2 * i + 1 - j) for i in laye...]
    ppermute x2 -> x10, waiting for transfers between devices: 9.03 us -> 25.9 us  [the longest x5 14.3 us: swap_sides(): lax.ppermute(value, ('z', 'y'), [(2 * i + j, 2 * i + 1 - j) for i in laye...]
    ppermute x21 -> x16, starting transfers between devices: 23.1 us -> 11 us  [shift(): lax.ppermute(value, axis, [(i, (i + by) % size) for i in range(size)])]
    all_to_all x1, waiting for transfers between devices: 10.9 us -> 0.01 us  [shards(): up = lax.all_to_all(up, ADP, split_axis=1, concat_axis=0, tiled=True)]
    pallas_call x4 -> x2, Pallas kernels: 16.9 us -> 11.1 us  [output_partial(): pl.pallas_call(output_kernel, grid_spec=pltpu.PrefetchScalarGridSpec(num_...]
    all_to_all x1, starting transfers between devices: 9.02 us -> 14.1 us  [shards(): up = lax.all_to_all(up, ADP, split_axis=1, concat_axis=0, tiled=True)]
  transfers between devices with their start and end apart: 28 -> 31, of which waited for: 15 -> 19; matrix products, arithmetic and copies ran while one was open for 4% -> 11% of each run, Pallas kernels for 6% -> 17%
where the time goes in v1:
time: 215 us; the launch traced here: 214 us
  waiting for transfers between devices  72.2 us (34%)
  starting transfers between devices  57.4 us (27%)
  Pallas kernels  40.3 us (19%)
  blocking collectives  15.5 us (7%)
  matrix products  10.5 us (5%)
  other arithmetic  10.1 us (5%)
  local copies, waits for them, and re-layouts  7.35 us (3%)
    ppermute x16, waiting for transfers between devices, shift(): lax.ppermute(value, axis, [(i, (i + by) % size) for i in range(size)])  32.1 us
    pallas_call x2, Pallas kernels, project(): pl.pallas_call(project_kernel, grid_spec=pltpu.PrefetchScalarGridSpec(num...  17.4 us
    all_to_all x1, blocking collectives, shards(): lax.all_to_all(context, ADP, split_axis=1, concat_axis=0, tiled=True)  15.5 us
    ppermute x5, waiting for transfers between devices, swap_sides(): lax.ppermute(value, ('z', 'y'), [(2 * i + j, 2 * i + 1 - j) for i in laye...  14.3 us
    all_to_all x1, starting transfers between devices, shards(): up = lax.all_to_all(up, ADP, split_axis=1, concat_axis=0, tiled=True)  14.1 us
    all_to_all x1, waiting for transfers between devices, shards(): lax.all_to_all(query, ADP, split_axis=0, concat_axis=1, tiled=True)  11.9 us
    ppermute x5, starting transfers between devices, swap_sides(): lax.ppermute(value, ('z', 'y'), [(2 * i + j, 2 * i + 1 - j) for i in laye...  11.2 us
    pallas_call x2, Pallas kernels, output_partial(): pl.pallas_call(output_kernel, grid_spec=pltpu.PrefetchScalarGridSpec(num_...  11.1 us
  transfers between devices with their start and end apart: 31, of which 19 were waited for; matrix products, arithmetic and copies ran while one was open for 11% of the time, Pallas kernels for 17%

profile of v1, /device:TPU:0, one launch (start us, length us, event | category | flops | bytes accessed | tf_op | source)
XLA Modules:
  0.0 213.9 jit_solution(2270472107811334703)
XLA Ops:
  0.5 4.9 %collective-permute-start = (bf16[384,512]{1,0:T(8,128)(2,1)}, bf16[384,512]{1,0:T(8,128)(2,1)S(1)}, u32[]{:S(2)}, u32[]{:S(2)}) collective-permute-start(bf16[384,512]{1,0:T(8,128)(2,1)} %refs_0_.5), channel_id=1, source_target_pairs={{0,4},{4,8},{8,12},{1,5},{5,9},{9,13},{2,6},{6,10},{10,14},{3,7},{... | collective-permute-start | bytes 1179656 | tf_op jit(solution)/shard_map/ppermute | solution.py:235
  5.5 1.6 collective-permute-start.8
  7.0 1.3 collective-permute-start.2
  8.3 6.0 %collective-permute-done.refs_2_ = bf16[384,512]{1,0:T(8,128)(2,1)S(1)} collective-permute-done((bf16[384,512]{1,0:T(8,128)(2,1)}, bf16[384,512]{1,0:T(8,128)(2,1)S(1)}, u32[]{:S(2)}, u32[]{:S(2)}) %collective-permute-start) | collective-permute-done | bytes 393248 | tf_op jit(solution)/shard_map/ppermute | solution.py:235
  14.3 2.2 %collective-permute-done.8.refs_1_ = bf16[384,512]{1,0:T(8,128)(2,1)S(1)} collective-permute-done((bf16[384,512]{1,0:T(8,128)(2,1)}, bf16[384,512]{1,0:T(8,128)(2,1)S(1)}, u32[]{:S(2)}, u32[]{:S(2)}) %collective-permute-start.8) | collective-permute-done | bytes 393248 | tf_op jit(solution)/shard_map/ppermute | solution.py:221
  16.6 1.4 collective-permute-start.9
  18.0 1.7 collective-permute-done.2.refs_4_
  19.7 1.4 collective-permute-start.1
  21.1 1.3 collective-permute-start.3
  22.4 0.8 copy.64
  23.3 14.1 %all-to-all-start = ((bf16[32,16,512]{2,0,1:T(8,128)(2,1)}), bf16[32,16,512]{2,0,1:T(8,128)(2,1)S(1)}, u32[]{:S(2)}, u32[]{:S(2)}) async-start(bf16[32,16,512]{2,0,1:T(8,128)(2,1)} %bitcast.50), calls=%async_computation | async-start | bytes 1048576 | tf_op jit(solution)/shard_map/all_to_all | solution.py:315
  37.4 3.8 %collective-permute-start.10 = (bf16[384,512]{1,0:T(8,128)(2,1)S(1)}, bf16[384,512]{1,0:T(8,128)(2,1)}, u32[]{:S(2)}, u32[]{:S(2)}) collective-permute-start(bf16[384,512]{1,0:T(8,128)(2,1)S(1)} %collective-permute-done.2.refs_4_), channel_id=1, source_target_pairs={{0,2},{2,0},{4,6},{6,4},{8,10},{10,8},{1,3},{3,1},{5,7},{7,5},{9,1... | collective-permute-start | bytes 1179656 | tf_op jit(solution)/shard_map/ppermute | solution.py:221
  41.3 3.2 %collective-permute-start.5 = (bf16[384,512]{1,0:T(8,128)(2,1)}, bf16[384,512]{1,0:T(8,128)(2,1)}, u32[]{:S(2)}, u32[]{:S(2)}) collective-permute-start(bf16[384,512]{1,0:T(8,128)(2,1)} %refs_0_.5), channel_id=1, source_target_pairs={{0,12},{12,0},{1,13},{13,1},{2,14},{14,2},{3,15},{15,3},{16,28},{2... | collective-permute-start | bytes 1179656 | tf_op jit(solution)/shard_map/ppermute | solution.py:240
  44.5 1.1 broadcast_select_fusion.refs_0_
  45.6 9.1 %collective-permute-done.10.refs_5_ = bf16[384,512]{1,0:T(8,128)(2,1)} collective-permute-done((bf16[384,512]{1,0:T(8,128)(2,1)S(1)}, bf16[384,512]{1,0:T(8,128)(2,1)}, u32[]{:S(2)}, u32[]{:S(2)}) %collective-permute-start.10) | collective-permute-done | bytes 393248 | tf_op jit(solution)/shard_map/ppermute | solution.py:221
  54.6 1.0 collective-permute-start.4
  55.7 3.8 %collective-permute-done.5.refs_2_ = bf16[384,512]{1,0:T(8,128)(2,1)} collective-permute-done((bf16[384,512]{1,0:T(8,128)(2,1)}, bf16[384,512]{1,0:T(8,128)(2,1)}, u32[]{:S(2)}, u32[]{:S(2)}) %collective-permute-start.5) | collective-permute-done | bytes 393248 | tf_op jit(solution)/shard_map/ppermute | solution.py:240
  59.5 3.4 %collective-permute-start.6 = (bf16[384,512]{1,0:T(8,128)(2,1)}, bf16[384,512]{1,0:T(8,128)(2,1)}, u32[]{:S(2)}, u32[]{:S(2)}) collective-permute-start(bf16[384,512]{1,0:T(8,128)(2,1)} %collective-permute-done.5.refs_2_), channel_id=1, source_target_pairs={{0,2},{2,0},{12,14},{14,12},{1,3},{3,1},{13,15},{15,13},{16,18},{1... | collective-permute-start | bytes 1179656 | tf_op jit(solution)/shard_map/ppermute | solution.py:221
  63.0 0.7 reduce
  63.7 0.6 stack.96.places
  64.3 0.7 stack.105.places
  65.0 0.7 select_reduce_fusion
  65.8 1.0 copy-done.2
  66.9 4.3 %shard_map.120.refs_12_ = f32[384,128]{1,0:T(8,128)} custom-call(s32[12]{0:T(128)} %stack.105.places, bf16[384,512]{1,0:T(8,128)(2,1)} %refs_0_.5, bf16[384,512]{1,0:T(8,128)(2,1)} %copy-done.8, bf16[384,512]{1,0:T(8,128)(2,1)} %copy-done.7, bf16[384,512]{1,0:T(8,128)(2,1)} %collective-permute-done.9.refs_3_, bf16[384,512]{1,0:T(8,128)(2,1)} %copy-done.9, ...), custom_call_target="tpu_custom_call" | custom-call | flops 301989888 | bytes 3145728 | tf_op jit(solution)/shard_map/pallas_call | solution.py:42
  71.2 3.0 %collective-permute-done.6.refs_3_ = bf16[384,512]{1,0:T(8,128)(2,1)} collective-permute-done((bf16[384,512]{1,0:T(8,128)(2,1)}, bf16[384,512]{1,0:T(8,128)(2,1)}, u32[]{:S(2)}, u32[]{:S(2)}) %collective-permute-start.6) | collective-permute-done | bytes 393248 | tf_op jit(solution)/shard_map/ppermute | solution.py:221
  74.2 4.0 %shard_map.121 = f32[384,128]{1,0:T(8,128)} custom-call(s32[8]{0:T(128)} %stack.96.places, bf16[384,512]{1,0:T(8,128)(2,1)} %copy-done.4, bf16[384,512]{1,0:T(8,128)(2,1)} %collective-permute-done.4.refs_1_, bf16[384,512]{1,0:T(8,128)(2,1)} %collective-permute-done.5.refs_2_, bf16[384,512]{1,0:T(8,128)(2,1)} %collective-permute-done.6.refs_3_, ...), custom_call_target="tpu_custom_call" | custom-call | flops 201326592 | bytes 2097152 | tf_op jit(solution)/shard_map/pallas_call | solution.py:42
  78.2 1.6 collective-permute-done.13
  79.8 1.0 add.291
  81.0 8.8 %shard_map.118 = (f32[384,512]{1,0:T(8,128)}, f32[384,512]{1,0:T(8,128)}) custom-call(s32[12]{0:T(128)} %stack.105.places, bf16[384,512]{1,0:T(8,128)(2,1)} %refs_0_.5, bf16[384,512]{1,0:T(8,128)(2,1)} %copy-done.8, bf16[384,512]{1,0:T(8,128)(2,1)} %copy-done.7, bf16[384,512]{1,0:T(8,128)(2,1)} %collective-permute-done.9.refs_3_, ...), custom_call_target="tpu_custom_call" | custom-call | flops 2415919104 | bytes 10223616 | tf_op jit(solution)/shard_map/pallas_call | solution.py:82
  89.9 8.5 %shard_map.119 = (f32[384,512]{1,0:T(8,128)}, f32[384,512]{1,0:T(8,128)}) custom-call(s32[8]{0:T(128)} %stack.96.places, bf16[384,512]{1,0:T(8,128)(2,1)} %copy-done.4, bf16[384,512]{1,0:T(8,128)(2,1)} %collective-permute-done.4.refs_1_, bf16[384,512]{1,0:T(8,128)(2,1)} %collective-permute-done.5.refs_2_, bf16[384,512]{1,0:T(8,128)(2,1)} %collective-permute-done.6.refs_3_, ...), custom_call_target="tpu_custom_call" | custom-call | flops 1610612736 | bytes 7340032 | tf_op jit(solution)/shard_map/pallas_call | solution.py:82
  98.7 1.1 collective-permute-start.14
  99.8 1.5 collective-permute-start.18
  101.3 1.6 collective-permute-done.14
  103.1 5.9 %collective-permute-done.15 = bf16[192,128]{1,0:T(8,128)(2,1)S(1)} collective-permute-done((bf16[192,128]{1,0:T(8,128)(2,1)S(1)}, bf16[192,128]{1,0:T(8,128)(2,1)S(1)}, u32[]{:S(2)}, u32[]{:S(2)}) %collective-permute-start.15) | collective-permute-done | bytes 49184 | tf_op jit(solution)/shard_map/ppermute | solution.py:213
  109.0 0.8 reduce_sum.23.slot
  109.8 3.3 %collective-permute-done.17 = bf16[192,128]{1,0:T(8,128)(2,1)S(1)} collective-permute-done((bf16[192,128]{1,0:T(8,128)(2,1)S(1)}, bf16[192,128]{1,0:T(8,128)(2,1)S(1)}, u32[]{:S(2)}, u32[]{:S(2)}) %collective-permute-start.17) | collective-permute-done | bytes 49184 | tf_op jit(solution)/shard_map/ppermute | solution.py:213
  113.1 0.6 add_add_fusion.low
  113.8 0.8 copy-done.11
  114.9 3.6 %shard_map.122 = bf16[384,512]{1,0:T(8,128)(2,1)} custom-call(s32[1]{0:T(128)} %bitcast.6.half, f32[384,512]{1,0:T(8,128)} %get-tuple-element.31.own, f32[384,512]{1,0:T(8,128)} %copy-done.10, bf16[192,128]{1,0:T(8,128)(2,1)} %add_add_fusion.low, s32[384,1]{1,0:T(8,128)} %reduce_sum.23.slot, bf16[512,512]{1,0:T(8,128)(2,1)} %bitcast.67, ...), custom_call_target="tpu_custom_call" | custom-call | flops 402653184 | bytes 3014656 | tf_op jit(solution)/shard_map/pallas_call | solution.py:128
  118.4 3.7 %all-to-all-start.1 = ((bf16[16,24,512]{2,1,0:T(8,128)(2,1)}), bf16[16,24,512]{2,1,0:T(8,128)(2,1)S(1)}, u32[]{:S(2)}, u32[]{:S(2)}) async-start(bf16[16,24,512]{2,1,0:T(8,128)(2,1)} %bitcast.69), calls=%async_computation.1 | async-start | bytes 786432 | tf_op jit(solution)/shard_map/all_to_all | solution.py:341
  122.4 11.9 %all-to-all-done.1 = bf16[16,24,512]{2,1,0:T(8,128)(2,1)S(1)} async-done(((bf16[16,24,512]{2,1,0:T(8,128)(2,1)}), bf16[16,24,512]{2,1,0:T(8,128)(2,1)S(1)}, u32[]{:S(2)}, u32[]{:S(2)}) %all-to-all-start.1) | async-done | bytes 393248 | tf_op jit(solution)/shard_map/all_to_all | solution.py:341
  134.9 5.5 %fusion.18 = (f32[8,24,8]{2,1,0:T(8,128)S(1)}, f32[8,24,8,128]{3,2,1,0:T(8,128)S(1)}) fusion(bf16[8,24,128,128]{3,2,1,0:T(8,128)(2,1)} %param.19, bf16[24,8,8,128]{3,2,1,0:T(8,128)(2,1)S(1)} %reshape.57, pred[24,128]{1,0:T(8,128)(4,1)S(1)} %iota_compare_fusion.1), kind=kOutput, calls=%fused_computation.38 | convolution fusion | flops 50723328 | bytes 7480320 | tf_op jit(solution)/shard_map/rkge,krje->krgj/dot_general | solution.py:197
  141.1 4.6 %fusion.5 = bf16[24,8,8,128]{3,2,1,0:T(8,128)(2,1)S(1)} fusion(bf16[8,24,128,128]{3,2,1,0:T(8,128)(2,1)} %param.20, f32[24,8,128]{2,1,0:T(8,128)S(1)} %bitcast.72, f32[24,8,8]{2,1,0:T(8,128)S(1)} %copy.40, f32[8,24,8,128]{3,2,1,0:T(8,128)S(1)} %get-tuple-element.52, f32[8,24,8]{2,1,0:T(8,128)S(1)} %get-tuple-element.46, f32[8,24,8]{2,1,0:T(8,128)S(1)} %max.3, ...), kind=kOutput, calls=%fused_computation.4 | convolution fusion | flops 51707904 | bytes 7590912 | tf_op jit(solution)/shard_map/krgj,krje->rkge/dot_general | solution.py:206
  146.2 15.5 %all_to_all.54 = bf16[24,16,512]{2,0,1:T(8,128)(2,1)S(1)} all-to-all(bf16[24,16,512]{2,0,1:T(8,128)(2,1)S(1)} %copy.41), channel_id=1, replica_groups=mesh['rep'=2,'z'=4,'y'=2,'core'=2] {'z','y','core'}, dimensions={1} | all-to-all | bytes 786432 | tf_op jit(solution)/shard_map/all_to_all | solution.py:346
  162.4 1.1 collective-permute-done.19.other
  163.5 0.7 copy-done.6
  164.2 4.2 %shard_map.124 = (bf16[384,512]{1,0:T(8,128)(2,1)}, bf16[384,512]{1,0:T(8,128)(2,1)}) custom-call(s32[2]{0:T(128)} %pad_add_fusion.places, bf16[384,512]{1,0:T(8,128)(2,1)} %bitcast.63, bf16[384,512]{1,0:T(8,128)(2,1)} %copy-done.6, bf16[512,8192]{1,0:T(8,128)(2,1)} %refs_1_.3, bf16[512,8192]{1,0:T(8,128)(2,1)} %refs_1_.3, ...), custom_call_target="tpu_custom_call" | custom-call | flops 805306368 | bytes 3670016 | tf_op jit(solution)/shard_map/pallas_call | solution.py:171
  169.6 6.8 %shard_map.123 = (bf16[384,512]{1,0:T(8,128)(2,1)}, bf16[384,512]{1,0:T(8,128)(2,1)}, bf16[384,512]{1,0:T(8,128)(2,1)}, bf16[384,512]{1,0:T(8,128)(2,1)}, bf16[3...) custom-call(s32[6]{0:T(128)} %stack.89.places, bf16[384,512]{1,0:T(8,128)(2,1)} %bitcast.64, bf16[384,512]{1,0:T(8,128)(2,1)} %copy-done.6, ...), custom_call_target="tpu_custom_call" | custom-call | flops 2415919104 | bytes 9437184 | tf_op jit(solution)/shard_map/pallas_call | solution.py:171
  176.5 1.5 collective-permute-start.22
  178.0 2.2 %collective-permute-done.23 = bf16[384,512]{1,0:T(8,128)(2,1)S(1)} collective-permute-done((bf16[384,512]{1,0:T(8,128)(2,1)}, bf16[384,512]{1,0:T(8,128)(2,1)S(1)}, u32[]{:S(2)}, u32[]{:S(2)}) %collective-permute-start.23) | collective-permute-done | bytes 393248 | tf_op jit(solution)/shard_map/ppermute | solution.py:213
  180.2 3.1 %collective-permute-start.24 = (bf16[384,512]{1,0:T(8,128)(2,1)S(1)}, bf16[384,512]{1,0:T(8,128)(2,1)S(1)}, u32[]{:S(2)}, u32[]{:S(2)}) collective-permute-start(bf16[384,512]{1,0:T(8,128)(2,1)S(1)} %add_convert_fusion.3), channel_id=1, source_target_pairs={{0,4},{4,8},{1,5},{5,9},{2,6},{6,10},{3,7},{7,11},{16,20},{20,24},... | collective-permute-start | bytes 1179656 | tf_op jit(solution)/shard_map/ppermute | solution.py:261
  183.9 0.7 collective-permute-start.27
  184.6 1.6 collective-permute-start.21
  186.2 2.5 %collective-permute-done.22 = bf16[384,512]{1,0:T(8,128)(2,1)S(1)} collective-permute-done((bf16[384,512]{1,0:T(8,128)(2,1)}, bf16[384,512]{1,0:T(8,128)(2,1)S(1)}, u32[]{:S(2)}, u32[]{:S(2)}) %collective-permute-start.22) | collective-permute-done | bytes 393248 | tf_op jit(solution)/shard_map/ppermute | solution.py:213
  188.7 2.3 %collective-permute-done.24 = bf16[384,512]{1,0:T(8,128)(2,1)S(1)} collective-permute-done((bf16[384,512]{1,0:T(8,128)(2,1)S(1)}, bf16[384,512]{1,0:T(8,128)(2,1)S(1)}, u32[]{:S(2)}, u32[]{:S(2)}) %collective-permute-start.24) | collective-permute-done | bytes 393248 | tf_op jit(solution)/shard_map/ppermute | solution.py:261
  191.0 1.1 add_convert_fusion.2
  192.2 2.5 %collective-permute-start.25 = (bf16[384,512]{1,0:T(8,128)(2,1)S(1)}, bf16[384,512]{1,0:T(8,128)(2,1)S(1)}, u32[]{:S(2)}, u32[]{:S(2)}) collective-permute-start(bf16[384,512]{1,0:T(8,128)(2,1)S(1)} %add_convert_fusion.2), channel_id=1, source_target_pairs={{0,4},{4,8},{8,12},{12,0},{1,5},{5,9},{9,13},{13,1},{2,6},{6,10},{... | collective-permute-start | bytes 1179656 | tf_op jit(solution)/shard_map/ppermute | solution.py:213
  194.7 2.4 %collective-permute-done.26 = bf16[384,512]{1,0:T(8,128)(2,1)S(1)} collective-permute-done((bf16[384,512]{1,0:T(8,128)(2,1)}, bf16[384,512]{1,0:T(8,128)(2,1)S(1)}, u32[]{:S(2)}, u32[]{:S(2)}) %collective-permute-start.26) | collective-permute-done | bytes 393248 | tf_op jit(solution)/shard_map/ppermute | solution.py:213
  197.1 1.1 add_convert_fusion.1
  198.3 2.2 %collective-permute-start.28 = (bf16[384,512]{1,0:T(8,128)(2,1)S(1)}, bf16[384,512]{1,0:T(8,128)(2,1)S(1)}, u32[]{:S(2)}, u32[]{:S(2)}) collective-permute-start(bf16[384,512]{1,0:T(8,128)(2,1)S(1)} %add_convert_fusion.1), channel_id=1, source_target_pairs={{0,12},{4,0},{8,4},{12,8},{1,13},{5,1},{9,5},{13,9},{2,14},{6,2},{... | collective-permute-start | bytes 1179656 | tf_op jit(solution)/shard_map/ppermute | solution.py:213
  200.4 4.6 %collective-permute-done.21 = bf16[384,512]{1,0:T(8,128)(2,1)S(1)} collective-permute-done((bf16[384,512]{1,0:T(8,128)(2,1)}, bf16[384,512]{1,0:T(8,128)(2,1)S(1)}, u32[]{:S(2)}, u32[]{:S(2)}) %collective-permute-start.21) | collective-permute-done | bytes 393248 | tf_op jit(solution)/shard_map/ppermute | solution.py:213
  205.1 0.8 collective-permute-done.25
  205.9 6.0 %collective-permute-done.28 = bf16[384,512]{1,0:T(8,128)(2,1)S(1)} collective-permute-done((bf16[384,512]{1,0:T(8,128)(2,1)S(1)}, bf16[384,512]{1,0:T(8,128)(2,1)S(1)}, u32[]{:S(2)}, u32[]{:S(2)}) %collective-permute-start.28) | collective-permute-done | bytes 393248 | tf_op jit(solution)/shard_map/ppermute | solution.py:213
  211.9 1.9 add_convert_fusion
  (75 shorter events, 6.1 us)
Async XLA Ops:
  0.0 22.4 %copy-start = (bf16[1,8192,64]{1,2,0:T(8,128)(2,1)S(1)}, bf16[1,8192,64]{1,2,0:T(8,128)(2,1)}, u32[]{:S(2)}) copy-start(bf16[1,8192,64]{1,2,0:T(8,128)(2,1)} %param.18) | copy-start | bytes 3145732
  0.0 81.0 %collective-permute-start.7 = (bf16[8192,512]{1,0:T(8,128)(2,1)}, bf16[8192,512]{1,0:T(8,128)(2,1)}, u32[]{:S(2)}, u32[]{:S(2)}) collective-permute-start(bf16[8192,512]{1,0:T(8,128)(2,1)} %refs_7_.3), channel_id=1, source_target_pairs={{0,1},{1,0},{2,3},{3,2},{4,5},{5,4},{6,7},{7,6},{8,9},{9,8},{10,11... | collective-permute-start | bytes 25165832 | tf_op jit(solution)/shard_map/ppermute | solution.py:213
  0.5 162.0 %collective-permute-start.20 = (bf16[512,8192]{1,0:T(8,128)(2,1)}, bf16[512,8192]{1,0:T(8,128)(2,1)}, u32[]{:S(2)}, u32[]{:S(2)}) collective-permute-start(bf16[512,8192]{1,0:T(8,128)(2,1)} %refs_1_.3), channel_id=1, source_target_pairs={{0,1},{1,0},{2,3},{3,2},{4,5},{5,4},{6,7},{7,6},{8,9},{9,8},{10,11... | collective-permute-start | bytes 25165832 | tf_op jit(solution)/shard_map/ppermute | solution.py:213
  0.5 13.8 %collective-permute-start = (bf16[384,512]{1,0:T(8,128)(2,1)}, bf16[384,512]{1,0:T(8,128)(2,1)S(1)}, u32[]{:S(2)}, u32[]{:S(2)}) collective-permute-start(bf16[384,512]{1,0:T(8,128)(2,1)} %refs_0_.5), channel_id=1, source_target_pairs={{0,4},{4,8},{8,12},{1,5},{5,9},{9,13},{2,6},{6,10},{10,14},{3,7},{... | collective-permute-start | bytes 1179656 | tf_op jit(solution)/shard_map/ppermute | solution.py:235
  5.5 11.1 %collective-permute-start.8 = (bf16[384,512]{1,0:T(8,128)(2,1)}, bf16[384,512]{1,0:T(8,128)(2,1)S(1)}, u32[]{:S(2)}, u32[]{:S(2)}) collective-permute-start(bf16[384,512]{1,0:T(8,128)(2,1)} %refs_0_.5), channel_id=1, source_target_pairs={{0,2},{2,0},{4,6},{6,4},{8,10},{10,8},{12,14},{14,12},{1,3},{3,1},... | collective-permute-start | bytes 1179656 | tf_op jit(solution)/shard_map/ppermute | solution.py:221
  7.0 12.6 %collective-permute-start.2 = (bf16[384,512]{1,0:T(8,128)(2,1)}, bf16[384,512]{1,0:T(8,128)(2,1)S(1)}, u32[]{:S(2)}, u32[]{:S(2)}) collective-permute-start(bf16[384,512]{1,0:T(8,128)(2,1)} %refs_0_.5), channel_id=1, source_target_pairs={{4,0},{8,4},{12,8},{5,1},{9,5},{13,9},{6,2},{10,6},{14,10},{7,3},{... | collective-permute-start | bytes 1179656 | tf_op jit(solution)/shard_map/ppermute | solution.py:236
  14.3 51.4 %copy-start.7 = (bf16[384,512]{1,0:T(8,128)(2,1)}, bf16[384,512]{1,0:T(8,128)(2,1)S(1)}, u32[]{:S(2)}) copy-start(bf16[384,512]{1,0:T(8,128)(2,1)S(1)} %collective-permute-done.refs_2_) | copy-start | bytes 1179652
  16.6 49.3 %copy-start.8 = (bf16[384,512]{1,0:T(8,128)(2,1)}, bf16[384,512]{1,0:T(8,128)(2,1)S(1)}, u32[]{:S(2)}) copy-start(bf16[384,512]{1,0:T(8,128)(2,1)S(1)} %collective-permute-done.8.refs_1_) | copy-start | bytes 1179652
  16.6 4.5 %collective-permute-start.9 = (bf16[384,512]{1,0:T(8,128)(2,1)S(1)}, bf16[384,512]{1,0:T(8,128)(2,1)}, u32[]{:S(2)}, u32[]{:S(2)}) collective-permute-start(bf16[384,512]{1,0:T(8,128)(2,1)S(1)} %collective-permute-done.refs_2_), channel_id=1, source_target_pairs={{4,6},{6,4},{8,10},{10,8},{12,14},{14,12},{5,7},{7,5},{9,11},{11,9... | collective-permute-start | bytes 1179656 | tf_op jit(solution)/shard_map/ppermute | solution.py:221
  18.0 47.8 %collective-permute-start.12 = (bf16[1,64,8192]{2,1,0:T(8,128)(2,1)}, bf16[1,64,8192]{2,1,0:T(8,128)(2,1)S(1)}, u32[]{:S(2)}, u32[]{:S(2)}) collective-permute-start(bf16[1,64,8192]{2,1,0:T(8,128)(2,1)} %bitcast.51), channel_id=1, source_target_pairs={{0,1},{1,0},{2,3},{3,2},{4,5},{5,4},{6,7},{7,6},{8,9},{9,8},{10,11... | collective-permute-start | bytes 3145736 | tf_op jit(solution)/shard_map/ppermute | solution.py:213
  19.7 46.1 %copy-start.9 = (bf16[384,512]{1,0:T(8,128)(2,1)}, bf16[384,512]{1,0:T(8,128)(2,1)S(1)}, u32[]{:S(2)}) copy-start(bf16[384,512]{1,0:T(8,128)(2,1)S(1)} %collective-permute-done.2.refs_4_) | copy-start | bytes 1179652
  19.7 17.7 %collective-permute-start.1 = (bf16[384,512]{1,0:T(8,128)(2,1)S(1)}, bf16[384,512]{1,0:T(8,128)(2,1)}, u32[]{:S(2)}, u32[]{:S(2)}) collective-permute-start(bf16[384,512]{1,0:T(8,128)(2,1)S(1)} %collective-permute-done.refs_2_), channel_id=1, source_target_pairs={{4,8},{8,12},{5,9},{9,13},{6,10},{10,14},{7,11},{11,15},{20,24},{2... | collective-permute-start | bytes 1179656 | tf_op jit(solution)/shard_map/ppermute | solution.py:239
  21.1 20.2 %collective-permute-start.3 = (bf16[384,512]{1,0:T(8,128)(2,1)S(1)}, bf16[384,512]{1,0:T(8,128)(2,1)}, u32[]{:S(2)}, u32[]{:S(2)}) collective-permute-start(bf16[384,512]{1,0:T(8,128)(2,1)S(1)} %collective-permute-done.2.refs_4_), channel_id=1, source_target_pairs={{8,4},{4,0},{9,5},{5,1},{10,6},{6,2},{11,7},{7,3},{24,20},{20,16},... | collective-permute-start | bytes 1179656 | tf_op jit(solution)/shard_map/ppermute | solution.py:239
  23.3 42.5 %all-to-all-start = ((bf16[32,16,512]{2,0,1:T(8,128)(2,1)}), bf16[32,16,512]{2,0,1:T(8,128)(2,1)S(1)}, u32[]{:S(2)}, u32[]{:S(2)}) async-start(bf16[32,16,512]{2,0,1:T(8,128)(2,1)} %bitcast.50), calls=%async_computation | async-start | bytes 1048576 | tf_op jit(solution)/shard_map/all_to_all | solution.py:315
  37.4 17.2 %collective-permute-start.10 = (bf16[384,512]{1,0:T(8,128)(2,1)S(1)}, bf16[384,512]{1,0:T(8,128)(2,1)}, u32[]{:S(2)}, u32[]{:S(2)}) collective-permute-start(bf16[384,512]{1,0:T(8,128)(2,1)S(1)} %collective-permute-done.2.refs_4_), channel_id=1, source_target_pairs={{0,2},{2,0},{4,6},{6,4},{8,10},{10,8},{1,3},{3,1},{5,7},{7,5},{9,1... | collective-permute-start | bytes 1179656 | tf_op jit(solution)/shard_map/ppermute | solution.py:221
  41.3 18.2 %collective-permute-start.5 = (bf16[384,512]{1,0:T(8,128)(2,1)}, bf16[384,512]{1,0:T(8,128)(2,1)}, u32[]{:S(2)}, u32[]{:S(2)}) collective-permute-start(bf16[384,512]{1,0:T(8,128)(2,1)} %refs_0_.5), channel_id=1, source_target_pairs={{0,12},{12,0},{1,13},{13,1},{2,14},{14,2},{3,15},{15,3},{16,28},{2... | collective-permute-start | bytes 1179656 | tf_op jit(solution)/shard_map/ppermute | solution.py:240
  45.5 28.7 %copy-start.4 = (bf16[384,512]{1,0:T(8,128)(2,1)}, bf16[384,512]{1,0:T(8,128)(2,1)S(1)}, u32[]{:S(2)}) copy-start(bf16[384,512]{1,0:T(8,128)(2,1)S(1)} %broadcast_select_fusion.refs_0_) | copy-start | bytes 1179652
  54.6 16.5 %collective-permute-start.4 = (bf16[384,512]{1,0:T(8,128)(2,1)S(1)}, bf16[384,512]{1,0:T(8,128)(2,1)}, u32[]{:S(2)}, u32[]{:S(2)}) collective-permute-start(bf16[384,512]{1,0:T(8,128)(2,1)S(1)} %broadcast_select_fusion.refs_0_), channel_id=1, source_target_pairs={{0,2},{2,0},{4,6},{6,4},{8,10},{10,8},{12,14},{14,12},{1,3},{3,1},... | collective-permute-start | bytes 1179656 | tf_op jit(solution)/shard_map/ppermute | solution.py:221
  59.5 14.7 %collective-permute-start.6 = (bf16[384,512]{1,0:T(8,128)(2,1)}, bf16[384,512]{1,0:T(8,128)(2,1)}, u32[]{:S(2)}, u32[]{:S(2)}) collective-permute-start(bf16[384,512]{1,0:T(8,128)(2,1)} %collective-permute-done.5.refs_2_), channel_id=1, source_target_pairs={{0,2},{2,0},{12,14},{14,12},{1,3},{3,1},{13,15},{15,13},{16,18},{1... | collective-permute-start | bytes 1179656 | tf_op jit(solution)/shard_map/ppermute | solution.py:221
  65.8 34.0 %copy-start.5 = (bf16[32,16,512]{2,0,1:T(8,128)(2,1)}, bf16[32,16,512]{2,0,1:T(8,128)(2,1)S(1)}, u32[]{:S(2)}) copy-start(bf16[32,16,512]{2,0,1:T(8,128)(2,1)S(1)} %all-to-all-done) | copy-start | bytes 1572868
  65.8 1.0 copy-start.2
  78.2 1.7 collective-permute-start.13
  89.9 32.3 %copy-start.13 = (bf16[24,1024]{1,0:T(8,128)(2,1)S(1)}, bf16[24,1024]{1,0:T(8,128)(2,1)}, u32[]{:S(2)}) copy-start(bf16[24,1024]{1,0:T(8,128)(2,1)} %param.21) | copy-start | bytes 147460
  89.9 32.3 %copy-start.14 = (bf16[24,1024]{1,0:T(8,128)(2,1)S(1)}, bf16[24,1024]{1,0:T(8,128)(2,1)}, u32[]{:S(2)}) copy-start(bf16[24,1024]{1,0:T(8,128)(2,1)} %param.22) | copy-start | bytes 147460
  89.9 32.4 %copy-start.15 = (s32[24]{0:T(128)S(1)}, s32[24]{0:T(128)}, u32[]{:S(2)}) copy-start(s32[24]{0:T(128)} %param.15) | copy-start | bytes 292
  98.4 15.3 %collective-permute-start.11 = (f32[384,512]{1,0:T(8,128)}, f32[384,512]{1,0:T(8,128)S(1)}, u32[]{:S(2)}, u32[]{:S(2)}) collective-permute-start(f32[384,512]{1,0:T(8,128)} %get-tuple-element.32), channel_id=1, source_target_pairs={{0,1},{1,0},{2,3},{3,2},{4,5},{5,4},{6,7},{7,6},{8,9},{9,8},{10,11... | collective-permute-start | bytes 2359304 | tf_op jit(solution)/shard_map/ppermute | solution.py:213
  98.7 4.2 %collective-permute-start.14 = (bf16[192,128]{1,0:T(8,128)(2,1)S(1)}, bf16[192,128]{1,0:T(8,128)(2,1)S(1)}, u32[]{:S(2)}, u32[]{:S(2)}) collective-permute-start(bf16[192,128]{1,0:T(8,128)(2,1)S(1)} %pad_maximum_fusion), channel_id=1, source_target_pairs={{0,2},{2,0},{1,3},{3,1},{4,6},{6,4},{5,7},{7,5},{8,10},{10,8},{9,1... | collective-permute-start | bytes 147464 | tf_op jit(solution)/shard_map/ppermute | solution.py:213
  99.8 14.0 %collective-permute-start.18 = (bf16[512,512]{1,0:T(8,128)(2,1)S(1)}, bf16[512,512]{1,0:T(8,128)(2,1)S(1)}, u32[]{:S(2)}, u32[]{:S(2)}) collective-permute-start(bf16[512,512]{1,0:T(8,128)(2,1)S(1)} %bitcast.66), channel_id=1, source_target_pairs={{0,16},{16,0},{1,17},{17,1},{2,18},{18,2},{3,19},{19,3},{4,20},{20... | collective-permute-start | bytes 1572872 | tf_op jit(solution)/shard_map/ppermute | solution.py:316
  103.0 6.0 %collective-permute-start.15 = (bf16[192,128]{1,0:T(8,128)(2,1)S(1)}, bf16[192,128]{1,0:T(8,128)(2,1)S(1)}, u32[]{:S(2)}, u32[]{:S(2)}) collective-permute-start(bf16[192,128]{1,0:T(8,128)(2,1)S(1)} %fusion.20), channel_id=1, source_target_pairs={{0,4},{4,8},{8,12},{12,0},{1,5},{5,9},{9,13},{13,1},{2,6},{6,10},{... | collective-permute-start | bytes 147464 | tf_op jit(solution)/shard_map/ppermute | solution.py:213
  103.1 6.8 %collective-permute-start.16 = (bf16[192,128]{1,0:T(8,128)(2,1)S(1)}, bf16[192,128]{1,0:T(8,128)(2,1)S(1)}, u32[]{:S(2)}, u32[]{:S(2)}) collective-permute-start(bf16[192,128]{1,0:T(8,128)(2,1)S(1)} %fusion.20), channel_id=1, source_target_pairs={{0,8},{4,12},{8,0},{12,4},{1,9},{5,13},{9,1},{13,5},{2,10},{6,14},... | collective-permute-start | bytes 147464 | tf_op jit(solution)/shard_map/ppermute | solution.py:213
  109.0 4.1 %collective-permute-start.17 = (bf16[192,128]{1,0:T(8,128)(2,1)S(1)}, bf16[192,128]{1,0:T(8,128)(2,1)S(1)}, u32[]{:S(2)}, u32[]{:S(2)}) collective-permute-start(bf16[192,128]{1,0:T(8,128)(2,1)S(1)} %fusion.20), channel_id=1, source_target_pairs={{0,12},{4,0},{8,4},{12,8},{1,13},{5,1},{9,5},{13,9},{2,14},{6,2},{... | collective-permute-start | bytes 147464 | tf_op jit(solution)/shard_map/ppermute | solution.py:213
  113.8 0.8 copy-start.11
  113.8 1.1 copy-start.10
  118.4 15.8 %all-to-all-start.1 = ((bf16[16,24,512]{2,1,0:T(8,128)(2,1)}), bf16[16,24,512]{2,1,0:T(8,128)(2,1)S(1)}, u32[]{:S(2)}, u32[]{:S(2)}) async-start(bf16[16,24,512]{2,1,0:T(8,128)(2,1)} %bitcast.69), calls=%async_computation.1 | async-start | bytes 786432 | tf_op jit(solution)/shard_map/all_to_all | solution.py:341
  161.7 1.7 copy-start.3
  161.7 1.7 collective-permute-start.19
  163.5 0.7 copy-start.6
  168.4 11.7 %collective-permute-start.23 = (bf16[384,512]{1,0:T(8,128)(2,1)}, bf16[384,512]{1,0:T(8,128)(2,1)S(1)}, u32[]{:S(2)}, u32[]{:S(2)}) collective-permute-start(bf16[384,512]{1,0:T(8,128)(2,1)} %get-tuple-element.41), channel_id=1, source_target_pairs={{0,2},{2,0},{1,3},{3,1},{4,6},{6,4},{5,7},{7,5},{8,10},{10,8},{9,1... | collective-permute-start | bytes 1179656 | tf_op jit(solution)/shard_map/ppermute | solution.py:213
  169.6 10.5 %copy-start.12 = (bf16[384,512]{1,0:T(8,128)(2,1)S(1)}, bf16[384,512]{1,0:T(8,128)(2,1)}, u32[]{:S(2)}) copy-start(bf16[384,512]{1,0:T(8,128)(2,1)} %get-tuple-element.40) | copy-start | bytes 1179652
  169.6 44.2 %copy-start.1 = (bf16[1,8192,64]{1,2,0:T(8,128)(2,1)S(1)}, bf16[1,8192,64]{1,2,0:T(8,128)(2,1)}, u32[]{:S(2)}) copy-start(bf16[1,8192,64]{1,2,0:T(8,128)(2,1)} %param.18) | copy-start | bytes 3145732
  176.5 12.2 %collective-permute-start.22 = (bf16[384,512]{1,0:T(8,128)(2,1)}, bf16[384,512]{1,0:T(8,128)(2,1)S(1)}, u32[]{:S(2)}, u32[]{:S(2)}) collective-permute-start(bf16[384,512]{1,0:T(8,128)(2,1)} %get-tuple-element.38), channel_id=1, source_target_pairs={{0,2},{2,0},{1,3},{3,1},{4,6},{6,4},{5,7},{7,5},{8,10},{10,8},{9,1... | collective-permute-start | bytes 1179656 | tf_op jit(solution)/shard_map/ppermute | solution.py:213
  180.2 10.8 %collective-permute-start.24 = (bf16[384,512]{1,0:T(8,128)(2,1)S(1)}, bf16[384,512]{1,0:T(8,128)(2,1)S(1)}, u32[]{:S(2)}, u32[]{:S(2)}) collective-permute-start(bf16[384,512]{1,0:T(8,128)(2,1)S(1)} %add_convert_fusion.3), channel_id=1, source_target_pairs={{0,4},{4,8},{1,5},{5,9},{2,6},{6,10},{3,7},{7,11},{16,20},{20,24},... | collective-permute-start | bytes 1179656 | tf_op jit(solution)/shard_map/ppermute | solution.py:261
  183.3 13.8 %collective-permute-start.26 = (bf16[384,512]{1,0:T(8,128)(2,1)}, bf16[384,512]{1,0:T(8,128)(2,1)S(1)}, u32[]{:S(2)}, u32[]{:S(2)}) collective-permute-start(bf16[384,512]{1,0:T(8,128)(2,1)} %get-tuple-element.44), channel_id=1, source_target_pairs={{0,2},{2,0},{1,3},{3,1},{4,6},{6,4},{5,7},{7,5},{8,10},{10,8},{9,1... | collective-permute-start | bytes 1179656 | tf_op jit(solution)/shard_map/ppermute | solution.py:213
  183.9 13.2 %collective-permute-start.27 = (bf16[384,512]{1,0:T(8,128)(2,1)S(1)}, bf16[384,512]{1,0:T(8,128)(2,1)S(1)}, u32[]{:S(2)}, u32[]{:S(2)}) collective-permute-start(bf16[384,512]{1,0:T(8,128)(2,1)S(1)} %add_convert_fusion.3), channel_id=1, source_target_pairs={{12,8},{8,4},{13,9},{9,5},{14,10},{10,6},{15,11},{11,7},{28,24},{2... | collective-permute-start | bytes 1179656 | tf_op jit(solution)/shard_map/ppermute | solution.py:262
  184.6 20.5 %collective-permute-start.21 = (bf16[384,512]{1,0:T(8,128)(2,1)}, bf16[384,512]{1,0:T(8,128)(2,1)S(1)}, u32[]{:S(2)}, u32[]{:S(2)}) collective-permute-start(bf16[384,512]{1,0:T(8,128)(2,1)} %get-tuple-element.35), channel_id=1, source_target_pairs={{0,2},{2,0},{1,3},{3,1},{4,6},{6,4},{5,7},{7,5},{8,10},{10,8},{9,1... | collective-permute-start | bytes 1179656 | tf_op jit(solution)/shard_map/ppermute | solution.py:213
  192.2 13.7 %collective-permute-start.25 = (bf16[384,512]{1,0:T(8,128)(2,1)S(1)}, bf16[384,512]{1,0:T(8,128)(2,1)S(1)}, u32[]{:S(2)}, u32[]{:S(2)}) collective-permute-start(bf16[384,512]{1,0:T(8,128)(2,1)S(1)} %add_convert_fusion.2), channel_id=1, source_target_pairs={{0,4},{4,8},{8,12},{12,0},{1,5},{5,9},{9,13},{13,1},{2,6},{6,10},{... | collective-permute-start | bytes 1179656 | tf_op jit(solution)/shard_map/ppermute | solution.py:213
  198.3 13.6 %collective-permute-start.28 = (bf16[384,512]{1,0:T(8,128)(2,1)S(1)}, bf16[384,512]{1,0:T(8,128)(2,1)S(1)}, u32[]{:S(2)}, u32[]{:S(2)}) collective-permute-start(bf16[384,512]{1,0:T(8,128)(2,1)S(1)} %add_convert_fusion.1), channel_id=1, source_target_pairs={{0,12},{4,0},{8,4},{12,8},{1,13},{5,1},{9,5},{13,9},{2,14},{6,2},{... | collective-permute-start | bytes 1179656 | tf_op jit(solution)/shard_map/ppermute | solution.py:213

commit v2 on v1

--- a/solution.py
+++ b/solution.py
@@ -13,90 +13,63 @@
 VMEM_LIMIT = 56 << 20
 
 
-def low_kernel(places, *refs):
-    count = places.shape[0] // 2
-    blocks, a_own, a_other = (refs[i * count : (i + 1) * count] for i in range(3))
-    out = refs[-1]
-    out[...] = refs[-2][...] if len(refs) > 3 * count + 1 else jnp.zeros_like(out)
+def project_kernel(places, *refs):
+    count = places.shape[0]
+    blocks, w_own, w_other, a_own, a_other = (refs[i * count : (i + 1) * count] for i in range(5))
+    ins, outs = refs[5 * count : -3], refs[-3:]
     first_core = places[0] % 2 == 0
+    sums = [ref[...] for ref in ins]
     for i in range(count):
-
-        @pl.when(places[count + i] > 0)
-        def _():
-            own, other = a_own[i][0], a_other[i][0]
-            pair = jnp.concatenate(
-                [jnp.where(first_core, own, other), jnp.where(first_core, other, own)], axis=0
-            )
-            out[...] += lax.dot_general(
-                blocks[i][...], pair, NT, preferred_element_type=jnp.float32
-            )
-
-
-def add_low(places, blocks, down, down_other, sums):
+        x = blocks[i][...]
+        own, other = a_own[i][0], a_other[i][0]
+        pair = jnp.concatenate(
+            [jnp.where(first_core, own, other), jnp.where(first_core, other, own)], axis=0
+        )
+        parts = (
+            jnp.dot(x, w_own[i][...], preferred_element_type=jnp.float32),
+            jnp.dot(x, w_other[i][...], preferred_element_type=jnp.float32),
+            lax.dot_general(x, pair, NT, preferred_element_type=jnp.float32),
+        )
+        sums = [total + part for total, part in zip(sums, parts)] if sums else parts
+    for out, total in zip(outs, sums):
+        out[...] = total
+
+
+def project(places, blocks, weight, weight_other, down, down_other, sums):
     count = len(blocks)
     rows, width = blocks[0].shape
-    rank = down.shape[1]
+    cols, rank = weight.shape[1], down.shape[1]
     flat = lambda shape: pl.BlockSpec(shape, lambda j, p: (0, 0))
-    shape = (rows, 2 * rank)
+    shapes = [(rows, cols), (rows, cols), (rows, 2 * rank)]
+    weights = [pl.BlockSpec((width, cols), lambda j, p, i=i: (p[i], 0)) for i in range(count)]
     maps = [pl.BlockSpec((1, rank, width), lambda j, p, i=i: (0, 0, p[i])) for i in range(count)]
-    return pl.pallas_call(
-        low_kernel,
-        grid_spec=pltpu.PrefetchScalarGridSpec(
-            num_scalar_prefetch=1,
-            grid=(1,),
-            in_specs=[flat((rows, width))] * count + maps * 2 + [flat(shape)] * len(sums),
-            out_specs=flat(shape),
-        ),
-        out_shape=jax.ShapeDtypeStruct(shape, jnp.float32),
-        compiler_params=pltpu.CompilerParams(vmem_limit_bytes=VMEM_LIMIT),
-        cost_estimate=pl.CostEstimate(
-            flops=4 * count * rows * width * rank,
-            bytes_accessed=2 * count * width * (rows + 2 * rank),
-            transcendentals=0,
-        ),
-    )(places, *blocks, *[down] * count, *[down_other] * count, *sums)
-
-
-def project_kernel(places, *refs):
-    count = places.shape[0] // 2
-    blocks, w_own, w_other = (refs[i * count : (i + 1) * count] for i in range(3))
-    outs = refs[-2:]
-    for j, (out, weights) in enumerate(zip(outs, (w_own, w_other))):
-        out[...] = refs[3 * count + j][...] if len(refs) > 3 * count + 2 else jnp.zeros_like(out)
-        for i in range(count):
-
-            @pl.when(places[count + i] > 0)
-            def _():
-                out[...] += jnp.dot(
-                    blocks[i][...], weights[i][...], preferred_element_type=jnp.float32
-                )
-
-
-def project(places, blocks, weight, weight_other, sums):
-    count = len(blocks)
-    rows, width = blocks[0].shape
-    cols = weight.shape[1]
-    tile = cols // 2 if cols % 256 == 0 else cols
-    sum_spec = pl.BlockSpec((rows, tile), lambda j, p: (0, j))
-    weights = [pl.BlockSpec((width, tile), lambda j, p, i=i: (p[i], j)) for i in range(count)]
     return pl.pallas_call(
         project_kernel,
         grid_spec=pltpu.PrefetchScalarGridSpec(
             num_scalar_prefetch=1,
-            grid=(cols // tile,),
-            in_specs=[pl.BlockSpec((rows, width), lambda j, p: (0, 0))] * count
+            grid=(1,),
+            in_specs=[flat((rows, width))] * count
             + weights * 2
-            + [sum_spec] * len(sums),
-            out_specs=[sum_spec] * 2,
-        ),
-        out_shape=[jax.ShapeDtypeStruct((rows, cols), jnp.float32)] * 2,
+            + maps * 2
+            + [flat(shape) for shape in shapes[: len(sums)]],
+            out_specs=[flat(shape) for shape in shapes],
+        ),
+        out_shape=[jax.ShapeDtypeStruct(shape, jnp.float32) for shape in shapes],
         compiler_params=pltpu.CompilerParams(vmem_limit_bytes=VMEM_LIMIT),
         cost_estimate=pl.CostEstimate(
-            flops=4 * count * rows * width * cols,
+            flops=4 * count * rows * width * (cols + rank),
             bytes_accessed=2 * count * width * (rows + 2 * cols) + 8 * rows * cols,
             transcendentals=0,
         ),
-    )(places, *blocks, *[weight] * count, *[weight_other] * count, *sums)
+    )(
+        places,
+        *blocks,
+        *[weight] * count,
+        *[weight_other] * count,
+        *[down] * count,
+        *[down_other] * count,
+        *sums,
+    )
 
 
 def query_kernel(half, own, received, low, slot, up_own, up_other, out):
@@ -217,10 +190,6 @@
     return lax.optimization_barrier((value, *others))[0]
 
 
-def swap_sides(value, layers):
-    return lax.ppermute(value, ("z", "y"), [(2 * i + j, 2 * i + 1 - j) for i in layers for j in (0, 1)])
-
-
 def gather_features(tokens):
     layers, sides = lax.axis_size("z"), lax.axis_size("y")
     z = lax.axis_index("z")
@@ -228,26 +197,22 @@
         entries = []
         for k in range(layers):
             block = shift(tokens, "z", k) if k else tokens
-            pair = [block, shift(block, "y", 1)] if sides == 2 else [block]
-            entries.append(((z - k) % layers, True, pair))
-        return [entries[:-1], entries[-1:]]
-    own_side = swap_sides(tokens, range(4))
-    below = lax.ppermute(tokens, "z", [(0, 1), (1, 2), (2, 3)])
-    above = lax.ppermute(tokens, "z", [(1, 0), (2, 1), (3, 2)])
-    below_side = swap_sides(after(below, own_side), (1, 2, 3))
-    above_side = swap_sides(above, (0, 1, 2))
-    two = lax.ppermute(below, "z", [(1, 2), (2, 3)]), lax.ppermute(above, "z", [(2, 1), (1, 0)])
-    far = lax.ppermute(after(tokens, below, above), "z", [(0, 3), (3, 0)])
-    two = jnp.where(z >= 2, *two)
-    two_side = swap_sides(two, range(4))
-    far_side = swap_sides(far, (0, 3))
+            entries.append(((z - k) % layers, [block, shift(block, "y", 1)][:sides]))
+        return entries
+    side = shift(tokens, "y", 1)
+    below, above = shift(tokens, "z", 1), shift(tokens, "z", 3)
+    from_below = lax.ppermute(below, "z", [(1, 2), (2, 3)])
+    from_above = lax.ppermute(above, "z", [(2, 1), (1, 0)])
+    below_side = shift(after(below, side), "y", 1)
+    above_side = shift(after(above, side), "y", 1)
+    two = jnp.where(z >= 2, from_below, from_above)
+    two = after(two, below_side, above_side)
+    two_side = shift(two, "y", 1)
     return [
-        [
-            (z, True, [tokens, own_side]),
-            ((z - 1) % 4, z >= 1, [below, below_side]),
-            ((z + 1) % 4, z <= 2, [above, above_side]),
-        ],
-        [((z + 2) % 4, True, [two, two_side]), (3 - z, (z == 0) | (z == 3), [far, far_side])],
+        (z, [tokens, side]),
+        ((z - 1) % 4, [below, below_side]),
+        ((z + 1) % 4, [above, above_side]),
+        ((z + 2) % 4, [two, two_side]),
     ]
 
 
@@ -299,34 +264,31 @@
         jnp.where(ids[:, None] == numbers[None, :], adapter_storage_slot[None, :], 0), axis=1
     )[:, None]
 
-    groups = []
-    for entries in gather_features(tokens):
-        chips = [chip for layer, _, _ in entries for chip in chips_of(layer)]
-        valid = [flag for _, flag, pair in entries for _ in pair]
-        places = [2 * chip + core for chip in chips] + valid
-        places = jnp.stack([jnp.asarray(place, jnp.int32) for place in places])
-        groups.append((places, [block for _, _, pair in entries for block in pair]))
+    entries = gather_features(tokens)
 
     reps = lax.axis_size("rep")
     half = lax.axis_index("rep") % 2
     up = jnp.swapaxes(adapter_up_maps, 1, 2)[0]
     up = lax.dynamic_slice_in_dim(up, half * (rank // 2), rank // 2, 0)
-    up = after(up, groups[0][1][2])
+    up = after(up, entries[-1][1][0])
     up = lax.all_to_all(up, ADP, split_axis=1, concat_axis=0, tiled=True)
     up_other = lax.ppermute(up, "rep", [(i, i ^ 1) for i in range(reps)])
 
-    sums, low = [], []
-    for index, (places, blocks) in enumerate(groups):
-        if index == 0:
+    sums = []
+    for group in (entries[:-1], entries[-1:]):
+        chips = [chip for layer, _ in group for chip in chips_of(layer)]
+        places = jnp.stack([2 * chip + core for chip in chips]).astype(jnp.int32)
+        blocks = [block for _, pair in group for block in pair]
+        if sums:
             places = after(places, up)
-        low = [add_low(places, blocks, down, down_other, low)]
-        if index:
-            low_other = shift(low[0], "core", 1)
-        sums = project(places, blocks, query_weight, query_weight_other, sums)
-    own, sent = sums
+        sums = project(
+            places, blocks, query_weight, query_weight_other, down, down_other, sums
+        )
+    own, sent, low = sums
+    low_other = shift(low, "core", 1)
     received = shift(sent, "core", 1)
 
-    low = low[0] + low_other
+    low = low + low_other
     chip = z * sides + y
     low = jnp.where(slot == 2 * chip, low[:, :rank], 0.0) + jnp.where(
         slot == 2 * chip + 1, low[:, rank:], 0.0
@@ -346,11 +308,12 @@
     context = lax.all_to_all(context, ADP, split_axis=1, concat_axis=0, tiled=True)
     context_other = shift(context, "core", 1)
 
+    order = [2, 1, 3, 0] if layers == 4 else list(range(1, layers)) + [0]
+    keys = [(k, side) for k in order for side in reversed(range(sides))]
     made = {}
-    order = [2, 1, 3, 0] if layers == 4 else list(range(1, layers)) + [0]
-    for group in (order[:1], order[1:]):
+    for group in (keys[:1], keys[1:]):
         outs = output_partial(
-            [chip for k in group for chip in chips_of(z + k)],
+            [chips_of(z + k)[side] for k, side in group],
             core,
             context,
             context_other,
@@ -358,12 +321,11 @@
             output_weight_other,
             width,
         )
-        for index, k in enumerate(group):
-            made[k] = outs[index * sides : (index + 1) * sides]
-    other_side = {k: shift(made[k][1], "y", 1) for k in order if sides == 2}
+        made.update(zip(group, outs))
+    other_side = {k: shift(made[k, 1], "y", 1) for k in order if sides == 2}
     parts = [None] * layers
     for k in order:
-        parts[k] = after(made[k][0], made[order[-1]][0]).astype(jnp.float32)
+        parts[k] = after(made[k, 0], made[keys[-1]]).astype(jnp.float32)
         if sides == 2:
             parts[k] = parts[k] + other_side[k].astype(jnp.float32)
     return scatter_layers(parts).astype(jnp.bfloat16)

time: 215 us -> 197 us (0.916)
  starting transfers between devices: 57.4 us -> 41.2 us
  Pallas kernels: 40.3 us -> 27.7 us
  waiting for transfers between devices: 72.2 us -> 81.4 us
    ppermute x10 -> x2, starting transfers between devices: 23.3 us -> 1.96 us  [the longest x1 1.28 us: gather_features(): from_above = lax.ppermute(above, 'z', [(2, 1), (1, 0)])]
    ppermute x16 -> x22, starting transfers between devices: 11 us -> 25 us  [shift(): lax.ppermute(value, axis, [(i, (i + by) % size) for i in range(size)])]
    ppermute x10 -> x2, waiting for transfers between devices: 25.9 us -> 13.7 us  [the longest x1 13.7 us: gather_features(): from_above = lax.ppermute(above, 'z', [(2, 1), (1, 0)])]
    ppermute x16 -> x22, waiting for transfers between devices: 32.1 us -> 43.1 us  [shift(): lax.ppermute(value, axis, [(i, (i + by) % size) for i in range(size)])]
    all_to_all x1, waiting for transfers between devices: 0.01 us -> 9.9 us  [shards(): up = lax.all_to_all(up, ADP, split_axis=1, concat_axis=0, tiled=True)]
    all_to_all x1, starting transfers between devices: 14.1 us -> 4.46 us  [shards(): up = lax.all_to_all(up, ADP, split_axis=1, concat_axis=0, tiled=True)]
    pallas_call x2 -> x0, Pallas kernels: 8.27 us -> none  [add_low(): pl.pallas_call(low_kernel, grid_spec=pltpu.PrefetchScalarGridSpec(num_sca...]
    pallas_call x2, Pallas kernels: 17.4 us -> 13.9 us  [project(): pl.pallas_call(project_kernel, grid_spec=pltpu.PrefetchScalarGridSpec(num...]
  transfers between devices with their start and end apart: 31 -> 29, of which waited for: 19 -> 18; matrix products, arithmetic and copies ran while one was open for 11% -> 12% of each run, Pallas kernels for 17% -> 13%
where the time goes in v2:
time: 197 us; the launch traced here: 196 us
  waiting for transfers between devices  81.4 us (41%)
  starting transfers between devices  41.2 us (21%)
  Pallas kernels  27.7 us (14%)
  blocking collectives  15.5 us (8%)
  other arithmetic  11.1 us (6%)
  matrix products  10.4 us (5%)
  local copies, waits for them, and re-layouts  8.24 us (4%)
    ppermute x22, waiting for transfers between devices, shift(): lax.ppermute(value, axis, [(i, (i + by) % size) for i in range(size)])  43.1 us
    ppermute x22, starting transfers between devices, shift(): lax.ppermute(value, axis, [(i, (i + by) % size) for i in range(size)])  25 us
    all_to_all x1, blocking collectives, shards(): lax.all_to_all(context, ADP, split_axis=1, concat_axis=0, tiled=True)  15.5 us
    pallas_call x2, Pallas kernels, project(): pl.pallas_call(project_kernel, grid_spec=pltpu.PrefetchScalarGridSpec(num...  13.9 us
    ppermute x1, waiting for transfers between devices, gather_features(): from_above = lax.ppermute(above, 'z', [(2, 1), (1, 0)])  13.7 us
    all_to_all x1, waiting for transfers between devices, shards(): lax.all_to_all(query, ADP, split_axis=0, concat_axis=1, tiled=True)  12 us
    pallas_call x2, Pallas kernels, output_partial(): pl.pallas_call(output_kernel, grid_spec=pltpu.PrefetchScalarGridSpec(num_...  10.2 us
    all_to_all x1, waiting for transfers between devices, shards(): up = lax.all_to_all(up, ADP, split_axis=1, concat_axis=0, tiled=True)  9.9 us
  transfers between devices with their start and end apart: 29, of which 18 were waited for; matrix products, arithmetic and copies ran while one was open for 12% of the time, Pallas kernels for 13%

profile of v2, /device:TPU:0, one launch (start us, length us, event | category | flops | bytes accessed | tf_op | source)
XLA Modules:
  0.0 196.0 jit_solution(7920388265894308193)
XLA Ops:
  0.5 3.0 %collective-permute-start = (bf16[384,512]{1,0:T(8,128)(2,1)}, bf16[384,512]{1,0:T(8,128)(2,1)S(1)}, u32[]{:S(2)}, u32[]{:S(2)}) collective-permute-start(bf16[384,512]{1,0:T(8,128)(2,1)} %refs_0_.3), channel_id=1, source_target_pairs={{0,4},{4,8},{8,12},{12,0},{1,5},{5,9},{9,13},{13,1},{2,6},{6,10},{... | collective-permute-start | bytes 1179656 | tf_op jit(solution)/shard_map/ppermute | solution.py:186
  3.5 1.5 collective-permute-start.4
  5.1 2.2 %collective-permute-start.2 = (bf16[384,512]{1,0:T(8,128)(2,1)}, bf16[384,512]{1,0:T(8,128)(2,1)}, u32[]{:S(2)}, u32[]{:S(2)}) collective-permute-start(bf16[384,512]{1,0:T(8,128)(2,1)} %refs_0_.3), channel_id=1, source_target_pairs={{0,12},{4,0},{8,4},{12,8},{1,13},{5,1},{9,5},{13,9},{2,14},{6,2},{... | collective-permute-start | bytes 1179656 | tf_op jit(solution)/shard_map/ppermute | solution.py:186
  7.3 8.4 %collective-permute-done.refs_2_ = bf16[384,512]{1,0:T(8,128)(2,1)S(1)} collective-permute-done((bf16[384,512]{1,0:T(8,128)(2,1)}, bf16[384,512]{1,0:T(8,128)(2,1)S(1)}, u32[]{:S(2)}, u32[]{:S(2)}) %collective-permute-start) | collective-permute-done | bytes 393248 | tf_op jit(solution)/shard_map/ppermute | solution.py:186
  15.7 0.7 collective-permute-start.1
  16.4 1.8 collective-permute-start.5
  18.3 5.4 %collective-permute-done.2.refs_4_ = bf16[384,512]{1,0:T(8,128)(2,1)} collective-permute-done((bf16[384,512]{1,0:T(8,128)(2,1)}, bf16[384,512]{1,0:T(8,128)(2,1)}, u32[]{:S(2)}, u32[]{:S(2)}) %collective-permute-start.2) | collective-permute-done | bytes 393248 | tf_op jit(solution)/shard_map/ppermute | solution.py:186
  23.7 1.2 collective-permute-start.6
  24.8 1.3 collective-permute-start.3
  26.2 13.7 %collective-permute-done.3 = bf16[384,512]{1,0:T(8,128)(2,1)S(1)} collective-permute-done((bf16[384,512]{1,0:T(8,128)(2,1)}, bf16[384,512]{1,0:T(8,128)(2,1)S(1)}, u32[]{:S(2)}, u32[]{:S(2)}) %collective-permute-start.3) | collective-permute-done | bytes 393248 | tf_op jit(solution)/shard_map/ppermute | solution.py:205
  39.9 0.8 copy-done.13
  40.7 1.0 broadcast_select_fusion.refs_0_
  41.7 0.9 copy.64
  42.6 4.5 %all-to-all-start = ((bf16[32,16,512]{2,0,1:T(8,128)(2,1)}), bf16[32,16,512]{2,0,1:T(8,128)(2,1)S(1)}, u32[]{:S(2)}, u32[]{:S(2)}) async-start(bf16[32,16,512]{2,0,1:T(8,128)(2,1)} %bitcast.45), calls=%async_computation | async-start | bytes 1048576 | tf_op jit(solution)/shard_map/all_to_all | solution.py:274
  47.1 1.9 collective-permute-start.7
  49.6 0.7 reduce
  50.3 0.6 stack.68.places
  50.9 0.7 select_reduce_fusion
  51.7 9.9 %all-to-all-done = bf16[32,16,512]{2,0,1:T(8,128)(2,1)S(1)} async-done(((bf16[32,16,512]{2,0,1:T(8,128)(2,1)}), bf16[32,16,512]{2,0,1:T(8,128)(2,1)S(1)}, u32[]{:S(2)}, u32[]{:S(2)}) %all-to-all-start) | async-done | bytes 524320 | tf_op jit(solution)/shard_map/all_to_all | solution.py:274
  61.6 1.0 copy-done.2
  62.6 8.5 %shard_map.118 = (f32[384,512]{1,0:T(8,128)}, f32[384,512]{1,0:T(8,128)}, f32[384,128]{1,0:T(8,128)}) custom-call(s32[6]{0:T(128)} %stack.68.places, bf16[384,512]{1,0:T(8,128)(2,1)} %refs_0_.3, bf16[384,512]{1,0:T(8,128)(2,1)} %copy-done.10, bf16[384,512]{1,0:T(8,128)(2,1)} %copy-done.9, bf16[384,512]{1,0:T(8,128)(2,1)} %collective-permute-done.5.refs_3_, ...), custom_call_target="tpu_custom_call" | custom-call | flops 2717908992 | bytes 10223616 | tf_op jit(solution)/shard_map/pallas_call | solution.py:46
  71.2 0.8 copy-done.11
  71.9 5.3 %shard_map.119 = (f32[384,512]{1,0:T(8,128)}, f32[384,512]{1,0:T(8,128)}, f32[384,128]{1,0:T(8,128)}) custom-call(s32[2]{0:T(128)} %pad_add_fusion.places, bf16[384,512]{1,0:T(8,128)(2,1)} %copy-done.5, bf16[384,512]{1,0:T(8,128)(2,1)} %copy-done.11, bf16[8192,512]{1,0:T(8,128)(2,1)} %refs_3_.2, bf16[8192,512]{1,0:T(8,128)(2,1)} %refs_3_.2, ...), custom_call_target="tpu_custom_call" | custom-call | flops 905969664 | bytes 4456448 | tf_op jit(solution)/shard_map/pallas_call | solution.py:46
  77.8 1.1 collective-permute-done.11
  78.9 0.9 add.272
  80.2 0.8 collective-permute-start.12
  81.1 1.5 collective-permute-start.16
  82.6 1.8 collective-permute-done.12
  84.5 1.5 collective-permute-start.13
  86.0 0.9 collective-permute-start.14
  86.9 3.5 %collective-permute-done.13 = bf16[192,128]{1,0:T(8,128)(2,1)S(1)} collective-permute-done((bf16[192,128]{1,0:T(8,128)(2,1)S(1)}, bf16[192,128]{1,0:T(8,128)(2,1)S(1)}, u32[]{:S(2)}, u32[]{:S(2)}) %collective-permute-start.13) | collective-permute-done | bytes 49184 | tf_op jit(solution)/shard_map/ppermute | solution.py:186
  90.4 0.8 reduce_sum.23.slot
  91.7 2.8 %collective-permute-done.15 = bf16[192,128]{1,0:T(8,128)(2,1)S(1)} collective-permute-done((bf16[192,128]{1,0:T(8,128)(2,1)S(1)}, bf16[192,128]{1,0:T(8,128)(2,1)S(1)}, u32[]{:S(2)}, u32[]{:S(2)}) %collective-permute-start.15) | collective-permute-done | bytes 49184 | tf_op jit(solution)/shard_map/ppermute | solution.py:186
  94.5 0.6 add_add_fusion.low
  95.2 0.8 copy-done.8
  96.2 3.6 %shard_map.120 = bf16[384,512]{1,0:T(8,128)(2,1)} custom-call(s32[1]{0:T(128)} %bitcast.7.half, f32[384,512]{1,0:T(8,128)} %get-tuple-element.35.own, f32[384,512]{1,0:T(8,128)} %copy-done.7, bf16[192,128]{1,0:T(8,128)(2,1)} %add_add_fusion.low, s32[384,1]{1,0:T(8,128)} %reduce_sum.23.slot, bf16[512,512]{1,0:T(8,128)(2,1)} %bitcast.60, ...), custom_call_target="tpu_custom_call" | custom-call | flops 402653184 | bytes 3014656 | tf_op jit(solution)/shard_map/pallas_call | solution.py:101
  99.8 4.5 %all-to-all-start.1 = ((bf16[16,24,512]{2,1,0:T(8,128)(2,1)}), bf16[16,24,512]{2,1,0:T(8,128)(2,1)S(1)}, u32[]{:S(2)}, u32[]{:S(2)}) async-start(bf16[16,24,512]{2,1,0:T(8,128)(2,1)} %bitcast.62), calls=%async_computation.1 | async-start | bytes 786432 | tf_op jit(solution)/shard_map/all_to_all | solution.py:303
  104.5 12.0 %all-to-all-done.1 = bf16[16,24,512]{2,1,0:T(8,128)(2,1)S(1)} async-done(((bf16[16,24,512]{2,1,0:T(8,128)(2,1)}), bf16[16,24,512]{2,1,0:T(8,128)(2,1)S(1)}, u32[]{:S(2)}, u32[]{:S(2)}) %all-to-all-start.1) | async-done | bytes 393248 | tf_op jit(solution)/shard_map/all_to_all | solution.py:303
  117.2 5.5 %fusion.18 = (f32[8,24,8]{2,1,0:T(8,128)S(1)}, f32[8,24,8,128]{3,2,1,0:T(8,128)S(1)}) fusion(bf16[8,24,128,128]{3,2,1,0:T(8,128)(2,1)} %param.19, bf16[24,8,8,128]{3,2,1,0:T(8,128)(2,1)S(1)} %reshape.57, pred[24,128]{1,0:T(8,128)(4,1)S(1)} %iota_compare_fusion.1), kind=kOutput, calls=%fused_computation.38 | convolution fusion | flops 50723328 | bytes 7480320 | tf_op jit(solution)/shard_map/rkge,krje->krgj/dot_general | solution.py:170
  123.4 4.6 %fusion.5 = bf16[24,8,8,128]{3,2,1,0:T(8,128)(2,1)S(1)} fusion(bf16[8,24,128,128]{3,2,1,0:T(8,128)(2,1)} %param.20, f32[24,8,128]{2,1,0:T(8,128)S(1)} %bitcast.65, f32[24,8,8]{2,1,0:T(8,128)S(1)} %copy.40, f32[8,24,8,128]{3,2,1,0:T(8,128)S(1)} %get-tuple-element.56, f32[8,24,8]{2,1,0:T(8,128)S(1)} %get-tuple-element.50, f32[8,24,8]{2,1,0:T(8,128)S(1)} %max.3, ...), kind=kOutput, calls=%fused_computation.4 | convolution fusion | flops 51707904 | bytes 7590912 | tf_op jit(solution)/shard_map/krgj,krje->rkge/dot_general | solution.py:179
  128.5 15.5 %all_to_all.54 = bf16[24,16,512]{2,0,1:T(8,128)(2,1)S(1)} all-to-all(bf16[24,16,512]{2,0,1:T(8,128)(2,1)S(1)} %copy.41), channel_id=1, replica_groups=mesh['rep'=2,'z'=4,'y'=2,'core'=2] {'z','y','core'}, dimensions={1} | all-to-all | bytes 786432 | tf_op jit(solution)/shard_map/all_to_all | solution.py:308
  144.1 1.6 collective-permute-done.17.other
  145.7 0.7 copy-done.6
  146.5 2.8 %shard_map.122 = bf16[384,512]{1,0:T(8,128)(2,1)} custom-call(s32[1]{0:T(128)} %bitcast.28.places, bf16[384,512]{1,0:T(8,128)(2,1)} %bitcast.56, bf16[384,512]{1,0:T(8,128)(2,1)} %copy-done.6, bf16[512,8192]{1,0:T(8,128)(2,1)} %refs_0_.5, bf16[512,8192]{1,0:T(8,128)(2,1)} %collective-permute-done.18.refs_7_.refs_8_.refs_9_.refs_10_.refs_11_.refs_12_.refs_13_.refs_1_), custom_call_target="tpu_custom_call" | custom-call | flops 402653184 | bytes 2228224 | tf_op jit(solution)/shard_map/pallas_call | solution.py:144
  149.8 0.6 stack.60.places
  150.5 7.5 %shard_map.121 = (bf16[384,512]{1,0:T(8,128)(2,1)}, bf16[384,512]{1,0:T(8,128)(2,1)}, bf16[384,512]{1,0:T(8,128)(2,1)}, bf16[384,512]{1,0:T(8,128)(2,1)}, bf16[3...) custom-call(s32[7]{0:T(128)} %stack.60.places, bf16[384,512]{1,0:T(8,128)(2,1)} %bitcast.57, ...), custom_call_target="tpu_custom_call" | custom-call | flops 2818572288 | bytes 10878976 | tf_op jit(solution)/shard_map/pallas_call | solution.py:144
  157.9 1.5 collective-permute-start.20
  159.4 1.2 collective-permute-done.21
  160.6 1.1 add_convert_fusion.3
  161.7 3.1 %collective-permute-start.22 = (bf16[384,512]{1,0:T(8,128)(2,1)S(1)}, bf16[384,512]{1,0:T(8,128)(2,1)S(1)}, u32[]{:S(2)}, u32[]{:S(2)}) collective-permute-start(bf16[384,512]{1,0:T(8,128)(2,1)S(1)} %add_convert_fusion.3), channel_id=1, source_target_pairs={{0,4},{4,8},{1,5},{5,9},{2,6},{6,10},{3,7},{7,11},{16,20},{20,24},... | collective-permute-start | bytes 1179656 | tf_op jit(solution)/shard_map/ppermute | solution.py:226
  164.8 0.9 collective-permute-start.24
  165.7 0.7 collective-permute-start.25
  166.4 1.3 collective-permute-start.19
  167.6 2.6 %collective-permute-done.20 = bf16[384,512]{1,0:T(8,128)(2,1)S(1)} collective-permute-done((bf16[384,512]{1,0:T(8,128)(2,1)}, bf16[384,512]{1,0:T(8,128)(2,1)S(1)}, u32[]{:S(2)}, u32[]{:S(2)}) %collective-permute-start.20) | collective-permute-done | bytes 393248 | tf_op jit(solution)/shard_map/ppermute | solution.py:186
  170.2 2.6 %collective-permute-done.22 = bf16[384,512]{1,0:T(8,128)(2,1)S(1)} collective-permute-done((bf16[384,512]{1,0:T(8,128)(2,1)S(1)}, bf16[384,512]{1,0:T(8,128)(2,1)S(1)}, u32[]{:S(2)}, u32[]{:S(2)}) %collective-permute-start.22) | collective-permute-done | bytes 393248 | tf_op jit(solution)/shard_map/ppermute | solution.py:226
  172.8 1.1 add_convert_fusion.2
  174.0 2.5 %collective-permute-start.23 = (bf16[384,512]{1,0:T(8,128)(2,1)S(1)}, bf16[384,512]{1,0:T(8,128)(2,1)S(1)}, u32[]{:S(2)}, u32[]{:S(2)}) collective-permute-start(bf16[384,512]{1,0:T(8,128)(2,1)S(1)} %add_convert_fusion.2), channel_id=1, source_target_pairs={{0,4},{4,8},{8,12},{12,0},{1,5},{5,9},{9,13},{13,1},{2,6},{6,10},{... | collective-permute-start | bytes 1179656 | tf_op jit(solution)/shard_map/ppermute | solution.py:186
  176.5 2.1 %collective-permute-done.24 = bf16[384,512]{1,0:T(8,128)(2,1)S(1)} collective-permute-done((bf16[384,512]{1,0:T(8,128)(2,1)}, bf16[384,512]{1,0:T(8,128)(2,1)S(1)}, u32[]{:S(2)}, u32[]{:S(2)}) %collective-permute-start.24) | collective-permute-done | bytes 393248 | tf_op jit(solution)/shard_map/ppermute | solution.py:186
  178.6 1.1 add_convert_fusion.1
  179.8 2.2 %collective-permute-start.26 = (bf16[384,512]{1,0:T(8,128)(2,1)S(1)}, bf16[384,512]{1,0:T(8,128)(2,1)S(1)}, u32[]{:S(2)}, u32[]{:S(2)}) collective-permute-start(bf16[384,512]{1,0:T(8,128)(2,1)S(1)} %add_convert_fusion.1), channel_id=1, source_target_pairs={{0,12},{4,0},{8,4},{12,8},{1,13},{5,1},{9,5},{13,9},{2,14},{6,2},{... | collective-permute-start | bytes 1179656 | tf_op jit(solution)/shard_map/ppermute | solution.py:186
  181.9 4.2 %collective-permute-done.19 = bf16[384,512]{1,0:T(8,128)(2,1)S(1)} collective-permute-done((bf16[384,512]{1,0:T(8,128)(2,1)}, bf16[384,512]{1,0:T(8,128)(2,1)S(1)}, u32[]{:S(2)}, u32[]{:S(2)}) %collective-permute-start.19) | collective-permute-done | bytes 393248 | tf_op jit(solution)/shard_map/ppermute | solution.py:186
  186.2 1.7 collective-permute-done.23
  187.9 6.1 %collective-permute-done.26 = bf16[384,512]{1,0:T(8,128)(2,1)S(1)} collective-permute-done((bf16[384,512]{1,0:T(8,128)(2,1)S(1)}, bf16[384,512]{1,0:T(8,128)(2,1)S(1)}, u32[]{:S(2)}, u32[]{:S(2)}) %collective-permute-start.26) | collective-permute-done | bytes 393248 | tf_op jit(solution)/shard_map/ppermute | solution.py:186
  194.0 1.9 add_convert_fusion
  (69 shorter events, 5.5 us)
Async XLA Ops:
  0.0 26.1 %copy-start = (bf16[1,8192,64]{1,2,0:T(8,128)(2,1)S(1)}, bf16[1,8192,64]{1,2,0:T(8,128)(2,1)}, u32[]{:S(2)}) copy-start(bf16[1,8192,64]{1,2,0:T(8,128)(2,1)} %param.18) | copy-start | bytes 3145732
  0.0 61.6 %collective-permute-start.8 = (bf16[8192,512]{1,0:T(8,128)(2,1)}, bf16[8192,512]{1,0:T(8,128)(2,1)}, u32[]{:S(2)}, u32[]{:S(2)}) collective-permute-start(bf16[8192,512]{1,0:T(8,128)(2,1)} %refs_3_.2), channel_id=1, source_target_pairs={{0,1},{1,0},{2,3},{3,2},{4,5},{5,4},{6,7},{7,6},{8,9},{9,8},{10,11... | collective-permute-start | bytes 25165832 | tf_op jit(solution)/shard_map/ppermute | solution.py:186
  0.5 143.7 %collective-permute-start.18 = (bf16[512,8192]{1,0:T(8,128)(2,1)}, bf16[512,8192]{1,0:T(8,128)(2,1)}, u32[]{:S(2)}, u32[]{:S(2)}) collective-permute-start(bf16[512,8192]{1,0:T(8,128)(2,1)} %refs_0_.5), channel_id=1, source_target_pairs={{0,1},{1,0},{2,3},{3,2},{4,5},{5,4},{6,7},{7,6},{8,9},{9,8},{10,11... | collective-permute-start | bytes 25165832 | tf_op jit(solution)/shard_map/ppermute | solution.py:186
  0.5 15.2 %collective-permute-start = (bf16[384,512]{1,0:T(8,128)(2,1)}, bf16[384,512]{1,0:T(8,128)(2,1)S(1)}, u32[]{:S(2)}, u32[]{:S(2)}) collective-permute-start(bf16[384,512]{1,0:T(8,128)(2,1)} %refs_0_.3), channel_id=1, source_target_pairs={{0,4},{4,8},{8,12},{12,0},{1,5},{5,9},{9,13},{13,1},{2,6},{6,10},{... | collective-permute-start | bytes 1179656 | tf_op jit(solution)/shard_map/ppermute | solution.py:186
  3.5 12.9 %collective-permute-start.4 = (bf16[384,512]{1,0:T(8,128)(2,1)}, bf16[384,512]{1,0:T(8,128)(2,1)S(1)}, u32[]{:S(2)}, u32[]{:S(2)}) collective-permute-start(bf16[384,512]{1,0:T(8,128)(2,1)} %refs_0_.3), channel_id=1, source_target_pairs={{0,2},{2,0},{1,3},{3,1},{4,6},{6,4},{5,7},{7,5},{8,10},{10,8},{9,1... | collective-permute-start | bytes 1179656 | tf_op jit(solution)/shard_map/ppermute | solution.py:186
  5.1 18.6 %collective-permute-start.2 = (bf16[384,512]{1,0:T(8,128)(2,1)}, bf16[384,512]{1,0:T(8,128)(2,1)}, u32[]{:S(2)}, u32[]{:S(2)}) collective-permute-start(bf16[384,512]{1,0:T(8,128)(2,1)} %refs_0_.3), channel_id=1, source_target_pairs={{0,12},{4,0},{8,4},{12,8},{1,13},{5,1},{9,5},{13,9},{2,14},{6,2},{... | collective-permute-start | bytes 1179656 | tf_op jit(solution)/shard_map/ppermute | solution.py:186
  15.7 45.9 %copy-start.9 = (bf16[384,512]{1,0:T(8,128)(2,1)}, bf16[384,512]{1,0:T(8,128)(2,1)S(1)}, u32[]{:S(2)}) copy-start(bf16[384,512]{1,0:T(8,128)(2,1)S(1)} %collective-permute-done.refs_2_) | copy-start | bytes 1179652
  15.7 9.1 %collective-permute-start.1 = (bf16[384,512]{1,0:T(8,128)(2,1)S(1)}, bf16[384,512]{1,0:T(8,128)(2,1)S(1)}, u32[]{:S(2)}, u32[]{:S(2)}) collective-permute-start(bf16[384,512]{1,0:T(8,128)(2,1)S(1)} %collective-permute-done.refs_2_), channel_id=1, source_target_pairs={{4,8},{8,12},{5,9},{9,13},{6,10},{10,14},{7,11},{11,15},{20,24},{2... | collective-permute-start | bytes 1179656 | tf_op jit(solution)/shard_map/ppermute | solution.py:204
  16.4 45.2 %copy-start.10 = (bf16[384,512]{1,0:T(8,128)(2,1)}, bf16[384,512]{1,0:T(8,128)(2,1)S(1)}, u32[]{:S(2)}) copy-start(bf16[384,512]{1,0:T(8,128)(2,1)S(1)} %collective-permute-done.4.refs_1_) | copy-start | bytes 1179652
  16.4 25.3 %collective-permute-start.5 = (bf16[384,512]{1,0:T(8,128)(2,1)S(1)}, bf16[384,512]{1,0:T(8,128)(2,1)}, u32[]{:S(2)}, u32[]{:S(2)}) collective-permute-start(bf16[384,512]{1,0:T(8,128)(2,1)S(1)} %collective-permute-done.refs_2_), channel_id=1, source_target_pairs={{0,2},{2,0},{1,3},{3,1},{4,6},{6,4},{5,7},{7,5},{8,10},{10,8},{9,1... | collective-permute-start | bytes 1179656 | tf_op jit(solution)/shard_map/ppermute | solution.py:186
  23.7 18.1 %collective-permute-start.6 = (bf16[384,512]{1,0:T(8,128)(2,1)}, bf16[384,512]{1,0:T(8,128)(2,1)}, u32[]{:S(2)}, u32[]{:S(2)}) collective-permute-start(bf16[384,512]{1,0:T(8,128)(2,1)} %collective-permute-done.2.refs_4_), channel_id=1, source_target_pairs={{0,2},{2,0},{1,3},{3,1},{4,6},{6,4},{5,7},{7,5},{8,10},{10,8},{9,1... | collective-permute-start | bytes 1179656 | tf_op jit(solution)/shard_map/ppermute | solution.py:186
  24.8 15.0 %copy-start.12 = (bf16[384,512]{1,0:T(8,128)(2,1)}, bf16[384,512]{1,0:T(8,128)(2,1)S(1)}, u32[]{:S(2)}) copy-start(bf16[384,512]{1,0:T(8,128)(2,1)S(1)} %collective-permute-done.1) | copy-start | bytes 1179652
  24.8 15.0 %collective-permute-start.3 = (bf16[384,512]{1,0:T(8,128)(2,1)}, bf16[384,512]{1,0:T(8,128)(2,1)S(1)}, u32[]{:S(2)}, u32[]{:S(2)}) collective-permute-start(bf16[384,512]{1,0:T(8,128)(2,1)} %collective-permute-done.2.refs_4_), channel_id=1, source_target_pairs={{8,4},{4,0},{9,5},{5,1},{10,6},{6,2},{11,7},{7,3},{24,20},{20,16},... | collective-permute-start | bytes 1179656 | tf_op jit(solution)/shard_map/ppermute | solution.py:205
  39.9 0.8 copy-start.13
  40.6 20.9 %collective-permute-start.9 = (bf16[1,64,8192]{2,1,0:T(8,128)(2,1)}, bf16[1,64,8192]{2,1,0:T(8,128)(2,1)S(1)}, u32[]{:S(2)}, u32[]{:S(2)}) collective-permute-start(bf16[1,64,8192]{2,1,0:T(8,128)(2,1)} %bitcast.46), channel_id=1, source_target_pairs={{0,1},{1,0},{2,3},{3,2},{4,5},{5,4},{6,7},{7,6},{8,9},{9,8},{10,11... | collective-permute-start | bytes 3145736 | tf_op jit(solution)/shard_map/ppermute | solution.py:186
  41.7 29.4 %copy-start.5 = (bf16[384,512]{1,0:T(8,128)(2,1)}, bf16[384,512]{1,0:T(8,128)(2,1)S(1)}, u32[]{:S(2)}) copy-start(bf16[384,512]{1,0:T(8,128)(2,1)S(1)} %broadcast_select_fusion.refs_0_) | copy-start | bytes 1179652
  42.6 19.0 %all-to-all-start = ((bf16[32,16,512]{2,0,1:T(8,128)(2,1)}), bf16[32,16,512]{2,0,1:T(8,128)(2,1)S(1)}, u32[]{:S(2)}, u32[]{:S(2)}) async-start(bf16[32,16,512]{2,0,1:T(8,128)(2,1)} %bitcast.45), calls=%async_computation | async-start | bytes 1048576 | tf_op jit(solution)/shard_map/all_to_all | solution.py:274
  47.1 24.0 %collective-permute-start.7 = (bf16[384,512]{1,0:T(8,128)(2,1)S(1)}, bf16[384,512]{1,0:T(8,128)(2,1)S(1)}, u32[]{:S(2)}, u32[]{:S(2)}) collective-permute-start(bf16[384,512]{1,0:T(8,128)(2,1)S(1)} %broadcast_select_fusion.refs_0_), channel_id=1, source_target_pairs={{0,2},{2,0},{1,3},{3,1},{4,6},{6,4},{5,7},{7,5},{8,10},{10,8},{9,1... | collective-permute-start | bytes 1179656 | tf_op jit(solution)/shard_map/ppermute | solution.py:186
  61.6 19.5 %copy-start.4 = (bf16[32,16,512]{2,0,1:T(8,128)(2,1)}, bf16[32,16,512]{2,0,1:T(8,128)(2,1)S(1)}, u32[]{:S(2)}) copy-start(bf16[32,16,512]{2,0,1:T(8,128)(2,1)S(1)} %all-to-all-done) | copy-start | bytes 1572868
  61.6 1.0 copy-start.2
  71.2 0.8 copy-start.11
  71.9 32.4 %copy-start.14 = (bf16[24,1024]{1,0:T(8,128)(2,1)S(1)}, bf16[24,1024]{1,0:T(8,128)(2,1)}, u32[]{:S(2)}) copy-start(bf16[24,1024]{1,0:T(8,128)(2,1)} %param.21) | copy-start | bytes 147460
  71.9 32.4 %copy-start.15 = (bf16[24,1024]{1,0:T(8,128)(2,1)S(1)}, bf16[24,1024]{1,0:T(8,128)(2,1)}, u32[]{:S(2)}) copy-start(bf16[24,1024]{1,0:T(8,128)(2,1)} %param.22) | copy-start | bytes 147460
  77.3 27.1 %copy-start.16 = (s32[24]{0:T(128)S(1)}, s32[24]{0:T(128)}, u32[]{:S(2)}) copy-start(s32[24]{0:T(128)} %param.15) | copy-start | bytes 292
  77.3 1.7 collective-permute-start.11
  77.3 17.8 %collective-permute-start.10 = (f32[384,512]{1,0:T(8,128)}, f32[384,512]{1,0:T(8,128)S(1)}, u32[]{:S(2)}, u32[]{:S(2)}) collective-permute-start(f32[384,512]{1,0:T(8,128)} %get-tuple-element.36), channel_id=1, source_target_pairs={{0,1},{1,0},{2,3},{3,2},{4,5},{5,4},{6,7},{7,6},{8,9},{9,8},{10,11... | collective-permute-start | bytes 2359304 | tf_op jit(solution)/shard_map/ppermute | solution.py:186
  80.2 4.2 %collective-permute-start.12 = (bf16[192,128]{1,0:T(8,128)(2,1)S(1)}, bf16[192,128]{1,0:T(8,128)(2,1)S(1)}, u32[]{:S(2)}, u32[]{:S(2)}) collective-permute-start(bf16[192,128]{1,0:T(8,128)(2,1)S(1)} %pad_maximum_fusion), channel_id=1, source_target_pairs={{0,2},{2,0},{1,3},{3,1},{4,6},{6,4},{5,7},{7,5},{8,10},{10,8},{9,1... | collective-permute-start | bytes 147464 | tf_op jit(solution)/shard_map/ppermute | solution.py:186
  81.1 14.1 %collective-permute-start.16 = (bf16[512,512]{1,0:T(8,128)(2,1)S(1)}, bf16[512,512]{1,0:T(8,128)(2,1)S(1)}, u32[]{:S(2)}, u32[]{:S(2)}) collective-permute-start(bf16[512,512]{1,0:T(8,128)(2,1)S(1)} %bitcast.59), channel_id=1, source_target_pairs={{0,16},{16,0},{1,17},{17,1},{2,18},{18,2},{3,19},{19,3},{4,20},{20... | collective-permute-start | bytes 1572872 | tf_op jit(solution)/shard_map/ppermute | solution.py:275
  84.5 5.9 %collective-permute-start.13 = (bf16[192,128]{1,0:T(8,128)(2,1)S(1)}, bf16[192,128]{1,0:T(8,128)(2,1)S(1)}, u32[]{:S(2)}, u32[]{:S(2)}) collective-permute-start(bf16[192,128]{1,0:T(8,128)(2,1)S(1)} %fusion.20), channel_id=1, source_target_pairs={{0,4},{4,8},{8,12},{12,0},{1,5},{5,9},{9,13},{13,1},{2,6},{6,10},{... | collective-permute-start | bytes 147464 | tf_op jit(solution)/shard_map/ppermute | solution.py:186
  86.0 5.7 %collective-permute-start.14 = (bf16[192,128]{1,0:T(8,128)(2,1)S(1)}, bf16[192,128]{1,0:T(8,128)(2,1)S(1)}, u32[]{:S(2)}, u32[]{:S(2)}) collective-permute-start(bf16[192,128]{1,0:T(8,128)(2,1)S(1)} %fusion.20), channel_id=1, source_target_pairs={{0,8},{4,12},{8,0},{12,4},{1,9},{5,13},{9,1},{13,5},{2,10},{6,14},... | collective-permute-start | bytes 147464 | tf_op jit(solution)/shard_map/ppermute | solution.py:186
  90.4 4.1 %collective-permute-start.15 = (bf16[192,128]{1,0:T(8,128)(2,1)S(1)}, bf16[192,128]{1,0:T(8,128)(2,1)S(1)}, u32[]{:S(2)}, u32[]{:S(2)}) collective-permute-start(bf16[192,128]{1,0:T(8,128)(2,1)S(1)} %fusion.20), channel_id=1, source_target_pairs={{0,12},{4,0},{8,4},{12,8},{1,13},{5,1},{9,5},{13,9},{2,14},{6,2},{... | collective-permute-start | bytes 147464 | tf_op jit(solution)/shard_map/ppermute | solution.py:186
  95.1 0.8 copy-start.8
  95.2 1.1 copy-start.7
  99.8 16.7 %all-to-all-start.1 = ((bf16[16,24,512]{2,1,0:T(8,128)(2,1)}), bf16[16,24,512]{2,1,0:T(8,128)(2,1)S(1)}, u32[]{:S(2)}, u32[]{:S(2)}) async-start(bf16[16,24,512]{2,1,0:T(8,128)(2,1)} %bitcast.62), calls=%async_computation.1 | async-start | bytes 786432 | tf_op jit(solution)/shard_map/all_to_all | solution.py:303
  144.0 1.7 copy-start.3
  144.0 1.7 collective-permute-start.17
  145.7 0.7 copy-start.6
  149.2 11.4 %collective-permute-start.21 = (bf16[384,512]{1,0:T(8,128)(2,1)}, bf16[384,512]{1,0:T(8,128)(2,1)S(1)}, u32[]{:S(2)}, u32[]{:S(2)}) collective-permute-start(bf16[384,512]{1,0:T(8,128)(2,1)} %shard_map.122), channel_id=1, source_target_pairs={{0,2},{2,0},{1,3},{3,1},{4,6},{6,4},{5,7},{7,5},{8,10},{10,8},{9,1... | collective-permute-start | bytes 1179656 | tf_op jit(solution)/shard_map/ppermute | solution.py:186
  150.5 45.5 %copy-start.1 = (bf16[1,8192,64]{1,2,0:T(8,128)(2,1)S(1)}, bf16[1,8192,64]{1,2,0:T(8,128)(2,1)}, u32[]{:S(2)}) copy-start(bf16[1,8192,64]{1,2,0:T(8,128)(2,1)} %param.18) | copy-start | bytes 3145732
  157.9 12.2 %collective-permute-start.20 = (bf16[384,512]{1,0:T(8,128)(2,1)}, bf16[384,512]{1,0:T(8,128)(2,1)S(1)}, u32[]{:S(2)}, u32[]{:S(2)}) collective-permute-start(bf16[384,512]{1,0:T(8,128)(2,1)} %get-tuple-element.43), channel_id=1, source_target_pairs={{0,2},{2,0},{1,3},{3,1},{4,6},{6,4},{5,7},{7,5},{8,10},{10,8},{9,1... | collective-permute-start | bytes 1179656 | tf_op jit(solution)/shard_map/ppermute | solution.py:186
  161.7 11.1 %collective-permute-start.22 = (bf16[384,512]{1,0:T(8,128)(2,1)S(1)}, bf16[384,512]{1,0:T(8,128)(2,1)S(1)}, u32[]{:S(2)}, u32[]{:S(2)}) collective-permute-start(bf16[384,512]{1,0:T(8,128)(2,1)S(1)} %add_convert_fusion.3), channel_id=1, source_target_pairs={{0,4},{4,8},{1,5},{5,9},{2,6},{6,10},{3,7},{7,11},{16,20},{20,24},... | collective-permute-start | bytes 1179656 | tf_op jit(solution)/shard_map/ppermute | solution.py:226
  164.8 13.8 %collective-permute-start.24 = (bf16[384,512]{1,0:T(8,128)(2,1)}, bf16[384,512]{1,0:T(8,128)(2,1)S(1)}, u32[]{:S(2)}, u32[]{:S(2)}) collective-permute-start(bf16[384,512]{1,0:T(8,128)(2,1)} %get-tuple-element.48), channel_id=1, source_target_pairs={{0,2},{2,0},{1,3},{3,1},{4,6},{6,4},{5,7},{7,5},{8,10},{10,8},{9,1... | collective-permute-start | bytes 1179656 | tf_op jit(solution)/shard_map/ppermute | solution.py:186
  165.7 12.9 %collective-permute-start.25 = (bf16[384,512]{1,0:T(8,128)(2,1)S(1)}, bf16[384,512]{1,0:T(8,128)(2,1)S(1)}, u32[]{:S(2)}, u32[]{:S(2)}) collective-permute-start(bf16[384,512]{1,0:T(8,128)(2,1)S(1)} %add_convert_fusion.3), channel_id=1, source_target_pairs={{12,8},{8,4},{13,9},{9,5},{14,10},{10,6},{15,11},{11,7},{28,24},{2... | collective-permute-start | bytes 1179656 | tf_op jit(solution)/shard_map/ppermute | solution.py:227
  166.4 19.8 %collective-permute-start.19 = (bf16[384,512]{1,0:T(8,128)(2,1)}, bf16[384,512]{1,0:T(8,128)(2,1)S(1)}, u32[]{:S(2)}, u32[]{:S(2)}) collective-permute-start(bf16[384,512]{1,0:T(8,128)(2,1)} %get-tuple-element.40), channel_id=1, source_target_pairs={{0,2},{2,0},{1,3},{3,1},{4,6},{6,4},{5,7},{7,5},{8,10},{10,8},{9,1... | collective-permute-start | bytes 1179656 | tf_op jit(solution)/shard_map/ppermute | solution.py:186
  174.0 13.9 %collective-permute-start.23 = (bf16[384,512]{1,0:T(8,128)(2,1)S(1)}, bf16[384,512]{1,0:T(8,128)(2,1)S(1)}, u32[]{:S(2)}, u32[]{:S(2)}) collective-permute-start(bf16[384,512]{1,0:T(8,128)(2,1)S(1)} %add_convert_fusion.2), channel_id=1, source_target_pairs={{0,4},{4,8},{8,12},{12,0},{1,5},{5,9},{9,13},{13,1},{2,6},{6,10},{... | collective-permute-start | bytes 1179656 | tf_op jit(solution)/shard_map/ppermute | solution.py:186
  179.8 14.3 %collective-permute-start.26 = (bf16[384,512]{1,0:T(8,128)(2,1)S(1)}, bf16[384,512]{1,0:T(8,128)(2,1)S(1)}, u32[]{:S(2)}, u32[]{:S(2)}) collective-permute-start(bf16[384,512]{1,0:T(8,128)(2,1)S(1)} %add_convert_fusion.1), channel_id=1, source_target_pairs={{0,12},{4,0},{8,4},{12,8},{1,13},{5,1},{9,5},{13,9},{2,14},{6,2},{... | collective-permute-start | bytes 1179656 | tf_op jit(solution)/shard_map/ppermute | solution.py:186

commit v3 on v2

--- a/solution.py
+++ b/solution.py
@@ -249,6 +249,7 @@
     rows, width = tokens.shape
     total_adapters = adapter_storage_slot.shape[0]
     rank = adapter_down_maps.shape[2]
+    depth = output_weight.shape[0]
     chips_of = lambda layer: [
         (layer % layers) * sides + (y + side) % sides for side in range(sides)
     ]
@@ -266,24 +267,24 @@
 
     entries = gather_features(tokens)
 
-    reps = lax.axis_size("rep")
-    half = lax.axis_index("rep") % 2
-    up = jnp.swapaxes(adapter_up_maps, 1, 2)[0]
-    up = lax.dynamic_slice_in_dim(up, half * (rank // 2), rank // 2, 0)
-    up = after(up, entries[-1][1][0])
-    up = lax.all_to_all(up, ADP, split_axis=1, concat_axis=0, tiled=True)
-    up_other = lax.ppermute(up, "rep", [(i, i ^ 1) for i in range(reps)])
-
     sums = []
     for group in (entries[:-1], entries[-1:]):
         chips = [chip for layer, _ in group for chip in chips_of(layer)]
         places = jnp.stack([2 * chip + core for chip in chips]).astype(jnp.int32)
         blocks = [block for _, pair in group for block in pair]
-        if sums:
-            places = after(places, up)
         sums = project(
             places, blocks, query_weight, query_weight_other, down, down_other, sums
         )
+        first_sums = sums if len(group) > 1 else first_sums
+
+    reps = lax.axis_size("rep")
+    half = lax.axis_index("rep") % 2
+    up = jnp.swapaxes(adapter_up_maps, 1, 2)[0]
+    up = lax.dynamic_slice_in_dim(up, half * (rank // 2), rank // 2, 0)
+    up = after(up, first_sums[2])
+    up = lax.all_to_all(up, ADP, split_axis=1, concat_axis=0, tiled=True)
+    up_other = lax.ppermute(up, "rep", [(i, i ^ 1) for i in range(reps)])
+
     own, sent, low = sums
     low_other = shift(low, "core", 1)
     received = shift(sent, "core", 1)
@@ -305,7 +306,9 @@
     context = attention(
         query_local, cache_length, key_cache, value_cache, new_token_key, new_token_value
     )
-    context = lax.all_to_all(context, ADP, split_axis=1, concat_axis=0, tiled=True)
+    context = jnp.swapaxes(context.reshape(context.shape[0], -1, depth), 0, 1)
+    context = lax.all_to_all(context, ADP, split_axis=0, concat_axis=0, tiled=True)
+    context = context.reshape(rows, depth)
     context_other = shift(context, "core", 1)
 
     order = [2, 1, 3, 0] if layers == 4 else list(range(1, layers)) + [0]

time: 197 us -> 197 us (level)
  starting transfers between devices: 41.2 us -> 46.5 us
  waiting for transfers between devices: 81.4 us -> 77.5 us
    all_to_all x1, waiting for transfers between devices: 9.9 us -> 3.55 us  [shards(): up = lax.all_to_all(up, ADP, split_axis=1, concat_axis=0, tiled=True)]
    ppermute x22, waiting for transfers between devices: 43.1 us -> 48.9 us  [shift(): lax.ppermute(value, axis, [(i, (i + by) % size) for i in range(size)])]
    ppermute x1, waiting for transfers between devices: 13.7 us -> 8.77 us  [gather_features(): from_above = lax.ppermute(above, 'z', [(2, 1), (1, 0)])]
    all_to_all x1, starting transfers between devices: 4.46 us -> 8.96 us  [shards(): up = lax.all_to_all(up, ADP, split_axis=1, concat_axis=0, tiled=True)]
    unnamed x36 -> x34, local copies, waits for them, and re-layouts: 4.42 us -> 3.36 us
  transfers between devices with their start and end apart: 29 -> 29, of which waited for: 18 -> 19; matrix products, arithmetic and copies ran while one was open for 12% -> 12% of each run, Pallas kernels for 13% -> 13%
where the time goes in v3:
time: 197 us; the launch traced here: 196 us
  waiting for transfers between devices  77.5 us (39%)
  starting transfers between devices  46.5 us (24%)
  Pallas kernels  27.7 us (14%)
  blocking collectives  15.5 us (8%)
  other arithmetic  11.1 us (6%)
  matrix products  10.4 us (5%)
  local copies, waits for them, and re-layouts  7.24 us (4%)
    ppermute x22, waiting for transfers between devices, shift(): lax.ppermute(value, axis, [(i, (i + by) % size) for i in range(size)])  48.9 us
    ppermute x22, starting transfers between devices, shift(): lax.ppermute(value, axis, [(i, (i + by) % size) for i in range(size)])  25.8 us
    all_to_all x1, blocking collectives, shards(): lax.all_to_all(context, ADP, split_axis=0, concat_axis=0, tiled=True)  15.5 us
    pallas_call x2, Pallas kernels, project(): pl.pallas_call(project_kernel, grid_spec=pltpu.PrefetchScalarGridSpec(num...  13.9 us
    all_to_all x1, waiting for transfers between devices, shards(): lax.all_to_all(query, ADP, split_axis=0, concat_axis=1, tiled=True)  12 us
    pallas_call x2, Pallas kernels, output_partial(): pl.pallas_call(output_kernel, grid_spec=pltpu.PrefetchScalarGridSpec(num_...  10.2 us
    all_to_all x1, starting transfers between devices, shards(): up = lax.all_to_all(up, ADP, split_axis=1, concat_axis=0, tiled=True)  8.96 us
    ppermute x1, waiting for transfers between devices, gather_features(): from_above = lax.ppermute(above, 'z', [(2, 1), (1, 0)])  8.77 us
  transfers between devices with their start and end apart: 29, of which 19 were waited for; matrix products, arithmetic and copies ran while one was open for 12% of the time, Pallas kernels for 13%

profile of v3, /device:TPU:0, one launch (start us, length us, event | category | flops | bytes accessed | tf_op | source)
XLA Modules:
  0.0 196.4 jit_solution(4149217276695552149)
XLA Ops:
  0.5 3.0 %collective-permute-start = (bf16[384,512]{1,0:T(8,128)(2,1)}, bf16[384,512]{1,0:T(8,128)(2,1)S(1)}, u32[]{:S(2)}, u32[]{:S(2)}) collective-permute-start(bf16[384,512]{1,0:T(8,128)(2,1)} %refs_0_.3), channel_id=1, source_target_pairs={{0,4},{4,8},{8,12},{12,0},{1,5},{5,9},{9,13},{13,1},{2,6},{6,10},{... | collective-permute-start | bytes 1179656 | tf_op jit(solution)/shard_map/ppermute | solution.py:186
  3.5 2.0 %collective-permute-start.2 = (bf16[384,512]{1,0:T(8,128)(2,1)}, bf16[384,512]{1,0:T(8,128)(2,1)S(1)}, u32[]{:S(2)}, u32[]{:S(2)}) collective-permute-start(bf16[384,512]{1,0:T(8,128)(2,1)} %refs_0_.3), channel_id=1, source_target_pairs={{0,12},{4,0},{8,4},{12,8},{1,13},{5,1},{9,5},{13,9},{2,14},{6,2},{... | collective-permute-start | bytes 1179656 | tf_op jit(solution)/shard_map/ppermute | solution.py:186
  5.6 1.7 collective-permute-start.4
  7.3 8.4 %collective-permute-done.refs_2_ = bf16[384,512]{1,0:T(8,128)(2,1)S(1)} collective-permute-done((bf16[384,512]{1,0:T(8,128)(2,1)}, bf16[384,512]{1,0:T(8,128)(2,1)S(1)}, u32[]{:S(2)}, u32[]{:S(2)}) %collective-permute-start) | collective-permute-done | bytes 393248 | tf_op jit(solution)/shard_map/ppermute | solution.py:186
  15.7 0.7 collective-permute-start.1
  16.4 6.6 %collective-permute-done.2.refs_4_ = bf16[384,512]{1,0:T(8,128)(2,1)S(1)} collective-permute-done((bf16[384,512]{1,0:T(8,128)(2,1)}, bf16[384,512]{1,0:T(8,128)(2,1)S(1)}, u32[]{:S(2)}, u32[]{:S(2)}) %collective-permute-start.2) | collective-permute-done | bytes 393248 | tf_op jit(solution)/shard_map/ppermute | solution.py:186
  23.0 1.3 collective-permute-start.3
  24.3 0.7 copy-done.11
  25.1 1.6 collective-permute-start.5
  26.7 8.8 %collective-permute-done.3 = bf16[384,512]{1,0:T(8,128)(2,1)} collective-permute-done((bf16[384,512]{1,0:T(8,128)(2,1)S(1)}, bf16[384,512]{1,0:T(8,128)(2,1)}, u32[]{:S(2)}, u32[]{:S(2)}) %collective-permute-start.3) | collective-permute-done | bytes 393248 | tf_op jit(solution)/shard_map/ppermute | solution.py:205
  35.4 1.5 collective-permute-start.6
  37.0 0.7 reduce
  37.7 1.0 broadcast_select_fusion.refs_0_
  38.8 6.3 %collective-permute-done.6.refs_5_ = bf16[384,512]{1,0:T(8,128)(2,1)} collective-permute-done((bf16[384,512]{1,0:T(8,128)(2,1)S(1)}, bf16[384,512]{1,0:T(8,128)(2,1)}, u32[]{:S(2)}, u32[]{:S(2)}) %collective-permute-start.6) | collective-permute-done | bytes 393248 | tf_op jit(solution)/shard_map/ppermute | solution.py:186
  45.1 1.5 collective-permute-start.7
  46.6 0.7 select_reduce_fusion
  47.5 0.7 stack.68.places
  48.2 1.0 copy-done.2
  49.1 8.5 %shard_map.118 = (f32[384,512]{1,0:T(8,128)}, f32[384,512]{1,0:T(8,128)}, f32[384,128]{1,0:T(8,128)}) custom-call(s32[6]{0:T(128)} %stack.68.places, bf16[384,512]{1,0:T(8,128)(2,1)} %refs_0_.3, bf16[384,512]{1,0:T(8,128)(2,1)} %copy-done.11, bf16[384,512]{1,0:T(8,128)(2,1)} %copy-done.9, bf16[384,512]{1,0:T(8,128)(2,1)} %collective-permute-done.5.refs_3_, ...), custom_call_target="tpu_custom_call" | custom-call | flops 2717908992 | bytes 10223616 | tf_op jit(solution)/shard_map/pallas_call | solution.py:46
  57.7 0.9 copy.65
  58.5 9.0 %all-to-all-start = ((bf16[32,16,512]{2,0,1:T(8,128)(2,1)}), bf16[32,16,512]{2,0,1:T(8,128)(2,1)S(1)}, u32[]{:S(2)}, u32[]{:S(2)}) async-start(bf16[32,16,512]{2,0,1:T(8,128)(2,1)} %bitcast.45), calls=%async_computation | async-start | bytes 1048576 | tf_op jit(solution)/shard_map/all_to_all | solution.py:285
  68.2 5.3 %shard_map.119 = (f32[384,512]{1,0:T(8,128)}, f32[384,512]{1,0:T(8,128)}, f32[384,128]{1,0:T(8,128)}) custom-call(s32[2]{0:T(128)} %pad_add_fusion.places, bf16[384,512]{1,0:T(8,128)(2,1)} %copy-done.5, bf16[384,512]{1,0:T(8,128)(2,1)} %collective-permute-done.7.refs_1_, bf16[8192,512]{1,0:T(8,128)(2,1)} %refs_3_.2, bf16[8192,512]{1,0:T(8,128)(2,1)} %refs_3_.2, ...), custom_call_target="tpu_custom_call" | custom-call | flops 905969664 | bytes 4456448 | tf_op jit(solution)/shard_map/pallas_call | solution.py:46
  74.0 1.2 collective-permute-done.11
  75.2 0.9 add.271
  76.5 2.0 collective-permute-start.12
  78.4 3.5 %all-to-all-done = bf16[32,16,512]{2,0,1:T(8,128)(2,1)S(1)} async-done(((bf16[32,16,512]{2,0,1:T(8,128)(2,1)}), bf16[32,16,512]{2,0,1:T(8,128)(2,1)S(1)}, u32[]{:S(2)}, u32[]{:S(2)}) %all-to-all-start) | async-done | bytes 524320 | tf_op jit(solution)/shard_map/all_to_all | solution.py:285
  82.0 1.5 collective-permute-start.16
  83.6 1.2 collective-permute-start.13
  84.7 1.2 collective-permute-start.14
  86.0 3.6 %collective-permute-done.13 = bf16[192,128]{1,0:T(8,128)(2,1)S(1)} collective-permute-done((bf16[192,128]{1,0:T(8,128)(2,1)S(1)}, bf16[192,128]{1,0:T(8,128)(2,1)S(1)}, u32[]{:S(2)}, u32[]{:S(2)}) %collective-permute-start.13) | collective-permute-done | bytes 49184 | tf_op jit(solution)/shard_map/ppermute | solution.py:186
  89.5 0.8 reduce_sum.23.slot
  90.4 3.2 %collective-permute-done.15 = bf16[192,128]{1,0:T(8,128)(2,1)S(1)} collective-permute-done((bf16[192,128]{1,0:T(8,128)(2,1)S(1)}, bf16[192,128]{1,0:T(8,128)(2,1)S(1)}, u32[]{:S(2)}, u32[]{:S(2)}) %collective-permute-start.15) | collective-permute-done | bytes 49184 | tf_op jit(solution)/shard_map/ppermute | solution.py:186
  93.6 0.6 add_add_fusion.low
  94.3 1.6 collective-permute-done.16.up_other
  95.8 0.8 copy-done.8
  96.7 3.6 %shard_map.120 = bf16[384,512]{1,0:T(8,128)(2,1)} custom-call(s32[1]{0:T(128)} %bitcast.7.half, f32[384,512]{1,0:T(8,128)} %get-tuple-element.32.own, f32[384,512]{1,0:T(8,128)} %copy-done.7, bf16[192,128]{1,0:T(8,128)(2,1)} %add_add_fusion.low, s32[384,1]{1,0:T(8,128)} %reduce_sum.23.slot, bf16[512,512]{1,0:T(8,128)(2,1)} %bitcast.61, ...), custom_call_target="tpu_custom_call" | custom-call | flops 402653184 | bytes 3014656 | tf_op jit(solution)/shard_map/pallas_call | solution.py:101
  100.2 4.5 %all-to-all-start.1 = ((bf16[16,24,512]{2,1,0:T(8,128)(2,1)}), bf16[16,24,512]{2,1,0:T(8,128)(2,1)S(1)}, u32[]{:S(2)}, u32[]{:S(2)}) async-start(bf16[16,24,512]{2,1,0:T(8,128)(2,1)} %bitcast.64), calls=%async_computation.1 | async-start | bytes 786432 | tf_op jit(solution)/shard_map/all_to_all | solution.py:304
  104.9 12.0 %all-to-all-done.1 = bf16[16,24,512]{2,1,0:T(8,128)(2,1)S(1)} async-done(((bf16[16,24,512]{2,1,0:T(8,128)(2,1)}), bf16[16,24,512]{2,1,0:T(8,128)(2,1)S(1)}, u32[]{:S(2)}, u32[]{:S(2)}) %all-to-all-start.1) | async-done | bytes 393248 | tf_op jit(solution)/shard_map/all_to_all | solution.py:304
  117.7 5.5 %fusion.18 = (f32[8,24,8]{2,1,0:T(8,128)S(1)}, f32[8,24,8,128]{3,2,1,0:T(8,128)S(1)}) fusion(bf16[8,24,128,128]{3,2,1,0:T(8,128)(2,1)} %param.19, bf16[24,8,8,128]{3,2,1,0:T(8,128)(2,1)S(1)} %reshape.55, pred[24,128]{1,0:T(8,128)(4,1)S(1)} %iota_compare_fusion.1), kind=kOutput, calls=%fused_computation.39 | convolution fusion | flops 50723328 | bytes 7480320 | tf_op jit(solution)/shard_map/rkge,krje->krgj/dot_general | solution.py:170
  123.9 4.6 %fusion.5 = bf16[24,8,8,128]{3,2,1,0:T(8,128)(2,1)S(1)} fusion(bf16[8,24,128,128]{3,2,1,0:T(8,128)(2,1)} %param.20, f32[24,8,128]{2,1,0:T(8,128)S(1)} %bitcast.67, f32[24,8,8]{2,1,0:T(8,128)S(1)} %copy.40, f32[8,24,8,128]{3,2,1,0:T(8,128)S(1)} %get-tuple-element.54, f32[8,24,8]{2,1,0:T(8,128)S(1)} %get-tuple-element.48, f32[8,24,8]{2,1,0:T(8,128)S(1)} %max.3, ...), kind=kOutput, calls=%fused_computation.4 | convolution fusion | flops 51707904 | bytes 7590912 | tf_op jit(solution)/shard_map/krgj,krje->rkge/dot_general | solution.py:179
  128.9 15.5 %all_to_all.40 = bf16[16,24,512]{2,1,0:T(8,128)(2,1)S(1)} all-to-all(bf16[16,24,512]{2,1,0:T(8,128)(2,1)S(1)} %bitcast.63), channel_id=1, replica_groups=mesh['rep'=2,'z'=4,'y'=2,'core'=2] {'z','y','core'}, dimensions={0} | all-to-all | bytes 786432 | tf_op jit(solution)/shard_map/all_to_all | solution.py:310
  144.6 1.6 collective-permute-done.17.other
  146.2 0.7 copy-done.6
  146.9 2.8 %shard_map.122 = bf16[384,512]{1,0:T(8,128)(2,1)} custom-call(s32[1]{0:T(128)} %bitcast.27.places, bf16[384,512]{1,0:T(8,128)(2,1)} %bitcast.57, bf16[384,512]{1,0:T(8,128)(2,1)} %copy-done.6, bf16[512,8192]{1,0:T(8,128)(2,1)} %refs_0_.5, bf16[512,8192]{1,0:T(8,128)(2,1)} %collective-permute-done.18.refs_7_.refs_8_.refs_9_.refs_10_.refs_11_.refs_12_.refs_13_.refs_1_), custom_call_target="tpu_custom_call" | custom-call | flops 402653184 | bytes 2228224 | tf_op jit(solution)/shard_map/pallas_call | solution.py:144
  150.3 0.7 stack.60.places
  151.0 7.5 %shard_map.121 = (bf16[384,512]{1,0:T(8,128)(2,1)}, bf16[384,512]{1,0:T(8,128)(2,1)}, bf16[384,512]{1,0:T(8,128)(2,1)}, bf16[384,512]{1,0:T(8,128)(2,1)}, bf16[3...) custom-call(s32[7]{0:T(128)} %stack.60.places, bf16[384,512]{1,0:T(8,128)(2,1)} %bitcast.58, ...), custom_call_target="tpu_custom_call" | custom-call | flops 2818572288 | bytes 10878976 | tf_op jit(solution)/shard_map/pallas_call | solution.py:144
  158.4 1.5 collective-permute-start.20
  159.9 1.1 collective-permute-done.21
  161.1 1.1 add_convert_fusion.3
  162.1 3.1 %collective-permute-start.22 = (bf16[384,512]{1,0:T(8,128)(2,1)S(1)}, bf16[384,512]{1,0:T(8,128)(2,1)S(1)}, u32[]{:S(2)}, u32[]{:S(2)}) collective-permute-start(bf16[384,512]{1,0:T(8,128)(2,1)S(1)} %add_convert_fusion.3), channel_id=1, source_target_pairs={{0,4},{4,8},{1,5},{5,9},{2,6},{6,10},{3,7},{7,11},{16,20},{20,24},... | collective-permute-start | bytes 1179656 | tf_op jit(solution)/shard_map/ppermute | solution.py:226
  165.2 0.9 collective-permute-start.24
  166.1 0.7 collective-permute-start.25
  166.8 1.3 collective-permute-start.19
  168.1 2.6 %collective-permute-done.20 = bf16[384,512]{1,0:T(8,128)(2,1)S(1)} collective-permute-done((bf16[384,512]{1,0:T(8,128)(2,1)}, bf16[384,512]{1,0:T(8,128)(2,1)S(1)}, u32[]{:S(2)}, u32[]{:S(2)}) %collective-permute-start.20) | collective-permute-done | bytes 393248 | tf_op jit(solution)/shard_map/ppermute | solution.py:186
  170.7 2.6 %collective-permute-done.22 = bf16[384,512]{1,0:T(8,128)(2,1)S(1)} collective-permute-done((bf16[384,512]{1,0:T(8,128)(2,1)S(1)}, bf16[384,512]{1,0:T(8,128)(2,1)S(1)}, u32[]{:S(2)}, u32[]{:S(2)}) %collective-permute-start.22) | collective-permute-done | bytes 393248 | tf_op jit(solution)/shard_map/ppermute | solution.py:226
  173.3 1.1 add_convert_fusion.2
  174.4 2.5 %collective-permute-start.23 = (bf16[384,512]{1,0:T(8,128)(2,1)S(1)}, bf16[384,512]{1,0:T(8,128)(2,1)S(1)}, u32[]{:S(2)}, u32[]{:S(2)}) collective-permute-start(bf16[384,512]{1,0:T(8,128)(2,1)S(1)} %add_convert_fusion.2), channel_id=1, source_target_pairs={{0,4},{4,8},{8,12},{12,0},{1,5},{5,9},{9,13},{13,1},{2,6},{6,10},{... | collective-permute-start | bytes 1179656 | tf_op jit(solution)/shard_map/ppermute | solution.py:186
  177.0 2.1 %collective-permute-done.24 = bf16[384,512]{1,0:T(8,128)(2,1)S(1)} collective-permute-done((bf16[384,512]{1,0:T(8,128)(2,1)}, bf16[384,512]{1,0:T(8,128)(2,1)S(1)}, u32[]{:S(2)}, u32[]{:S(2)}) %collective-permute-start.24) | collective-permute-done | bytes 393248 | tf_op jit(solution)/shard_map/ppermute | solution.py:186
  179.1 1.1 add_convert_fusion.1
  180.3 2.2 %collective-permute-start.26 = (bf16[384,512]{1,0:T(8,128)(2,1)S(1)}, bf16[384,512]{1,0:T(8,128)(2,1)S(1)}, u32[]{:S(2)}, u32[]{:S(2)}) collective-permute-start(bf16[384,512]{1,0:T(8,128)(2,1)S(1)} %add_convert_fusion.1), channel_id=1, source_target_pairs={{0,12},{4,0},{8,4},{12,8},{1,13},{5,1},{9,5},{13,9},{2,14},{6,2},{... | collective-permute-start | bytes 1179656 | tf_op jit(solution)/shard_map/ppermute | solution.py:186
  182.4 4.2 %collective-permute-done.19 = bf16[384,512]{1,0:T(8,128)(2,1)S(1)} collective-permute-done((bf16[384,512]{1,0:T(8,128)(2,1)}, bf16[384,512]{1,0:T(8,128)(2,1)S(1)}, u32[]{:S(2)}, u32[]{:S(2)}) %collective-permute-start.19) | collective-permute-done | bytes 393248 | tf_op jit(solution)/shard_map/ppermute | solution.py:186
  186.7 1.7 collective-permute-done.23
  188.3 6.1 %collective-permute-done.26 = bf16[384,512]{1,0:T(8,128)(2,1)S(1)} collective-permute-done((bf16[384,512]{1,0:T(8,128)(2,1)S(1)}, bf16[384,512]{1,0:T(8,128)(2,1)S(1)}, u32[]{:S(2)}, u32[]{:S(2)}) %collective-permute-start.26) | collective-permute-done | bytes 393248 | tf_op jit(solution)/shard_map/ppermute | solution.py:186
  194.5 1.9 add_convert_fusion
  (67 shorter events, 4.9 us)
Async XLA Ops:
  0.0 37.0 %copy-start = (bf16[1,8192,64]{1,2,0:T(8,128)(2,1)S(1)}, bf16[1,8192,64]{1,2,0:T(8,128)(2,1)}, u32[]{:S(2)}) copy-start(bf16[1,8192,64]{1,2,0:T(8,128)(2,1)} %param.18) | copy-start | bytes 3145732
  0.0 48.1 %collective-permute-start.8 = (bf16[8192,512]{1,0:T(8,128)(2,1)}, bf16[8192,512]{1,0:T(8,128)(2,1)}, u32[]{:S(2)}, u32[]{:S(2)}) collective-permute-start(bf16[8192,512]{1,0:T(8,128)(2,1)} %refs_3_.2), channel_id=1, source_target_pairs={{0,1},{1,0},{2,3},{3,2},{4,5},{5,4},{6,7},{7,6},{8,9},{9,8},{10,11... | collective-permute-start | bytes 25165832 | tf_op jit(solution)/shard_map/ppermute | solution.py:186
  0.5 144.1 %collective-permute-start.18 = (bf16[512,8192]{1,0:T(8,128)(2,1)}, bf16[512,8192]{1,0:T(8,128)(2,1)}, u32[]{:S(2)}, u32[]{:S(2)}) collective-permute-start(bf16[512,8192]{1,0:T(8,128)(2,1)} %refs_0_.5), channel_id=1, source_target_pairs={{0,1},{1,0},{2,3},{3,2},{4,5},{5,4},{6,7},{7,6},{8,9},{9,8},{10,11... | collective-permute-start | bytes 25165832 | tf_op jit(solution)/shard_map/ppermute | solution.py:186
  0.5 15.2 %collective-permute-start = (bf16[384,512]{1,0:T(8,128)(2,1)}, bf16[384,512]{1,0:T(8,128)(2,1)S(1)}, u32[]{:S(2)}, u32[]{:S(2)}) collective-permute-start(bf16[384,512]{1,0:T(8,128)(2,1)} %refs_0_.3), channel_id=1, source_target_pairs={{0,4},{4,8},{8,12},{12,0},{1,5},{5,9},{9,13},{13,1},{2,6},{6,10},{... | collective-permute-start | bytes 1179656 | tf_op jit(solution)/shard_map/ppermute | solution.py:186
  3.5 19.4 %collective-permute-start.2 = (bf16[384,512]{1,0:T(8,128)(2,1)}, bf16[384,512]{1,0:T(8,128)(2,1)S(1)}, u32[]{:S(2)}, u32[]{:S(2)}) collective-permute-start(bf16[384,512]{1,0:T(8,128)(2,1)} %refs_0_.3), channel_id=1, source_target_pairs={{0,12},{4,0},{8,4},{12,8},{1,13},{5,1},{9,5},{13,9},{2,14},{6,2},{... | collective-permute-start | bytes 1179656 | tf_op jit(solution)/shard_map/ppermute | solution.py:186
  5.6 18.7 %collective-permute-start.4 = (bf16[384,512]{1,0:T(8,128)(2,1)}, bf16[384,512]{1,0:T(8,128)(2,1)S(1)}, u32[]{:S(2)}, u32[]{:S(2)}) collective-permute-start(bf16[384,512]{1,0:T(8,128)(2,1)} %refs_0_.3), channel_id=1, source_target_pairs={{0,2},{2,0},{1,3},{3,1},{4,6},{6,4},{5,7},{7,5},{8,10},{10,8},{9,1... | collective-permute-start | bytes 1179656 | tf_op jit(solution)/shard_map/ppermute | solution.py:186
  15.7 32.4 %copy-start.9 = (bf16[384,512]{1,0:T(8,128)(2,1)}, bf16[384,512]{1,0:T(8,128)(2,1)S(1)}, u32[]{:S(2)}) copy-start(bf16[384,512]{1,0:T(8,128)(2,1)S(1)} %collective-permute-done.refs_2_) | copy-start | bytes 1179652
  15.7 9.3 %collective-permute-start.1 = (bf16[384,512]{1,0:T(8,128)(2,1)S(1)}, bf16[384,512]{1,0:T(8,128)(2,1)S(1)}, u32[]{:S(2)}, u32[]{:S(2)}) collective-permute-start(bf16[384,512]{1,0:T(8,128)(2,1)S(1)} %collective-permute-done.refs_2_), channel_id=1, source_target_pairs={{4,8},{8,12},{5,9},{9,13},{6,10},{10,14},{7,11},{11,15},{20,24},{2... | collective-permute-start | bytes 1179656 | tf_op jit(solution)/shard_map/ppermute | solution.py:204
  23.0 25.2 %copy-start.10 = (bf16[384,512]{1,0:T(8,128)(2,1)}, bf16[384,512]{1,0:T(8,128)(2,1)S(1)}, u32[]{:S(2)}) copy-start(bf16[384,512]{1,0:T(8,128)(2,1)S(1)} %collective-permute-done.2.refs_4_) | copy-start | bytes 1179652
  23.0 12.4 %collective-permute-start.3 = (bf16[384,512]{1,0:T(8,128)(2,1)S(1)}, bf16[384,512]{1,0:T(8,128)(2,1)}, u32[]{:S(2)}, u32[]{:S(2)}) collective-permute-start(bf16[384,512]{1,0:T(8,128)(2,1)S(1)} %collective-permute-done.2.refs_4_), channel_id=1, source_target_pairs={{8,4},{4,0},{9,5},{5,1},{10,6},{6,2},{11,7},{7,3},{24,20},{20,16},... | collective-permute-start | bytes 1179656 | tf_op jit(solution)/shard_map/ppermute | solution.py:205
  24.3 0.8 copy-start.11
  25.1 23.1 %collective-permute-start.9 = (bf16[1,64,8192]{2,1,0:T(8,128)(2,1)}, bf16[1,64,8192]{2,1,0:T(8,128)(2,1)S(1)}, u32[]{:S(2)}, u32[]{:S(2)}) collective-permute-start(bf16[1,64,8192]{2,1,0:T(8,128)(2,1)} %bitcast.47), channel_id=1, source_target_pairs={{0,1},{1,0},{2,3},{3,2},{4,5},{5,4},{6,7},{7,6},{8,9},{9,8},{10,11... | collective-permute-start | bytes 3145736 | tf_op jit(solution)/shard_map/ppermute | solution.py:186
  25.1 10.4 %copy-start.12 = (bf16[384,512]{1,0:T(8,128)(2,1)}, bf16[384,512]{1,0:T(8,128)(2,1)S(1)}, u32[]{:S(2)}) copy-start(bf16[384,512]{1,0:T(8,128)(2,1)S(1)} %collective-permute-done.1) | copy-start | bytes 1179652
  25.1 13.7 %collective-permute-start.5 = (bf16[384,512]{1,0:T(8,128)(2,1)S(1)}, bf16[384,512]{1,0:T(8,128)(2,1)}, u32[]{:S(2)}, u32[]{:S(2)}) collective-permute-start(bf16[384,512]{1,0:T(8,128)(2,1)S(1)} %collective-permute-done.refs_2_), channel_id=1, source_target_pairs={{0,2},{2,0},{1,3},{3,1},{4,6},{6,4},{5,7},{7,5},{8,10},{10,8},{9,1... | collective-permute-start | bytes 1179656 | tf_op jit(solution)/shard_map/ppermute | solution.py:186
  35.4 9.7 %collective-permute-start.6 = (bf16[384,512]{1,0:T(8,128)(2,1)S(1)}, bf16[384,512]{1,0:T(8,128)(2,1)}, u32[]{:S(2)}, u32[]{:S(2)}) collective-permute-start(bf16[384,512]{1,0:T(8,128)(2,1)S(1)} %collective-permute-done.2.refs_4_), channel_id=1, source_target_pairs={{0,2},{2,0},{1,3},{3,1},{4,6},{6,4},{5,7},{7,5},{8,10},{10,8},{9,1... | collective-permute-start | bytes 1179656 | tf_op jit(solution)/shard_map/ppermute | solution.py:186
  38.8 18.9 %copy-start.5 = (bf16[384,512]{1,0:T(8,128)(2,1)}, bf16[384,512]{1,0:T(8,128)(2,1)S(1)}, u32[]{:S(2)}) copy-start(bf16[384,512]{1,0:T(8,128)(2,1)S(1)} %broadcast_select_fusion.refs_0_) | copy-start | bytes 1179652
  45.1 23.0 %collective-permute-start.7 = (bf16[384,512]{1,0:T(8,128)(2,1)S(1)}, bf16[384,512]{1,0:T(8,128)(2,1)}, u32[]{:S(2)}, u32[]{:S(2)}) collective-permute-start(bf16[384,512]{1,0:T(8,128)(2,1)S(1)} %broadcast_select_fusion.refs_0_), channel_id=1, source_target_pairs={{0,2},{2,0},{1,3},{3,1},{4,6},{6,4},{5,7},{7,5},{8,10},{10,8},{9,1... | collective-permute-start | bytes 1179656 | tf_op jit(solution)/shard_map/ppermute | solution.py:186
  48.1 1.0 copy-start.2
  58.5 23.4 %all-to-all-start = ((bf16[32,16,512]{2,0,1:T(8,128)(2,1)}), bf16[32,16,512]{2,0,1:T(8,128)(2,1)S(1)}, u32[]{:S(2)}, u32[]{:S(2)}) async-start(bf16[32,16,512]{2,0,1:T(8,128)(2,1)} %bitcast.45), calls=%async_computation | async-start | bytes 1048576 | tf_op jit(solution)/shard_map/all_to_all | solution.py:285
  68.2 36.6 %copy-start.13 = (bf16[24,1024]{1,0:T(8,128)(2,1)S(1)}, bf16[24,1024]{1,0:T(8,128)(2,1)}, u32[]{:S(2)}) copy-start(bf16[24,1024]{1,0:T(8,128)(2,1)} %param.21) | copy-start | bytes 147460
  68.2 36.6 %copy-start.14 = (bf16[24,1024]{1,0:T(8,128)(2,1)S(1)}, bf16[24,1024]{1,0:T(8,128)(2,1)}, u32[]{:S(2)}) copy-start(bf16[24,1024]{1,0:T(8,128)(2,1)} %param.22) | copy-start | bytes 147460
  73.5 31.3 %copy-start.15 = (s32[24]{0:T(128)S(1)}, s32[24]{0:T(128)}, u32[]{:S(2)}) copy-start(s32[24]{0:T(128)} %param.15) | copy-start | bytes 292
  73.5 1.7 collective-permute-start.11
  73.9 20.3 %collective-permute-start.10 = (f32[384,512]{1,0:T(8,128)}, f32[384,512]{1,0:T(8,128)S(1)}, u32[]{:S(2)}, u32[]{:S(2)}) collective-permute-start(f32[384,512]{1,0:T(8,128)} %get-tuple-element.33), channel_id=1, source_target_pairs={{0,1},{1,0},{2,3},{3,2},{4,5},{5,4},{6,7},{7,6},{8,9},{9,8},{10,11... | collective-permute-start | bytes 2359304 | tf_op jit(solution)/shard_map/ppermute | solution.py:186
  76.5 7.0 %collective-permute-start.12 = (bf16[192,128]{1,0:T(8,128)(2,1)S(1)}, bf16[192,128]{1,0:T(8,128)(2,1)S(1)}, u32[]{:S(2)}, u32[]{:S(2)}) collective-permute-start(bf16[192,128]{1,0:T(8,128)(2,1)S(1)} %pad_maximum_fusion), channel_id=1, source_target_pairs={{0,2},{2,0},{1,3},{3,1},{4,6},{6,4},{5,7},{7,5},{8,10},{10,8},{9,1... | collective-permute-start | bytes 147464 | tf_op jit(solution)/shard_map/ppermute | solution.py:186
  82.0 13.9 %copy-start.4 = (bf16[32,16,512]{2,0,1:T(8,128)(2,1)}, bf16[32,16,512]{2,0,1:T(8,128)(2,1)S(1)}, u32[]{:S(2)}) copy-start(bf16[32,16,512]{2,0,1:T(8,128)(2,1)S(1)} %all-to-all-done) | copy-start | bytes 1572868
  82.0 13.8 %collective-permute-start.16 = (bf16[512,512]{1,0:T(8,128)(2,1)S(1)}, bf16[512,512]{1,0:T(8,128)(2,1)S(1)}, u32[]{:S(2)}, u32[]{:S(2)}) collective-permute-start(bf16[512,512]{1,0:T(8,128)(2,1)S(1)} %bitcast.60), channel_id=1, source_target_pairs={{0,16},{16,0},{1,17},{17,1},{2,18},{18,2},{3,19},{19,3},{4,20},{20... | collective-permute-start | bytes 1572872 | tf_op jit(solution)/shard_map/ppermute | solution.py:286
  83.6 5.9 %collective-permute-start.13 = (bf16[192,128]{1,0:T(8,128)(2,1)S(1)}, bf16[192,128]{1,0:T(8,128)(2,1)S(1)}, u32[]{:S(2)}, u32[]{:S(2)}) collective-permute-start(bf16[192,128]{1,0:T(8,128)(2,1)S(1)} %fusion.20), channel_id=1, source_target_pairs={{0,4},{4,8},{8,12},{12,0},{1,5},{5,9},{9,13},{13,1},{2,6},{6,10},{... | collective-permute-start | bytes 147464 | tf_op jit(solution)/shard_map/ppermute | solution.py:186
  84.7 5.7 %collective-permute-start.14 = (bf16[192,128]{1,0:T(8,128)(2,1)S(1)}, bf16[192,128]{1,0:T(8,128)(2,1)S(1)}, u32[]{:S(2)}, u32[]{:S(2)}) collective-permute-start(bf16[192,128]{1,0:T(8,128)(2,1)S(1)} %fusion.20), channel_id=1, source_target_pairs={{0,8},{4,12},{8,0},{12,4},{1,9},{5,13},{9,1},{13,5},{2,10},{6,14},... | collective-permute-start | bytes 147464 | tf_op jit(solution)/shard_map/ppermute | solution.py:186
  89.5 4.1 %collective-permute-start.15 = (bf16[192,128]{1,0:T(8,128)(2,1)S(1)}, bf16[192,128]{1,0:T(8,128)(2,1)S(1)}, u32[]{:S(2)}, u32[]{:S(2)}) collective-permute-start(bf16[192,128]{1,0:T(8,128)(2,1)S(1)} %fusion.20), channel_id=1, source_target_pairs={{0,12},{4,0},{8,4},{12,8},{1,13},{5,1},{9,5},{13,9},{2,14},{6,2},{... | collective-permute-start | bytes 147464 | tf_op jit(solution)/shard_map/ppermute | solution.py:186
  94.3 1.6 copy-start.7
  95.8 0.8 copy-start.8
  100.2 16.7 %all-to-all-start.1 = ((bf16[16,24,512]{2,1,0:T(8,128)(2,1)}), bf16[16,24,512]{2,1,0:T(8,128)(2,1)S(1)}, u32[]{:S(2)}, u32[]{:S(2)}) async-start(bf16[16,24,512]{2,1,0:T(8,128)(2,1)} %bitcast.64), calls=%async_computation.1 | async-start | bytes 786432 | tf_op jit(solution)/shard_map/all_to_all | solution.py:304
  144.4 1.7 copy-start.3
  144.4 1.7 collective-permute-start.17
  146.2 0.7 copy-start.6
  149.7 11.4 %collective-permute-start.21 = (bf16[384,512]{1,0:T(8,128)(2,1)}, bf16[384,512]{1,0:T(8,128)(2,1)S(1)}, u32[]{:S(2)}, u32[]{:S(2)}) collective-permute-start(bf16[384,512]{1,0:T(8,128)(2,1)} %shard_map.122), channel_id=1, source_target_pairs={{0,2},{2,0},{1,3},{3,1},{4,6},{6,4},{5,7},{7,5},{8,10},{10,8},{9,1... | collective-permute-start | bytes 1179656 | tf_op jit(solution)/shard_map/ppermute | solution.py:186
  151.0 45.5 %copy-start.1 = (bf16[1,8192,64]{1,2,0:T(8,128)(2,1)S(1)}, bf16[1,8192,64]{1,2,0:T(8,128)(2,1)}, u32[]{:S(2)}) copy-start(bf16[1,8192,64]{1,2,0:T(8,128)(2,1)} %param.18) | copy-start | bytes 3145732
  158.4 12.2 %collective-permute-start.20 = (bf16[384,512]{1,0:T(8,128)(2,1)}, bf16[384,512]{1,0:T(8,128)(2,1)S(1)}, u32[]{:S(2)}, u32[]{:S(2)}) collective-permute-start(bf16[384,512]{1,0:T(8,128)(2,1)} %get-tuple-element.41), channel_id=1, source_target_pairs={{0,2},{2,0},{1,3},{3,1},{4,6},{6,4},{5,7},{7,5},{8,10},{10,8},{9,1... | collective-permute-start | bytes 1179656 | tf_op jit(solution)/shard_map/ppermute | solution.py:186
  162.1 11.1 %collective-permute-start.22 = (bf16[384,512]{1,0:T(8,128)(2,1)S(1)}, bf16[384,512]{1,0:T(8,128)(2,1)S(1)}, u32[]{:S(2)}, u32[]{:S(2)}) collective-permute-start(bf16[384,512]{1,0:T(8,128)(2,1)S(1)} %add_convert_fusion.3), channel_id=1, source_target_pairs={{0,4},{4,8},{1,5},{5,9},{2,6},{6,10},{3,7},{7,11},{16,20},{20,24},... | collective-permute-start | bytes 1179656 | tf_op jit(solution)/shard_map/ppermute | solution.py:226
  165.2 13.9 %collective-permute-start.24 = (bf16[384,512]{1,0:T(8,128)(2,1)}, bf16[384,512]{1,0:T(8,128)(2,1)S(1)}, u32[]{:S(2)}, u32[]{:S(2)}) collective-permute-start(bf16[384,512]{1,0:T(8,128)(2,1)} %get-tuple-element.46), channel_id=1, source_target_pairs={{0,2},{2,0},{1,3},{3,1},{4,6},{6,4},{5,7},{7,5},{8,10},{10,8},{9,1... | collective-permute-start | bytes 1179656 | tf_op jit(solution)/shard_map/ppermute | solution.py:186
  166.1 13.0 %collective-permute-start.25 = (bf16[384,512]{1,0:T(8,128)(2,1)S(1)}, bf16[384,512]{1,0:T(8,128)(2,1)S(1)}, u32[]{:S(2)}, u32[]{:S(2)}) collective-permute-start(bf16[384,512]{1,0:T(8,128)(2,1)S(1)} %add_convert_fusion.3), channel_id=1, source_target_pairs={{12,8},{8,4},{13,9},{9,5},{14,10},{10,6},{15,11},{11,7},{28,24},{2... | collective-permute-start | bytes 1179656 | tf_op jit(solution)/shard_map/ppermute | solution.py:227
  166.8 19.9 %collective-permute-start.19 = (bf16[384,512]{1,0:T(8,128)(2,1)}, bf16[384,512]{1,0:T(8,128)(2,1)S(1)}, u32[]{:S(2)}, u32[]{:S(2)}) collective-permute-start(bf16[384,512]{1,0:T(8,128)(2,1)} %get-tuple-element.38), channel_id=1, source_target_pairs={{0,2},{2,0},{1,3},{3,1},{4,6},{6,4},{5,7},{7,5},{8,10},{10,8},{9,1... | collective-permute-start | bytes 1179656 | tf_op jit(solution)/shard_map/ppermute | solution.py:186
  174.4 13.9 %collective-permute-start.23 = (bf16[384,512]{1,0:T(8,128)(2,1)S(1)}, bf16[384,512]{1,0:T(8,128)(2,1)S(1)}, u32[]{:S(2)}, u32[]{:S(2)}) collective-permute-start(bf16[384,512]{1,0:T(8,128)(2,1)S(1)} %add_convert_fusion.2), channel_id=1, source_target_pairs={{0,4},{4,8},{8,12},{12,0},{1,5},{5,9},{9,13},{13,1},{2,6},{6,10},{... | collective-permute-start | bytes 1179656 | tf_op jit(solution)/shard_map/ppermute | solution.py:186
  180.3 14.2 %collective-permute-start.26 = (bf16[384,512]{1,0:T(8,128)(2,1)S(1)}, bf16[384,512]{1,0:T(8,128)(2,1)S(1)}, u32[]{:S(2)}, u32[]{:S(2)}) collective-permute-start(bf16[384,512]{1,0:T(8,128)(2,1)S(1)} %add_convert_fusion.1), channel_id=1, source_target_pairs={{0,12},{4,0},{8,4},{12,8},{1,13},{5,1},{9,5},{13,9},{2,14},{6,2},{... | collective-permute-start | bytes 1179656 | tf_op jit(solution)/shard_map/ppermute | solution.py:186

commit v4 on v1

v4 whole, which is shorter than its diff:
```python
import jax
import jax.numpy as jnp
from jax import lax
from jax.experimental import pallas as pl
from jax.experimental.pallas import tpu as pltpu
from jax.sharding import Mesh
from jax.sharding import PartitionSpec as P

HEADS = 64
HEAD_DIM = 128
ADP = ("z", "y", "core")
NT = (((1,), (1,)), ((), ()))
VMEM_LIMIT = 60 << 20
QUICK = pl.CostEstimate(flops=1, bytes_accessed=1, transcendentals=0)


def adapter_pair(first_core, own, other):
    own, other = own[0], other[0]
    return jnp.concatenate(
        [jnp.where(first_core, own, other), jnp.where(first_core, other, own)], axis=0
    )


def low_kernel(places, first, count, *refs):
    blocks, a_own, a_other = (refs[i * count : (i + 1) * count] for i in range(3))
    rest, out = refs[3 * count : -1], refs[-1]
    first_core = places[0] % 2 == 0
    total = None
    for i in range(count):
        pair = adapter_pair(first_core, a_own[i], a_other[i])
        part = lax.dot_general(blocks[i][...], pair, NT, preferred_element_type=jnp.float32)
        total = part if total is None else total + part
    if not rest:
        out[...] = total
        return
    low_in, slot = rest
    total += low_in[...]
    rank = total.shape[1] // 2
    mine = places[0] - places[0] % 2
    low = jnp.where(slot[...] == mine, total[:, :rank], 0.0)
    low += jnp.where(slot[...] == mine + 1, total[:, rank:], 0.0)
    half = low.shape[0] // 2
    out[...] = jnp.concatenate([low[:half], low[half:]], axis=1)


def add_low(places, first, blocks, down, down_other, rest):
    count = len(blocks)
    rows, width = blocks[0].shape
    rank = down.shape[1]
    flat = lambda shape: pl.BlockSpec(shape, lambda j, p: (0, 0))
    maps = [
        pl.BlockSpec((1, rank, width), lambda j, p, i=i: (0, 0, p[first + i])) for i in range(count)
    ]
    shape = (rows // 2, 2 * rank) if rest else (rows, 2 * rank)

    def kernel(places, *refs):
        low_kernel(places, first, count, *refs)

    return pl.pallas_call(
        kernel,
        grid_spec=pltpu.PrefetchScalarGridSpec(
            num_scalar_prefetch=1,
            grid=(1,),
            in_specs=[flat((rows, width))] * count + maps * 2 + [flat(r.shape) for r in rest],
            out_specs=flat(shape),
        ),
        out_shape=jax.ShapeDtypeStruct(shape, jnp.float32),
        compiler_params=pltpu.CompilerParams(vmem_limit_bytes=VMEM_LIMIT),
        cost_estimate=QUICK,
    )(places, *blocks, *[down] * count, *[down_other] * count, *rest)


def base_kernel(places, count, *refs):
    blocks, w_own, w_other = (refs[i * count : (i + 1) * count] for i in range(3))
    ins, outs = refs[3 * count : -2], refs[-2:]
    for j, (out, weights) in enumerate(zip(outs, (w_own, w_other))):
        total = ins[j][...] if ins else None
        for block, weight in zip(blocks, weights):
            part = jnp.dot(block[...], weight[...], preferred_element_type=jnp.float32)
            total = part if total is None else total + part
        out[...] = total


def add_base(places, first, blocks, weight, weight_other, sums):
    count = len(blocks)
    rows, width = blocks[0].shape
    cols = weight.shape[1]
    tile = cols // 2 if cols % 256 == 0 else cols
    sum_spec = pl.BlockSpec((rows, tile), lambda j, p: (0, j))
    weights = [
        pl.BlockSpec((width, tile), lambda j, p, i=i: (p[first + i], j)) for i in range(count)
    ]

    def kernel(places, *refs):
        base_kernel(places, count, *refs)

    return pl.pallas_call(
        kernel,
        grid_spec=pltpu.PrefetchScalarGridSpec(
            num_scalar_prefetch=1,
            grid=(cols // tile,),
            in_specs=[pl.BlockSpec((rows, width), lambda j, p: (0, 0))] * count
            + weights * 2
            + [sum_spec] * len(sums),
            out_specs=[sum_spec] * 2,
        ),
        out_shape=[jax.ShapeDtypeStruct((rows, cols), jnp.float32)] * 2,
        compiler_params=pltpu.CompilerParams(vmem_limit_bytes=VMEM_LIMIT),
        cost_estimate=QUICK,
    )(places, *blocks, *[weight] * count, *[weight_other] * count, *sums)


def query_kernel(half, own, received, low, slot, owners, up_own, up_other, out):
    step = pl.program_id(0)
    lanes = low.shape[1]
    rank = lanes // 2
    part = rank // 2
    depth = up_own.shape[0]
    shape = (lanes, depth)
    lane = lax.broadcasted_iota(jnp.int32, shape, 1) % part
    row = lax.broadcasted_iota(jnp.int32, shape, 0)
    live = slot[...] == owners[...]
    total = own[...] + received[...]
    for h, up in ((half[0], up_own), (1 - half[0], up_other)):
        copies = (row == lane + rank * step + part * h).astype(jnp.bfloat16)
        spread = jnp.dot(low[...], copies, preferred_element_type=jnp.float32)
        spread = jnp.where(live, spread, 0.0).astype(jnp.bfloat16)
        total += jnp.dot(spread, up[...], preferred_element_type=jnp.float32)
    out[...] = (total * HEAD_DIM ** (-0.5)).astype(out.dtype)


def make_query(half, own, received, low, slot, owners, up_own, up_other):
    rows, cols = own.shape
    tile = rows // 2
    depth = up_own.shape[0]
    by_rows = lambda width: pl.BlockSpec((tile, width), lambda j, h: (j, 0))
    whole = lambda array: pl.BlockSpec(array.shape, lambda j, h: (0, 0))
    return pl.pallas_call(
        query_kernel,
        grid_spec=pltpu.PrefetchScalarGridSpec(
            num_scalar_prefetch=1,
            grid=(2,),
            in_specs=[
                by_rows(cols),
                by_rows(received.shape[1]),
                whole(low),
                by_rows(1),
                whole(owners),
                whole(up_own),
                whole(up_other),
            ],
            out_specs=by_rows(cols),
        ),
        out_shape=jax.ShapeDtypeStruct((rows, cols), jnp.bfloat16),
        compiler_params=pltpu.CompilerParams(vmem_limit_bytes=VMEM_LIMIT),
        cost_estimate=QUICK,
    )(half, own, received, low, slot, owners, up_own, up_other)


def output_kernel(places, count, own, other, *refs):
    for w_own, w_other, out in zip(refs[:count], refs[count : 2 * count], refs[2 * count :]):
        total = jnp.dot(own[...], w_own[...], preferred_element_type=jnp.float32)
        total += jnp.dot(other[...], w_other[...], preferred_element_type=jnp.float32)
        out[...] = total.astype(out.dtype)


def output_partial(places, first, count, own, other, weight, weight_other, width):
    rows, depth = own.shape
    tile = width // 2 if width % 256 == 0 else width
    steps = width // tile
    whole = pl.BlockSpec((rows, depth), lambda j, p: (0, 0))
    weights = [
        pl.BlockSpec((depth, tile), lambda j, p, i=i: (0, p[first + i] * steps + j))
        for i in range(count)
    ]

    def kernel(places, *refs):
        output_kernel(places, count, *refs)

    return pl.pallas_call(
        kernel,
        grid_spec=pltpu.PrefetchScalarGridSpec(
            num_scalar_prefetch=1,
            grid=(steps,),
            in_specs=[whole, whole] + weights * 2,
            out_specs=[pl.BlockSpec((rows, tile), lambda j, p: (0, j))] * count,
        ),
        out_shape=[jax.ShapeDtypeStruct((rows, width), jnp.bfloat16)] * count,
        compiler_params=pltpu.CompilerParams(vmem_limit_bytes=VMEM_LIMIT),
        cost_estimate=QUICK,
    )(places, own, other, *[weight] * count, *[weight_other] * count)


def attention(query, cache_length, key_cache, value_cache, k_new, v_new):
    local_reqs = query.shape[0]
    kv_count, _, span, dim = key_cache.shape
    group = HEADS // kv_count
    query = query.reshape(local_reqs, kv_count, group, dim)
    k_new = k_new.reshape(local_reqs, kv_count, dim)
    v_new = v_new.reshape(local_reqs, kv_count, dim)
    live = (jnp.arange(span)[None, :] < cache_length[:, None])[None, :, None, :]
    scores = jnp.einsum("rkge,krje->krgj", query, key_cache, preferred_element_type=jnp.float32)
    fresh = jnp.einsum("rkge,rke->krg", query, k_new, preferred_element_type=jnp.float32)
    scores = jnp.where(live, scores, -jnp.inf)
    top = jnp.maximum(jnp.max(scores, axis=3), fresh)
    expd = jnp.where(live, jnp.exp(scores - top[:, :, :, None]), 0.0)
    expf = jnp.exp(fresh - top)
    total = jnp.sum(expd, axis=3) + expf
    probs = (expd / total[:, :, :, None]).astype(jnp.bfloat16)
    probf = (expf / total).astype(jnp.bfloat16)
    context = jnp.einsum("krgj,krje->rkge", probs, value_cache, preferred_element_type=jnp.float32)
    fresh_part = jnp.einsum("krg,rke->rkge", probf.astype(jnp.float32), v_new.astype(jnp.float32))
    return (context + fresh_part).astype(jnp.bfloat16).reshape(local_reqs, HEADS * dim)


def shift(value, axis, by):
    size = lax.axis_size(axis)
    return lax.ppermute(value, axis, [(i, (i + by) % size) for i in range(size)])


def after(value, *others):
    return lax.optimization_barrier((value, *others))[0]


def swap_sides(value, layers):
    return lax.ppermute(value, ("z", "y"), [(2 * i + j, 2 * i + 1 - j) for i in layers for j in (0, 1)])


def gather_features(tokens, down_other, query_weight_other):
    layers, sides = lax.axis_size("z"), lax.axis_size("y")
    z = lax.axis_index("z")
    if layers != 4 or sides != 2:
        entries = []
        for k in range(layers):
            block = shift(tokens, "z", k) if k else tokens
            entries.append(((z - k) % layers, [block, shift(block, "y", 1)][:sides]))
        return entries[:-1], entries[-1:], down_other, query_weight_other
    side = swap_sides(tokens, range(4))
    below = lax.ppermute(tokens, "z", [(0, 1), (1, 2), (2, 3)])
    above = lax.ppermute(tokens, "z", [(1, 0), (2, 1), (3, 2)])
    below, above, side, down_other = lax.optimization_barrier((below, above, side, down_other))
    from_below = lax.ppermute(below, "z", [(1, 2), (2, 3)])
    from_above = lax.ppermute(above, "z", [(2, 1), (1, 0)])
    below_side = swap_sides(below, (1, 2, 3))
    above_side = swap_sides(above, (0, 1, 2))
    from_below, from_above, query_weight_other, below_side = lax.optimization_barrier(
        (from_below, from_above, query_weight_other, below_side)
    )
    far = lax.ppermute(after(tokens, from_below), "z", [(0, 3), (3, 0)])
    two = jnp.where(z >= 2, from_below, from_above)
    two_side = swap_sides(two, range(4))
    far_side = swap_sides(far, (0, 3))
    early = [
        (z, [tokens, side]),
        ((z - 1) % 4, [below, below_side]),
        ((z + 1) % 4, [above, above_side]),
    ]
    late = [((z + 2) % 4, [two, two_side]), (3 - z, [far, far_side])]
    return early, late, down_other, query_weight_other


def spread_up_maps(maps, half, width, early):
    layers, sides = lax.axis_size("z"), lax.axis_size("y")
    z, y, core = lax.axis_index("z"), lax.axis_index("y"), lax.axis_index("core")
    part = maps.shape[0] // 2
    if layers != 4 or sides != 2:
        maps = lax.dynamic_slice_in_dim(maps, half * part, part, 0)
        up = lax.all_to_all(maps, ADP, split_axis=1, concat_axis=0, tiled=True)
        return up, (jnp.arange(up.shape[0], dtype=jnp.int32) // part)[None, :]
    span = 4 * width
    maps = after(maps, early)
    pieces = []
    for k in range(4):
        piece = lax.dynamic_slice(maps, (half * part, (z + k) % 4 * span), (part, span))
        pieces.append(shift(piece, "z", k) if k else piece)
    pieces = jnp.stack(pieces)
    for axis, index in (("y", y), ("core", core)):
        span //= 2
        kept = lax.dynamic_slice_in_dim(pieces, index * span, span, 2)
        sent = lax.dynamic_slice_in_dim(pieces, (1 - index) * span, span, 2)
        pieces = jnp.concatenate([kept, shift(sent, axis, 1)])
    index = jnp.arange(16 * part, dtype=jnp.int32) // part
    layer = (z - index % 4) % 4
    owners = (layer * 2 + (y + index // 4) % 2) * 2 + (core + index // 8) % 2
    return pieces.reshape(16 * part, width), owners.astype(jnp.int32)[None, :]


def scatter_layers(parts):
    layers = lax.axis_size("z")
    wide = lambda value: value.astype(jnp.float32)
    narrow = lambda value: value.astype(jnp.bfloat16)
    if layers != 4:
        return sum([wide(shift(narrow(parts[k]), "z", k)) for k in range(1, layers)], parts[0])
    two = narrow(parts[2])
    up = lax.ppermute(two, "z", [(0, 1), (1, 2)])
    down = lax.ppermute(two, "z", [(3, 2), (2, 1)])
    above = shift(narrow(parts[1] + wide(up)), "z", 1)
    below = shift(narrow(parts[3] + wide(down)), "z", 3)
    return parts[0] + wide(above) + wide(below)


def shards(
    tokens,
    request_adapter,
    adapter_storage_slot,
    cache_length,
    query_weight,
    adapter_down_maps,
    adapter_up_maps,
    key_cache,
    value_cache,
    new_token_key,
    new_token_value,
    output_weight,
):
    layers, sides = lax.axis_size("z"), lax.axis_size("y")
    z, y, core = lax.axis_index("z"), lax.axis_index("y"), lax.axis_index("core")
    rows, width = tokens.shape
    total_adapters = adapter_storage_slot.shape[0]
    rank = adapter_down_maps.shape[2]
    depth = output_weight.shape[0]
    chips_of = lambda layer: [
        (layer % layers) * sides + (y + side) % sides for side in range(sides)
    ]

    down = jnp.swapaxes(adapter_down_maps, 1, 2)
    down_other = shift(down, "core", 1)
    query_weight_other = shift(query_weight, "core", 1)

    ids = request_adapter[:, 0]
    numbers = jnp.arange(total_adapters, dtype=jnp.int32)
    slot = jnp.sum(
        jnp.where(ids[:, None] == numbers[None, :], adapter_storage_slot[None, :], 0), axis=1
    )[:, None]

    early, late, down_other, query_weight_other = gather_features(
        tokens, down_other, query_weight_other
    )
    half = lax.axis_index("rep") % 2
    up, owners = spread_up_maps(jnp.swapaxes(adapter_up_maps, 1, 2)[0], half, width, late[-1][1][0])
    up_other = lax.ppermute(up, "rep", [(i, i ^ 1) for i in range(lax.axis_size("rep"))])
    out_order = [2, 1, 3, 0] if layers == 4 else list(range(1, layers)) + [0]
    out_keys = [(k, side) for k in out_order for side in reversed(range(sides))]
    chips = [chip for layer, _ in early + late for chip in chips_of(layer)]
    chips += [chips_of(z + k)[side] for k, side in out_keys]
    places = jnp.stack([2 * chip + core for chip in chips]).astype(jnp.int32)
    out_first = len(chips) - len(out_keys)
    early, late = ([block for _, pair in group for block in pair] for group in (early, late))

    weights, downs = (query_weight, query_weight_other), (down, down_other)
    base = add_base(after(places, late[0]), 0, early, *weights, ())
    low = add_low(after(places, base[0]), 0, early, *downs, ())
    count = len(late) // 2
    base = add_base(places, len(early), late[:count], *weights, base) if count else base
    low = add_low(after(places, base[0]), len(early), late, *downs, (low, slot))
    low = (low + shift(low, "core", 1)).astype(jnp.bfloat16)
    if sides == 2:
        low = low + shift(low, "y", 1)
    own, sent = add_base(
        after(places, low, up), len(early) + count, late[count:], *weights, base
    )
    received = shift(sent, "core", 1)
    output_weight_other = shift(after(output_weight, received), "core", 1)
    low = sum([shift(low, "z", k) for k in range(1, layers)], low)

    query = make_query(half.astype(jnp.int32).reshape(1), own, received, low, slot, owners, up, up_other)
    query_local = lax.all_to_all(query, ADP, split_axis=0, concat_axis=1, tiled=True)

    context = attention(
        query_local, cache_length, key_cache, value_cache, new_token_key, new_token_value
    )
    context = jnp.swapaxes(context.reshape(context.shape[0], -1, depth), 0, 1)
    context = lax.all_to_all(context, ADP, split_axis=0, concat_axis=0, tiled=True)
    context = context.reshape(rows, depth)
    context_other = shift(context, "core", 1)

    made = {}
    for first, count in ((0, 1), (1, len(out_keys) - 1)):
        outs = output_partial(
            places,
            out_first + first,
            count,
            context,
            context_other,
            output_weight,
            output_weight_other,
            width,
        )
        made.update(zip(out_keys[first : first + count], outs))
    other_side = {k: shift(made[k, 1], "y", 1) for k in out_order if sides == 2}
    parts = [None] * layers
    for k in out_order:
        parts[k] = after(made[k, 0], made[out_keys[-1]]).astype(jnp.float32)
        if sides == 2:
            parts[k] = parts[k] + other_side[k].astype(jnp.float32)
    return scatter_layers(parts).astype(jnp.bfloat16)


def solution(mesh):
    reps, adp = mesh.shape["rep"], mesh.shape["adp"]
    sides = 2 if adp == 16 else 1
    mesh = Mesh(mesh.devices.reshape(reps, adp // (2 * sides), sides, 2), ("rep",) + ADP)
    in_specs = (
        P("rep", ADP),
        P("rep", None),
        P(),
        P(("rep",) + ADP),
        P(None, ADP),
        P(ADP, None, None),
        P(ADP, None, None),
        P(None, ("rep",) + ADP, None, None),
        P(None, ("rep",) + ADP, None, None),
        P(("rep",) + ADP, None),
        P(("rep",) + ADP, None),
        P(ADP, None),
    )
    return jax.shard_map(
        shards, mesh=mesh, in_specs=in_specs, out_specs=P("rep", ADP), check_vma=False
    )
```

time: 215 us -> 212 us (0.986)
  starting transfers between devices: 57.4 us -> 51.9 us
  waiting for transfers between devices: 72.2 us -> 75.5 us
    ppermute x4, waiting for transfers between devices: 3.85 us -> 21.9 us  [the longest x1 12.1 us: gather_features(): from_above = lax.ppermute(above, 'z', [(2, 1), (1, 0)])]
    ppermute x5, waiting for transfers between devices: 14.3 us -> 0.01 us  [swap_sides(): lax.ppermute(value, ('z', 'y'), [(2 * i + j, 2 * i + 1 - j) for i in laye...]
    all_to_all x1 -> x0, starting transfers between devices: 14.1 us -> none  [shards(): up = lax.all_to_all(up, ADP, split_axis=1, concat_axis=0, tiled=True)]
    ppermute x16 -> x21, starting transfers between devices: 11 us -> 20.5 us  [shift(): lax.ppermute(value, axis, [(i, (i + by) % size) for i in range(size)])]
    ppermute x16 -> x21, waiting for transfers between devices: 32.1 us -> 28.3 us  [shift(): lax.ppermute(value, axis, [(i, (i + by) % size) for i in range(size)])]
    ppermute x1, waiting for transfers between devices: 1.71 us -> 4.03 us  [gather_features(): above = lax.ppermute(tokens, 'z', [(1, 0), (2, 1), (3, 2)])]
    pallas_call x6 -> x7, Pallas kernels: 36.7 us -> 35.3 us  [the longest x3 16.8 us: add_base(): pl.pallas_call(kernel, grid_spec=pltpu.PrefetchScalarGridSpec(num_scalar_...]
  transfers between devices with their start and end apart: 31 -> 35, of which waited for: 19 -> 19; matrix products, arithmetic and copies ran while one was open for 11% -> 12% of each run, Pallas kernels for 17% -> 14%
where the time goes in v4:
time: 212 us; the launch traced here: 211 us
  waiting for transfers between devices  75.5 us (36%)
  starting transfers between devices  51.9 us (24%)
  Pallas kernels  38.9 us (18%)
  blocking collectives  15.5 us (7%)
  other arithmetic  11.8 us (6%)
  matrix products  10.4 us (5%)
  local copies, waits for them, and re-layouts  6.83 us (3%)
    ppermute x21, waiting for transfers between devices, shift(): lax.ppermute(value, axis, [(i, (i + by) % size) for i in range(size)])  28.3 us
    ppermute x21, starting transfers between devices, shift(): lax.ppermute(value, axis, [(i, (i + by) % size) for i in range(size)])  20.5 us
    pallas_call x3, Pallas kernels, add_base(): pl.pallas_call(kernel, grid_spec=pltpu.PrefetchScalarGridSpec(num_scalar_...  16.8 us
    all_to_all x1, blocking collectives, shards(): lax.all_to_all(context, ADP, split_axis=0, concat_axis=0, tiled=True)  15.5 us
    ppermute x1, waiting for transfers between devices, gather_features(): from_above = lax.ppermute(above, 'z', [(2, 1), (1, 0)])  12.1 us
    all_to_all x1, waiting for transfers between devices, shards(): lax.all_to_all(query, ADP, split_axis=0, concat_axis=1, tiled=True)  12 us
    pallas_call x2, Pallas kernels, output_partial(): pl.pallas_call(kernel, grid_spec=pltpu.PrefetchScalarGridSpec(num_scalar_...  10.8 us
    ppermute x5, starting transfers between devices, swap_sides(): lax.ppermute(value, ('z', 'y'), [(2 * i + j, 2 * i + 1 - j) for i in laye...  10.7 us
  transfers between devices with their start and end apart: 35, of which 19 were waited for; matrix products, arithmetic and copies ran while one was open for 12% of the time, Pallas kernels for 14%

profile of v4, /device:TPU:0, one launch (start us, length us, event | category | flops | bytes accessed | tf_op | source)
XLA Modules:
  0.0 211.4 jit_solution(357218626420413310)
XLA Ops:
  0.5 4.9 %collective-permute-start = (bf16[384,512]{1,0:T(8,128)(2,1)}, bf16[384,512]{1,0:T(8,128)(2,1)S(1)}, u32[]{:S(2)}, u32[]{:S(2)}) collective-permute-start(bf16[384,512]{1,0:T(8,128)(2,1)} %refs_0_.3), channel_id=1, source_target_pairs={{0,4},{4,8},{8,12},{1,5},{5,9},{9,13},{2,6},{6,10},{10,14},{3,7},{... | collective-permute-start | bytes 1179656 | tf_op jit(solution)/shard_map/ppermute | solution.py:239
  5.5 1.3 collective-permute-start.1
  6.8 1.6 collective-permute-start.2
  8.3 5.9 %collective-permute-done.refs_2_ = bf16[384,512]{1,0:T(8,128)(2,1)S(1)} collective-permute-done((bf16[384,512]{1,0:T(8,128)(2,1)}, bf16[384,512]{1,0:T(8,128)(2,1)S(1)}, u32[]{:S(2)}, u32[]{:S(2)}) %collective-permute-start) | collective-permute-done | bytes 393248 | tf_op jit(solution)/shard_map/ppermute | solution.py:239
  14.3 4.0 %collective-permute-done.1.refs_4_ = bf16[384,512]{1,0:T(8,128)(2,1)S(1)} collective-permute-done((bf16[384,512]{1,0:T(8,128)(2,1)}, bf16[384,512]{1,0:T(8,128)(2,1)S(1)}, u32[]{:S(2)}, u32[]{:S(2)}) %collective-permute-start.1) | collective-permute-done | bytes 393248 | tf_op jit(solution)/shard_map/ppermute | solution.py:240
  19.0 1.3 collective-permute-start.5
  21.0 12.1 %collective-permute-done.5 = bf16[384,512]{1,0:T(8,128)(2,1)S(1)} collective-permute-done((bf16[384,512]{1,0:T(8,128)(2,1)S(1)}, bf16[384,512]{1,0:T(8,128)(2,1)S(1)}, u32[]{:S(2)}, u32[]{:S(2)}) %collective-permute-start.5) | collective-permute-done | bytes 393248 | tf_op jit(solution)/shard_map/ppermute | solution.py:243
  33.2 0.7 copy-done.14
  33.9 3.6 %collective-permute-start.10 = (bf16[384,512]{1,0:T(8,128)(2,1)}, bf16[384,512]{1,0:T(8,128)(2,1)S(1)}, u32[]{:S(2)}, u32[]{:S(2)}) collective-permute-start(bf16[384,512]{1,0:T(8,128)(2,1)} %refs_0_.3), channel_id=1, source_target_pairs={{0,12},{12,0},{1,13},{13,1},{2,14},{14,2},{3,15},{15,3},{16,28},{2... | collective-permute-start | bytes 1179656 | tf_op jit(solution)/shard_map/ppermute | solution.py:249
  37.6 3.4 %collective-permute-start.9 = (bf16[384,512]{1,0:T(8,128)(2,1)S(1)}, bf16[384,512]{1,0:T(8,128)(2,1)}, u32[]{:S(2)}, u32[]{:S(2)}) collective-permute-start(bf16[384,512]{1,0:T(8,128)(2,1)S(1)} %collective-permute-done.1.refs_4_), channel_id=1, source_target_pairs={{0,2},{2,0},{4,6},{6,4},{8,10},{10,8},{1,3},{3,1},{5,7},{7,5},{9,1... | collective-permute-start | bytes 1179656 | tf_op jit(solution)/shard_map/ppermute | solution.py:226
  41.1 5.4 %collective-permute-done.10.refs_2_.refs_0_ = bf16[384,512]{1,0:T(8,128)(2,1)S(1)} collective-permute-done((bf16[384,512]{1,0:T(8,128)(2,1)}, bf16[384,512]{1,0:T(8,128)(2,1)S(1)}, u32[]{:S(2)}, u32[]{:S(2)}) %collective-permute-start.10) | collective-permute-done | bytes 393248 | tf_op jit(solution)/shard_map/ppermute | solution.py:249
  46.5 1.3 dynamic-slice_bitcast_fusion
  47.8 2.3 %collective-permute-start.15 = (bf16[32,2048]{1,0:T(8,128)(2,1)S(1)}, bf16[32,2048]{1,0:T(8,128)(2,1)S(1)}, u32[]{:S(2)}, u32[]{:S(2)}) collective-permute-start(bf16[32,2048]{1,0:T(8,128)(2,1)S(1)} %get-tuple-element.71), channel_id=1, source_target_pairs={{0,8},{4,12},{8,0},{12,4},{1,9},{5,13},{9,1},{13,5},{2,10},{6,14},... | collective-permute-start | bytes 393224 | tf_op jit(solution)/shard_map/ppermute | solution.py:218
  50.1 1.5 collective-permute-start.16
  51.6 1.0 broadcast_select_fusion.refs_0_
  52.7 1.6 collective-permute-start.8
  54.8 3.4 %collective-permute-start.11 = (bf16[384,512]{1,0:T(8,128)(2,1)S(1)}, bf16[384,512]{1,0:T(8,128)(2,1)}, u32[]{:S(2)}, u32[]{:S(2)}) collective-permute-start(bf16[384,512]{1,0:T(8,128)(2,1)S(1)} %collective-permute-done.10.refs_2_.refs_0_), channel_id=1, source_target_pairs={{0,2},{2,0},{12,14},{14,12},{1,3},{3,1},{13,15},{15,13},{16,18},{1... | collective-permute-start | bytes 1179656 | tf_op jit(solution)/shard_map/ppermute | solution.py:226
  58.3 0.8 constant_dynamic-slice_fusion
  59.2 1.2 collective-permute-start.17
  61.1 0.7 select_reduce_fusion
  61.8 0.8 broadcast_in_dim.47.refs_13_.slot
  63.4 7.3 %shard_map.118 = (f32[384,512]{1,0:T(8,128)}, f32[384,512]{1,0:T(8,128)}) custom-call(s32[18]{0:T(128)} %stack.84.places, bf16[384,512]{1,0:T(8,128)(2,1)} %refs_0_.3, bf16[384,512]{1,0:T(8,128)(2,1)} %copy-done.7, bf16[384,512]{1,0:T(8,128)(2,1)} %copy-done.5, bf16[384,512]{1,0:T(8,128)(2,1)} %copy-done.8, bf16[384,512]{1,0:T(8,128)(2,1)} %copy-done.6, ...), custom_call_target="tpu_custom_call" | custom-call | flops 1 | bytes 1 | tf_op jit(solution)/shard_map/pallas_call | solution.py:97
  70.7 3.9 %shard_map.120.refs_12_ = f32[384,128]{1,0:T(8,128)} custom-call(s32[18]{0:T(128)} %stack.84.places, bf16[384,512]{1,0:T(8,128)(2,1)} %refs_0_.3, bf16[384,512]{1,0:T(8,128)(2,1)} %copy-done.7, bf16[384,512]{1,0:T(8,128)(2,1)} %copy-done.5, bf16[384,512]{1,0:T(8,128)(2,1)} %copy-done.8, bf16[384,512]{1,0:T(8,128)(2,1)} %copy-done.6, ...), custom_call_target="tpu_custom_call" | custom-call | flops 1 | bytes 1 | tf_op jit(solution)/shard_map/pallas_call | solution.py:59
  74.6 4.7 %shard_map.119 = (f32[384,512]{1,0:T(8,128)}, f32[384,512]{1,0:T(8,128)}) custom-call(s32[18]{0:T(128)} %stack.84.places, bf16[384,512]{1,0:T(8,128)(2,1)} %copy-done.1, bf16[384,512]{1,0:T(8,128)(2,1)} %collective-permute-done.8.refs_1_, bf16[8192,512]{1,0:T(8,128)(2,1)} %refs_3_.4, bf16[8192,512]{1,0:T(8,128)(2,1)} %refs_3_.4, ...), custom_call_target="tpu_custom_call" | custom-call | flops 1 | bytes 1 | tf_op jit(solution)/shard_map/pallas_call | solution.py:97
  79.3 3.8 %shard_map.121 = f32[192,128]{1,0:T(8,128)} custom-call(s32[18]{0:T(128)} %stack.84.places, bf16[384,512]{1,0:T(8,128)(2,1)} %copy-done.1, bf16[384,512]{1,0:T(8,128)(2,1)} %collective-permute-done.8.refs_1_, bf16[384,512]{1,0:T(8,128)(2,1)} %copy-done.4, bf16[384,512]{1,0:T(8,128)(2,1)} %collective-permute-done.11.refs_3_.refs_1_, ...), custom_call_target="tpu_custom_call" | custom-call | flops 1 | bytes 1 | tf_op jit(solution)/shard_map/pallas_call | solution.py:59
  83.1 1.0 fusion.14
  84.7 0.9 add_convert_fusion.4
  85.6 0.9 collective-permute-start.13
  86.5 3.3 %collective-permute-done.13 = bf16[192,128]{1,0:T(8,128)(2,1)S(1)} collective-permute-done((bf16[192,128]{1,0:T(8,128)(2,1)S(1)}, bf16[192,128]{1,0:T(8,128)(2,1)S(1)}, u32[]{:S(2)}, u32[]{:S(2)}) %collective-permute-start.13) | collective-permute-done | bytes 49184 | tf_op jit(solution)/shard_map/ppermute | solution.py:218
  89.9 4.8 %shard_map.122 = (f32[384,512]{1,0:T(8,128)}, f32[384,512]{1,0:T(8,128)}) custom-call(s32[18]{0:T(128)} %stack.84.places, bf16[384,512]{1,0:T(8,128)(2,1)} %copy-done.4, bf16[384,512]{1,0:T(8,128)(2,1)} %collective-permute-done.11.refs_3_.refs_1_, bf16[8192,512]{1,0:T(8,128)(2,1)} %refs_3_.4, bf16[8192,512]{1,0:T(8,128)(2,1)} %refs_3_.4, ...), custom_call_target="tpu_custom_call" | custom-call | flops 1 | bytes 1 | tf_op jit(solution)/shard_map/pallas_call | solution.py:97
  94.7 2.5 %collective-permute-done.19.received = f32[384,512]{1,0:T(8,128)S(1)} collective-permute-done((f32[384,512]{1,0:T(8,128)}, f32[384,512]{1,0:T(8,128)S(1)}, u32[]{:S(2)}, u32[]{:S(2)}) %collective-permute-start.19) | collective-permute-done | bytes 786464 | tf_op jit(solution)/shard_map/ppermute | solution.py:218
  97.4 1.5 collective-permute-start.23
  98.9 2.0 collective-permute-start.20
  101.2 2.0 collective-permute-start.22
  103.8 1.2 collective-permute-done.20
  105.0 1.6 collective-permute-done.21
  107.2 4.3 %collective-permute-done.23.up_other = bf16[512,512]{1,0:T(8,128)(2,1)S(1)} collective-permute-done((bf16[512,512]{1,0:T(8,128)(2,1)S(1)}, bf16[512,512]{1,0:T(8,128)(2,1)S(1)}, u32[]{:S(2)}, u32[]{:S(2)}) %collective-permute-start.23) | collective-permute-done | bytes 524320 | tf_op jit(solution)/shard_map/ppermute | solution.py:341
  111.6 0.8 copy-done.12
  112.4 3.6 %shard_map.123 = bf16[384,512]{1,0:T(8,128)(2,1)} custom-call(s32[1]{0:T(128)} %bitcast.16.half, f32[384,512]{1,0:T(8,128)} %get-tuple-element.55.own, f32[384,512]{1,0:T(8,128)} %copy-done.11, bf16[192,128]{1,0:T(8,128)(2,1)} %add_add_fusion.low, s32[384,1]{1,0:T(8,128)} %broadcast_in_dim.47.refs_13_.slot, s32[1,512]{1,0:T(1,128)} %fusion.18.owners, ...), custom_call_target="tpu_custom_call" | custom-call | flops 1 | bytes 1 | tf_op jit(solution)/shard_map/pallas_call | solution.py:138
  115.9 3.6 %all-to-all-start = ((bf16[16,24,512]{2,1,0:T(8,128)(2,1)}), bf16[16,24,512]{2,1,0:T(8,128)(2,1)S(1)}, u32[]{:S(2)}, u32[]{:S(2)}) async-start(bf16[16,24,512]{2,1,0:T(8,128)(2,1)} %bitcast.63), calls=%async_computation | async-start | bytes 786432 | tf_op jit(solution)/shard_map/all_to_all | solution.py:367
  119.7 12.0 %all-to-all-done = bf16[16,24,512]{2,1,0:T(8,128)(2,1)S(1)} async-done(((bf16[16,24,512]{2,1,0:T(8,128)(2,1)}), bf16[16,24,512]{2,1,0:T(8,128)(2,1)S(1)}, u32[]{:S(2)}, u32[]{:S(2)}) %all-to-all-start) | async-done | bytes 393248 | tf_op jit(solution)/shard_map/all_to_all | solution.py:367
  132.4 5.5 %fusion.24 = (f32[8,24,8]{2,1,0:T(8,128)S(1)}, f32[8,24,8,128]{3,2,1,0:T(8,128)S(1)}) fusion(bf16[8,24,128,128]{3,2,1,0:T(8,128)(2,1)} %param.19, bf16[24,8,8,128]{3,2,1,0:T(8,128)(2,1)S(1)} %reshape.295, pred[24,128]{1,0:T(8,128)(4,1)S(1)} %iota_compare_fusion.1), kind=kOutput, calls=%fused_computation.68 | convolution fusion | flops 50723328 | bytes 7480320 | tf_op jit(solution)/shard_map/rkge,krje->krgj/dot_general | solution.py:202
  138.5 4.6 %fusion.5 = bf16[24,8,8,128]{3,2,1,0:T(8,128)(2,1)S(1)} fusion(bf16[8,24,128,128]{3,2,1,0:T(8,128)(2,1)} %param.20, f32[24,8,128]{2,1,0:T(8,128)S(1)} %bitcast.72, f32[24,8,8]{2,1,0:T(8,128)S(1)} %copy.39, f32[8,24,8,128]{3,2,1,0:T(8,128)S(1)} %get-tuple-element.80, f32[8,24,8]{2,1,0:T(8,128)S(1)} %get-tuple-element.78, f32[8,24,8]{2,1,0:T(8,128)S(1)} %max.3, ...), kind=kOutput, calls=%fused_computation.4 | convolution fusion | flops 51707904 | bytes 7590912 | tf_op jit(solution)/shard_map/krgj,krje->rkge/dot_general | solution.py:211
  143.6 15.5 %all_to_all.21 = bf16[16,24,512]{2,1,0:T(8,128)(2,1)S(1)} all-to-all(bf16[16,24,512]{2,1,0:T(8,128)(2,1)S(1)} %bitcast.65), channel_id=1, replica_groups=mesh['rep'=2,'z'=4,'y'=2,'core'=2] {'z','y','core'}, dimensions={0} | all-to-all | bytes 786432 | tf_op jit(solution)/shard_map/all_to_all | solution.py:373
  159.2 1.6 collective-permute-done.24.refs_1_
  160.8 0.8 copy-done.9
  161.6 3.4 %shard_map.125 = bf16[384,512]{1,0:T(8,128)(2,1)} custom-call(s32[18]{0:T(128)} %stack.84.places, bf16[384,512]{1,0:T(8,128)(2,1)} %bitcast.59, bf16[384,512]{1,0:T(8,128)(2,1)} %copy-done.9, bf16[512,8192]{1,0:T(8,128)(2,1)} %refs_2_.7, bf16[512,8192]{1,0:T(8,128)(2,1)} %collective-permute-done.25.refs_9_.refs_10_.refs_11_.refs_12_.refs_13_.refs_14_.refs_15_.refs_3_), custom_call_target="tpu_custom_call" | custom-call | flops 1 | bytes 1 | tf_op jit(solution)/shard_map/pallas_call | solution.py:180
  165.6 7.3 %shard_map.124 = (bf16[384,512]{1,0:T(8,128)(2,1)}, bf16[384,512]{1,0:T(8,128)(2,1)}, bf16[384,512]{1,0:T(8,128)(2,1)}, bf16[384,512]{1,0:T(8,128)(2,1)}, bf16[3...) custom-call(s32[18]{0:T(128)} %stack.84.places, bf16[384,512]{1,0:T(8,128)(2,1)} %bitcast.60, ...), custom_call_target="tpu_custom_call" | custom-call | flops 1 | bytes 1 | tf_op jit(solution)/shard_map/pallas_call | solution.py:180
  173.0 1.5 collective-permute-start.27
  174.5 2.3 %collective-permute-done.28 = bf16[384,512]{1,0:T(8,128)(2,1)S(1)} collective-permute-done((bf16[384,512]{1,0:T(8,128)(2,1)}, bf16[384,512]{1,0:T(8,128)(2,1)S(1)}, u32[]{:S(2)}, u32[]{:S(2)}) %collective-permute-start.28) | collective-permute-done | bytes 393248 | tf_op jit(solution)/shard_map/ppermute | solution.py:218
  176.8 1.1 add_convert_fusion.3
  177.9 3.1 %collective-permute-start.29 = (bf16[384,512]{1,0:T(8,128)(2,1)S(1)}, bf16[384,512]{1,0:T(8,128)(2,1)S(1)}, u32[]{:S(2)}, u32[]{:S(2)}) collective-permute-start(bf16[384,512]{1,0:T(8,128)(2,1)S(1)} %add_convert_fusion.3), channel_id=1, source_target_pairs={{0,4},{4,8},{1,5},{5,9},{2,6},{6,10},{3,7},{7,11},{16,20},{20,24},... | collective-permute-start | bytes 1179656 | tf_op jit(solution)/shard_map/ppermute | solution.py:295
  182.2 1.6 collective-permute-start.26
  183.8 1.4 collective-permute-done.27
  185.2 3.4 %collective-permute-done.29 = bf16[384,512]{1,0:T(8,128)(2,1)S(1)} collective-permute-done((bf16[384,512]{1,0:T(8,128)(2,1)S(1)}, bf16[384,512]{1,0:T(8,128)(2,1)S(1)}, u32[]{:S(2)}, u32[]{:S(2)}) %collective-permute-start.29) | collective-permute-done | bytes 393248 | tf_op jit(solution)/shard_map/ppermute | solution.py:295
  188.6 1.1 add_convert_fusion.2
  189.8 2.5 %collective-permute-start.30 = (bf16[384,512]{1,0:T(8,128)(2,1)S(1)}, bf16[384,512]{1,0:T(8,128)(2,1)S(1)}, u32[]{:S(2)}, u32[]{:S(2)}) collective-permute-start(bf16[384,512]{1,0:T(8,128)(2,1)S(1)} %add_convert_fusion.2), channel_id=1, source_target_pairs={{0,4},{4,8},{8,12},{12,0},{1,5},{5,9},{9,13},{13,1},{2,6},{6,10},{... | collective-permute-start | bytes 1179656 | tf_op jit(solution)/shard_map/ppermute | solution.py:218
  192.3 1.4 collective-permute-done.31
  193.6 1.1 add_convert_fusion.1
  194.8 2.2 %collective-permute-start.33 = (bf16[384,512]{1,0:T(8,128)(2,1)S(1)}, bf16[384,512]{1,0:T(8,128)(2,1)S(1)}, u32[]{:S(2)}, u32[]{:S(2)}) collective-permute-start(bf16[384,512]{1,0:T(8,128)(2,1)S(1)} %add_convert_fusion.1), channel_id=1, source_target_pairs={{0,12},{4,0},{8,4},{12,8},{1,13},{5,1},{9,5},{13,9},{2,14},{6,2},{... | collective-permute-start | bytes 1179656 | tf_op jit(solution)/shard_map/ppermute | solution.py:218
  197.0 4.7 %collective-permute-done.26 = bf16[384,512]{1,0:T(8,128)(2,1)S(1)} collective-permute-done((bf16[384,512]{1,0:T(8,128)(2,1)}, bf16[384,512]{1,0:T(8,128)(2,1)S(1)}, u32[]{:S(2)}, u32[]{:S(2)}) %collective-permute-start.26) | collective-permute-done | bytes 393248 | tf_op jit(solution)/shard_map/ppermute | solution.py:218
  201.7 2.0 collective-permute-done.30
  203.7 5.8 %collective-permute-done.33 = bf16[384,512]{1,0:T(8,128)(2,1)S(1)} collective-permute-done((bf16[384,512]{1,0:T(8,128)(2,1)S(1)}, bf16[384,512]{1,0:T(8,128)(2,1)S(1)}, u32[]{:S(2)}, u32[]{:S(2)}) %collective-permute-start.33) | collective-permute-done | bytes 393248 | tf_op jit(solution)/shard_map/ppermute | solution.py:218
  209.5 1.9 add_convert_fusion
  (84 shorter events, 10.2 us)
Async XLA Ops:
  0.0 33.2 %collective-permute-start.6 = (bf16[8192,512]{1,0:T(8,128)(2,1)}, bf16[8192,512]{1,0:T(8,128)(2,1)}, u32[]{:S(2)}, u32[]{:S(2)}) collective-permute-start(bf16[8192,512]{1,0:T(8,128)(2,1)} %refs_3_.4), channel_id=1, source_target_pairs={{0,1},{1,0},{2,3},{3,2},{4,5},{5,4},{6,7},{7,6},{8,9},{9,8},{10,11... | collective-permute-start | bytes 25165832 | tf_op jit(solution)/shard_map/ppermute | solution.py:218
  0.5 17.9 %collective-permute-start.3 = (bf16[1,64,8192]{2,1,0:T(8,128)(2,1)}, bf16[1,64,8192]{2,1,0:T(8,128)(2,1)S(1)}, u32[]{:S(2)}, u32[]{:S(2)}) collective-permute-start(bf16[1,64,8192]{2,1,0:T(8,128)(2,1)} %bitcast.47), channel_id=1, source_target_pairs={{0,1},{1,0},{2,3},{3,2},{4,5},{5,4},{6,7},{7,6},{8,9},{9,8},{10,11... | collective-permute-start | bytes 3145736 | tf_op jit(solution)/shard_map/ppermute | solution.py:218
  0.5 13.8 %collective-permute-start = (bf16[384,512]{1,0:T(8,128)(2,1)}, bf16[384,512]{1,0:T(8,128)(2,1)S(1)}, u32[]{:S(2)}, u32[]{:S(2)}) collective-permute-start(bf16[384,512]{1,0:T(8,128)(2,1)} %refs_0_.3), channel_id=1, source_target_pairs={{0,4},{4,8},{8,12},{1,5},{5,9},{9,13},{2,6},{6,10},{10,14},{3,7},{... | collective-permute-start | bytes 1179656 | tf_op jit(solution)/shard_map/ppermute | solution.py:239
  5.5 12.8 %collective-permute-start.1 = (bf16[384,512]{1,0:T(8,128)(2,1)}, bf16[384,512]{1,0:T(8,128)(2,1)S(1)}, u32[]{:S(2)}, u32[]{:S(2)}) collective-permute-start(bf16[384,512]{1,0:T(8,128)(2,1)} %refs_0_.3), channel_id=1, source_target_pairs={{4,0},{8,4},{12,8},{5,1},{9,5},{13,9},{6,2},{10,6},{14,10},{7,3},{... | collective-permute-start | bytes 1179656 | tf_op jit(solution)/shard_map/ppermute | solution.py:240
  6.8 11.6 %collective-permute-start.2 = (bf16[384,512]{1,0:T(8,128)(2,1)}, bf16[384,512]{1,0:T(8,128)(2,1)S(1)}, u32[]{:S(2)}, u32[]{:S(2)}) collective-permute-start(bf16[384,512]{1,0:T(8,128)(2,1)} %refs_0_.3), channel_id=1, source_target_pairs={{0,2},{2,0},{4,6},{6,4},{8,10},{10,8},{12,14},{14,12},{1,3},{3,1},... | collective-permute-start | bytes 1179656 | tf_op jit(solution)/shard_map/ppermute | solution.py:226
  14.3 49.1 %copy-start.5 = (bf16[384,512]{1,0:T(8,128)(2,1)}, bf16[384,512]{1,0:T(8,128)(2,1)S(1)}, u32[]{:S(2)}) copy-start(bf16[384,512]{1,0:T(8,128)(2,1)S(1)} %collective-permute-done.refs_2_) | copy-start | bytes 1179652
  18.3 45.0 %copy-start.6 = (bf16[384,512]{1,0:T(8,128)(2,1)}, bf16[384,512]{1,0:T(8,128)(2,1)S(1)}, u32[]{:S(2)}) copy-start(bf16[384,512]{1,0:T(8,128)(2,1)S(1)} %collective-permute-done.1.refs_4_) | copy-start | bytes 1179652
  18.3 45.0 %copy-start.7 = (bf16[384,512]{1,0:T(8,128)(2,1)}, bf16[384,512]{1,0:T(8,128)(2,1)S(1)}, u32[]{:S(2)}) copy-start(bf16[384,512]{1,0:T(8,128)(2,1)S(1)} %collective-permute-done.2.refs_1_) | copy-start | bytes 1179652
  18.3 52.3 %copy-start = (bf16[1,64,8192]{2,1,0:T(8,128)(2,1)}, bf16[1,64,8192]{2,1,0:T(8,128)(2,1)S(1)}, u32[]{:S(2)}) copy-start(bf16[1,64,8192]{2,1,0:T(8,128)(2,1)S(1)} %collective-permute-done.3.refs_12_.refs_13_.refs_14_.refs_15_.refs_16_.refs_17_.refs_8_.refs_9_.refs_10_.refs_11_) | copy-start | bytes 3145732
  18.3 2.7 %collective-permute-start.4 = (bf16[384,512]{1,0:T(8,128)(2,1)S(1)}, bf16[384,512]{1,0:T(8,128)(2,1)S(1)}, u32[]{:S(2)}, u32[]{:S(2)}) collective-permute-start(bf16[384,512]{1,0:T(8,128)(2,1)S(1)} %collective-permute-done.refs_2_), channel_id=1, source_target_pairs={{4,8},{8,12},{5,9},{9,13},{6,10},{10,14},{7,11},{11,15},{20,24},{2... | collective-permute-start | bytes 1179656 | tf_op jit(solution)/shard_map/ppermute | solution.py:242
  19.0 14.1 %collective-permute-start.5 = (bf16[384,512]{1,0:T(8,128)(2,1)S(1)}, bf16[384,512]{1,0:T(8,128)(2,1)S(1)}, u32[]{:S(2)}, u32[]{:S(2)}) collective-permute-start(bf16[384,512]{1,0:T(8,128)(2,1)S(1)} %collective-permute-done.1.refs_4_), channel_id=1, source_target_pairs={{8,4},{4,0},{9,5},{5,1},{10,6},{6,2},{11,7},{7,3},{24,20},{20,16},... | collective-permute-start | bytes 1179656 | tf_op jit(solution)/shard_map/ppermute | solution.py:243
  20.3 12.8 %collective-permute-start.7 = (bf16[384,512]{1,0:T(8,128)(2,1)S(1)}, bf16[384,512]{1,0:T(8,128)(2,1)S(1)}, u32[]{:S(2)}, u32[]{:S(2)}) collective-permute-start(bf16[384,512]{1,0:T(8,128)(2,1)S(1)} %collective-permute-done.refs_2_), channel_id=1, source_target_pairs={{4,6},{6,4},{8,10},{10,8},{12,14},{14,12},{5,7},{7,5},{9,11},{11,9... | collective-permute-start | bytes 1179656 | tf_op jit(solution)/shard_map/ppermute | solution.py:226
  21.0 12.1 %copy-start.13 = (bf16[384,512]{1,0:T(8,128)(2,1)}, bf16[384,512]{1,0:T(8,128)(2,1)S(1)}, u32[]{:S(2)}) copy-start(bf16[384,512]{1,0:T(8,128)(2,1)S(1)} %collective-permute-done.4) | copy-start | bytes 1179652
  33.1 0.7 copy-start.14
  33.1 30.2 %copy-start.8 = (bf16[384,512]{1,0:T(8,128)(2,1)}, bf16[384,512]{1,0:T(8,128)(2,1)S(1)}, u32[]{:S(2)}) copy-start(bf16[384,512]{1,0:T(8,128)(2,1)S(1)} %collective-permute-done.7.refs_3_) | copy-start | bytes 1179652
  33.9 12.6 %collective-permute-start.10 = (bf16[384,512]{1,0:T(8,128)(2,1)}, bf16[384,512]{1,0:T(8,128)(2,1)S(1)}, u32[]{:S(2)}, u32[]{:S(2)}) collective-permute-start(bf16[384,512]{1,0:T(8,128)(2,1)} %refs_0_.3), channel_id=1, source_target_pairs={{0,12},{12,0},{1,13},{13,1},{2,14},{14,2},{3,15},{15,3},{16,28},{2... | collective-permute-start | bytes 1179656 | tf_op jit(solution)/shard_map/ppermute | solution.py:249
  37.6 25.7 %collective-permute-start.9 = (bf16[384,512]{1,0:T(8,128)(2,1)S(1)}, bf16[384,512]{1,0:T(8,128)(2,1)}, u32[]{:S(2)}, u32[]{:S(2)}) collective-permute-start(bf16[384,512]{1,0:T(8,128)(2,1)S(1)} %collective-permute-done.1.refs_4_), channel_id=1, source_target_pairs={{0,2},{2,0},{4,6},{6,4},{8,10},{10,8},{1,3},{3,1},{5,7},{7,5},{9,1... | collective-permute-start | bytes 1179656 | tf_op jit(solution)/shard_map/ppermute | solution.py:226
  46.5 24.2 %copy-start.4 = (bf16[384,512]{1,0:T(8,128)(2,1)}, bf16[384,512]{1,0:T(8,128)(2,1)S(1)}, u32[]{:S(2)}) copy-start(bf16[384,512]{1,0:T(8,128)(2,1)S(1)} %collective-permute-done.10.refs_2_.refs_0_) | copy-start | bytes 1179652
  47.7 7.1 %collective-permute-start.14 = (bf16[32,2048]{1,0:T(8,128)(2,1)S(1)}, bf16[32,2048]{1,0:T(8,128)(2,1)S(1)}, u32[]{:S(2)}, u32[]{:S(2)}) collective-permute-start(bf16[32,2048]{1,0:T(8,128)(2,1)S(1)} %get-tuple-element.72), channel_id=1, source_target_pairs={{0,4},{4,8},{8,12},{12,0},{1,5},{5,9},{9,13},{13,1},{2,6},{6,10},{... | collective-permute-start | bytes 393224 | tf_op jit(solution)/shard_map/ppermute | solution.py:218
  47.8 10.4 %collective-permute-start.15 = (bf16[32,2048]{1,0:T(8,128)(2,1)S(1)}, bf16[32,2048]{1,0:T(8,128)(2,1)S(1)}, u32[]{:S(2)}, u32[]{:S(2)}) collective-permute-start(bf16[32,2048]{1,0:T(8,128)(2,1)S(1)} %get-tuple-element.71), channel_id=1, source_target_pairs={{0,8},{4,12},{8,0},{12,4},{1,9},{5,13},{9,1},{13,5},{2,10},{6,14},... | collective-permute-start | bytes 393224 | tf_op jit(solution)/shard_map/ppermute | solution.py:218
  50.1 8.1 %collective-permute-start.16 = (bf16[32,2048]{1,0:T(8,128)(2,1)S(1)}, bf16[32,2048]{1,0:T(8,128)(2,1)S(1)}, u32[]{:S(2)}, u32[]{:S(2)}) collective-permute-start(bf16[32,2048]{1,0:T(8,128)(2,1)S(1)} %get-tuple-element.70), channel_id=1, source_target_pairs={{0,12},{4,0},{8,4},{12,8},{1,13},{5,1},{9,5},{13,9},{2,14},{6,2},{... | collective-permute-start | bytes 393224 | tf_op jit(solution)/shard_map/ppermute | solution.py:218
  52.7 18.0 %copy-start.1 = (bf16[384,512]{1,0:T(8,128)(2,1)}, bf16[384,512]{1,0:T(8,128)(2,1)S(1)}, u32[]{:S(2)}) copy-start(bf16[384,512]{1,0:T(8,128)(2,1)S(1)} %broadcast_select_fusion.refs_0_) | copy-start | bytes 1179652
  52.7 21.9 %collective-permute-start.8 = (bf16[384,512]{1,0:T(8,128)(2,1)S(1)}, bf16[384,512]{1,0:T(8,128)(2,1)}, u32[]{:S(2)}, u32[]{:S(2)}) collective-permute-start(bf16[384,512]{1,0:T(8,128)(2,1)S(1)} %broadcast_select_fusion.refs_0_), channel_id=1, source_target_pairs={{0,2},{2,0},{4,6},{6,4},{8,10},{10,8},{12,14},{14,12},{1,3},{3,1},... | collective-permute-start | bytes 1179656 | tf_op jit(solution)/shard_map/ppermute | solution.py:226
  54.8 24.5 %collective-permute-start.11 = (bf16[384,512]{1,0:T(8,128)(2,1)S(1)}, bf16[384,512]{1,0:T(8,128)(2,1)}, u32[]{:S(2)}, u32[]{:S(2)}) collective-permute-start(bf16[384,512]{1,0:T(8,128)(2,1)S(1)} %collective-permute-done.10.refs_2_.refs_0_), channel_id=1, source_target_pairs={{0,2},{2,0},{12,14},{14,12},{1,3},{3,1},{13,15},{15,13},{16,18},{1... | collective-permute-start | bytes 1179656 | tf_op jit(solution)/shard_map/ppermute | solution.py:226
  59.2 23.9 %collective-permute-start.17 = (bf16[4,32,1024]{2,1,0:T(8,128)(2,1)}, bf16[4,32,1024]{2,1,0:T(8,128)(2,1)}, u32[]{:S(2)}, u32[]{:S(2)}) collective-permute-start(bf16[4,32,1024]{2,1,0:T(8,128)(2,1)} %get-tuple-element.75), channel_id=1, source_target_pairs={{0,2},{2,0},{1,3},{3,1},{4,6},{6,4},{5,7},{7,5},{8,10},{10,8},{9,1... | collective-permute-start | bytes 786440 | tf_op jit(solution)/shard_map/ppermute | solution.py:218
  79.3 3.8 %copy-start.10 = (bf16[4,32,1024]{2,1,0:T(8,128)(2,1)S(1)}, bf16[4,32,1024]{2,1,0:T(8,128)(2,1)}, u32[]{:S(2)}) copy-start(bf16[4,32,1024]{2,1,0:T(8,128)(2,1)} %get-tuple-element.76) | copy-start | bytes 786436
  83.1 1.6 collective-permute-start.12
  84.1 5.6 %collective-permute-start.18 = (bf16[8,32,512]{2,1,0:T(8,128)(2,1)S(1)}, bf16[8,32,512]{2,1,0:T(8,128)(2,1)S(1)}, u32[]{:S(2)}, u32[]{:S(2)}) collective-permute-start(bf16[8,32,512]{2,1,0:T(8,128)(2,1)S(1)} %get-tuple-element.74), channel_id=1, source_target_pairs={{0,1},{1,0},{2,3},{3,2},{4,5},{5,4},{6,7},{7,6},{8,9},{9,8},{10,11... | collective-permute-start | bytes 786440 | tf_op jit(solution)/shard_map/ppermute | solution.py:218
  85.6 4.2 %collective-permute-start.13 = (bf16[192,128]{1,0:T(8,128)(2,1)S(1)}, bf16[192,128]{1,0:T(8,128)(2,1)S(1)}, u32[]{:S(2)}, u32[]{:S(2)}) collective-permute-start(bf16[192,128]{1,0:T(8,128)(2,1)S(1)} %add_convert_fusion.4), channel_id=1, source_target_pairs={{0,2},{2,0},{1,3},{3,1},{4,6},{6,4},{5,7},{7,5},{8,10},{10,8},{9,1... | collective-permute-start | bytes 147464 | tf_op jit(solution)/shard_map/ppermute | solution.py:218
  89.9 7.5 %copy-start.3 = (bf16[16,32,512]{2,1,0:T(8,128)(2,1)}, bf16[16,32,512]{2,1,0:T(8,128)(2,1)S(1)}, u32[]{:S(2)}) copy-start(bf16[16,32,512]{2,1,0:T(8,128)(2,1)S(1)} %pad_maximum_fusion.1) | copy-start | bytes 1572868
  89.9 29.6 %copy-start.15 = (bf16[24,1024]{1,0:T(8,128)(2,1)S(1)}, bf16[24,1024]{1,0:T(8,128)(2,1)}, u32[]{:S(2)}) copy-start(bf16[24,1024]{1,0:T(8,128)(2,1)} %param.21) | copy-start | bytes 147460
  89.9 29.6 %copy-start.16 = (bf16[24,1024]{1,0:T(8,128)(2,1)S(1)}, bf16[24,1024]{1,0:T(8,128)(2,1)}, u32[]{:S(2)}) copy-start(bf16[24,1024]{1,0:T(8,128)(2,1)} %param.22) | copy-start | bytes 147460
  89.9 29.7 %copy-start.17 = (s32[24]{0:T(128)S(1)}, s32[24]{0:T(128)}, u32[]{:S(2)}) copy-start(s32[24]{0:T(128)} %param.15) | copy-start | bytes 292
  94.7 2.5 %collective-permute-start.19 = (f32[384,512]{1,0:T(8,128)}, f32[384,512]{1,0:T(8,128)S(1)}, u32[]{:S(2)}, u32[]{:S(2)}) collective-permute-start(f32[384,512]{1,0:T(8,128)} %get-tuple-element.56), channel_id=1, source_target_pairs={{0,1},{1,0},{2,3},{3,2},{4,5},{5,4},{6,7},{7,6},{8,9},{9,8},{10,11... | collective-permute-start | bytes 2359304 | tf_op jit(solution)/shard_map/ppermute | solution.py:218
  97.2 14.3 %copy-start.11 = (f32[384,512]{1,0:T(8,128)}, f32[384,512]{1,0:T(8,128)S(1)}, u32[]{:S(2)}) copy-start(f32[384,512]{1,0:T(8,128)S(1)} %collective-permute-done.19.received) | copy-start | bytes 2359300
  97.2 63.6 %collective-permute-start.25 = (bf16[512,8192]{1,0:T(8,128)(2,1)}, bf16[512,8192]{1,0:T(8,128)(2,1)}, u32[]{:S(2)}, u32[]{:S(2)}) collective-permute-start(bf16[512,8192]{1,0:T(8,128)(2,1)} %refs_2_.7), channel_id=1, source_target_pairs={{0,1},{1,0},{2,3},{3,2},{4,5},{5,4},{6,7},{7,6},{8,9},{9,8},{10,11... | collective-permute-start | bytes 25165832 | tf_op jit(solution)/shard_map/ppermute | solution.py:218
  97.4 14.2 %collective-permute-start.23 = (bf16[512,512]{1,0:T(8,128)(2,1)S(1)}, bf16[512,512]{1,0:T(8,128)(2,1)S(1)}, u32[]{:S(2)}, u32[]{:S(2)}) collective-permute-start(bf16[512,512]{1,0:T(8,128)(2,1)S(1)} %bitcast.61), channel_id=1, source_target_pairs={{0,16},{16,0},{1,17},{17,1},{2,18},{18,2},{3,19},{19,3},{4,20},{20... | collective-permute-start | bytes 1572872 | tf_op jit(solution)/shard_map/ppermute | solution.py:341
  98.9 6.2 %collective-permute-start.20 = (bf16[192,128]{1,0:T(8,128)(2,1)S(1)}, bf16[192,128]{1,0:T(8,128)(2,1)S(1)}, u32[]{:S(2)}, u32[]{:S(2)}) collective-permute-start(bf16[192,128]{1,0:T(8,128)(2,1)S(1)} %add.438), channel_id=1, source_target_pairs={{0,4},{4,8},{8,12},{12,0},{1,5},{5,9},{9,13},{13,1},{2,6},{6,10},{... | collective-permute-start | bytes 147464 | tf_op jit(solution)/shard_map/ppermute | solution.py:218
  100.8 5.8 %collective-permute-start.21 = (bf16[192,128]{1,0:T(8,128)(2,1)S(1)}, bf16[192,128]{1,0:T(8,128)(2,1)S(1)}, u32[]{:S(2)}, u32[]{:S(2)}) collective-permute-start(bf16[192,128]{1,0:T(8,128)(2,1)S(1)} %add.438), channel_id=1, source_target_pairs={{0,8},{4,12},{8,0},{12,4},{1,9},{5,13},{9,1},{13,5},{2,10},{6,14},... | collective-permute-start | bytes 147464 | tf_op jit(solution)/shard_map/ppermute | solution.py:218
  101.2 5.4 %collective-permute-start.22 = (bf16[192,128]{1,0:T(8,128)(2,1)S(1)}, bf16[192,128]{1,0:T(8,128)(2,1)S(1)}, u32[]{:S(2)}, u32[]{:S(2)}) collective-permute-start(bf16[192,128]{1,0:T(8,128)(2,1)S(1)} %add.438), channel_id=1, source_target_pairs={{0,12},{4,0},{8,4},{12,8},{1,13},{5,1},{9,5},{13,9},{2,14},{6,2},{... | collective-permute-start | bytes 147464 | tf_op jit(solution)/shard_map/ppermute | solution.py:218
  111.6 0.8 copy-start.12
  115.9 15.7 %all-to-all-start = ((bf16[16,24,512]{2,1,0:T(8,128)(2,1)}), bf16[16,24,512]{2,1,0:T(8,128)(2,1)S(1)}, u32[]{:S(2)}, u32[]{:S(2)}) async-start(bf16[16,24,512]{2,1,0:T(8,128)(2,1)} %bitcast.63), calls=%async_computation | async-start | bytes 786432 | tf_op jit(solution)/shard_map/all_to_all | solution.py:367
  159.1 1.7 copy-start.2
  159.1 1.7 collective-permute-start.24
  160.8 0.8 copy-start.9
  165.0 11.8 %collective-permute-start.28 = (bf16[384,512]{1,0:T(8,128)(2,1)}, bf16[384,512]{1,0:T(8,128)(2,1)S(1)}, u32[]{:S(2)}, u32[]{:S(2)}) collective-permute-start(bf16[384,512]{1,0:T(8,128)(2,1)} %shard_map.125), channel_id=1, source_target_pairs={{0,2},{2,0},{1,3},{3,1},{4,6},{6,4},{5,7},{7,5},{8,10},{10,8},{9,1... | collective-permute-start | bytes 1179656 | tf_op jit(solution)/shard_map/ppermute | solution.py:218
  173.0 12.2 %collective-permute-start.27 = (bf16[384,512]{1,0:T(8,128)(2,1)}, bf16[384,512]{1,0:T(8,128)(2,1)S(1)}, u32[]{:S(2)}, u32[]{:S(2)}) collective-permute-start(bf16[384,512]{1,0:T(8,128)(2,1)} %get-tuple-element.63), channel_id=1, source_target_pairs={{0,2},{2,0},{1,3},{3,1},{4,6},{6,4},{5,7},{7,5},{8,10},{10,8},{9,1... | collective-permute-start | bytes 1179656 | tf_op jit(solution)/shard_map/ppermute | solution.py:218
  177.9 10.7 %collective-permute-start.29 = (bf16[384,512]{1,0:T(8,128)(2,1)S(1)}, bf16[384,512]{1,0:T(8,128)(2,1)S(1)}, u32[]{:S(2)}, u32[]{:S(2)}) collective-permute-start(bf16[384,512]{1,0:T(8,128)(2,1)S(1)} %add_convert_fusion.3), channel_id=1, source_target_pairs={{0,4},{4,8},{1,5},{5,9},{2,6},{6,10},{3,7},{7,11},{16,20},{20,24},... | collective-permute-start | bytes 1179656 | tf_op jit(solution)/shard_map/ppermute | solution.py:295
  181.0 12.7 %collective-permute-start.31 = (bf16[384,512]{1,0:T(8,128)(2,1)}, bf16[384,512]{1,0:T(8,128)(2,1)S(1)}, u32[]{:S(2)}, u32[]{:S(2)}) collective-permute-start(bf16[384,512]{1,0:T(8,128)(2,1)} %get-tuple-element.68), channel_id=1, source_target_pairs={{0,2},{2,0},{1,3},{3,1},{4,6},{6,4},{5,7},{7,5},{8,10},{10,8},{9,1... | collective-permute-start | bytes 1179656 | tf_op jit(solution)/shard_map/ppermute | solution.py:218
  181.5 12.2 %collective-permute-start.32 = (bf16[384,512]{1,0:T(8,128)(2,1)S(1)}, bf16[384,512]{1,0:T(8,128)(2,1)S(1)}, u32[]{:S(2)}, u32[]{:S(2)}) collective-permute-start(bf16[384,512]{1,0:T(8,128)(2,1)S(1)} %add_convert_fusion.3), channel_id=1, source_target_pairs={{12,8},{8,4},{13,9},{9,5},{14,10},{10,6},{15,11},{11,7},{28,24},{2... | collective-permute-start | bytes 1179656 | tf_op jit(solution)/shard_map/ppermute | solution.py:296
  182.2 19.5 %collective-permute-start.26 = (bf16[384,512]{1,0:T(8,128)(2,1)}, bf16[384,512]{1,0:T(8,128)(2,1)S(1)}, u32[]{:S(2)}, u32[]{:S(2)}) collective-permute-start(bf16[384,512]{1,0:T(8,128)(2,1)} %get-tuple-element.60), channel_id=1, source_target_pairs={{0,2},{2,0},{1,3},{3,1},{4,6},{6,4},{5,7},{7,5},{8,10},{10,8},{9,1... | collective-permute-start | bytes 1179656 | tf_op jit(solution)/shard_map/ppermute | solution.py:218
  189.8 13.9 %collective-permute-start.30 = (bf16[384,512]{1,0:T(8,128)(2,1)S(1)}, bf16[384,512]{1,0:T(8,128)(2,1)S(1)}, u32[]{:S(2)}, u32[]{:S(2)}) collective-permute-start(bf16[384,512]{1,0:T(8,128)(2,1)S(1)} %add_convert_fusion.2), channel_id=1, source_target_pairs={{0,4},{4,8},{8,12},{12,0},{1,5},{5,9},{9,13},{13,1},{2,6},{6,10},{... | collective-permute-start | bytes 1179656 | tf_op jit(solution)/shard_map/ppermute | solution.py:218
  194.8 14.7 %collective-permute-start.33 = (bf16[384,512]{1,0:T(8,128)(2,1)S(1)}, bf16[384,512]{1,0:T(8,128)(2,1)S(1)}, u32[]{:S(2)}, u32[]{:S(2)}) collective-permute-start(bf16[384,512]{1,0:T(8,128)(2,1)S(1)} %add_convert_fusion.1), channel_id=1, source_target_pairs={{0,12},{4,0},{8,4},{12,8},{1,13},{5,1},{9,5},{13,9},{2,14},{6,2},{... | collective-permute-start | bytes 1179656 | tf_op jit(solution)/shard_map/ppermute | solution.py:218

commit v5 on v3

--- a/solution.py
+++ b/solution.py
@@ -11,14 +11,14 @@
 ADP = ("z", "y", "core")
 NT = (((1,), (1,)), ((), ()))
 VMEM_LIMIT = 56 << 20
-
-
-def project_kernel(places, *refs):
-    count = places.shape[0]
+QUICK = pl.CostEstimate(flops=1, bytes_accessed=1, transcendentals=0)
+
+
+def project_kernel(places, first, count, *refs):
     blocks, w_own, w_other, a_own, a_other = (refs[i * count : (i + 1) * count] for i in range(5))
     ins, outs = refs[5 * count : -3], refs[-3:]
     first_core = places[0] % 2 == 0
-    sums = [ref[...] for ref in ins]
+    sums = [ref[...] for ref in ins[:3]]
     for i in range(count):
         x = blocks[i][...]
         own, other = a_own[i][0], a_other[i][0]
@@ -31,36 +31,49 @@
             lax.dot_general(x, pair, NT, preferred_element_type=jnp.float32),
         )
         sums = [total + part for total, part in zip(sums, parts)] if sums else parts
-    for out, total in zip(outs, sums):
-        out[...] = total
-
-
-def project(places, blocks, weight, weight_other, down, down_other, sums):
+    outs[0][...], outs[1][...] = sums[:2]
+    low = sums[2]
+    if ins:
+        slot = ins[3][...]
+        rank = low.shape[1] // 2
+        mine = places[0] - places[0] % 2
+        low = jnp.where(slot == mine, low[:, :rank], 0.0) + jnp.where(
+            slot == mine + 1, low[:, rank:], 0.0
+        )
+        half = low.shape[0] // 2
+        low = jnp.concatenate([low[:half], low[half:]], axis=1)
+    outs[2][...] = low
+
+
+def project(places, first, blocks, weight, weight_other, down, down_other, rest):
     count = len(blocks)
     rows, width = blocks[0].shape
     cols, rank = weight.shape[1], down.shape[1]
     flat = lambda shape: pl.BlockSpec(shape, lambda j, p: (0, 0))
-    shapes = [(rows, cols), (rows, cols), (rows, 2 * rank)]
-    weights = [pl.BlockSpec((width, cols), lambda j, p, i=i: (p[i], 0)) for i in range(count)]
-    maps = [pl.BlockSpec((1, rank, width), lambda j, p, i=i: (0, 0, p[i])) for i in range(count)]
+    low_rows = rows // 2 if rest else rows
+    shapes = [(rows, cols), (rows, cols), (low_rows, 2 * rank)]
+    weights = [pl.BlockSpec((width, cols), lambda j, p, i=i: (p[first + i], 0)) for i in range(count)]
+    maps = [
+        pl.BlockSpec((1, rank, width), lambda j, p, i=i: (0, 0, p[first + i])) for i in range(count)
+    ]
+
+    def kernel(places, *refs):
+        project_kernel(places, first, count, *refs)
+
     return pl.pallas_call(
-        project_kernel,
+        kernel,
         grid_spec=pltpu.PrefetchScalarGridSpec(
             num_scalar_prefetch=1,
             grid=(1,),
             in_specs=[flat((rows, width))] * count
             + weights * 2
             + maps * 2
-            + [flat(shape) for shape in shapes[: len(sums)]],
+            + [flat(array.shape) for array in rest],
             out_specs=[flat(shape) for shape in shapes],
         ),
         out_shape=[jax.ShapeDtypeStruct(shape, jnp.float32) for shape in shapes],
         compiler_params=pltpu.CompilerParams(vmem_limit_bytes=VMEM_LIMIT),
-        cost_estimate=pl.CostEstimate(
-            flops=4 * count * rows * width * (cols + rank),
-            bytes_accessed=2 * count * width * (rows + 2 * cols) + 8 * rows * cols,
-            transcendentals=0,
-        ),
+        cost_estimate=QUICK,
     )(
         places,
         *blocks,
@@ -68,13 +81,13 @@
         *[weight_other] * count,
         *[down] * count,
         *[down_other] * count,
-        *sums,
+        *rest,
     )
 
 
 def query_kernel(half, own, received, low, slot, up_own, up_other, out):
     step = pl.program_id(0)
-    cols, lanes = own.shape[1], low.shape[1]
+    lanes = low.shape[1]
     rank = lanes // 2
     part = rank // 2
     depth = up_own.shape[0]
@@ -83,7 +96,7 @@
     row = lax.broadcasted_iota(jnp.int32, shape, 0)
     owner = lax.broadcasted_iota(jnp.int32, (own.shape[0], depth), 1) // part
     live = slot[...] == owner
-    total = own[...] + received[:, :cols]
+    total = own[...] + received[...]
     for h, up in ((half[0], up_own), (1 - half[0], up_other)):
         copies = (row == lane + rank * step + part * h).astype(jnp.bfloat16)
         spread = jnp.dot(low[...], copies, preferred_element_type=jnp.float32)
@@ -115,34 +128,32 @@
         ),
         out_shape=jax.ShapeDtypeStruct((rows, cols), jnp.bfloat16),
         compiler_params=pltpu.CompilerParams(vmem_limit_bytes=VMEM_LIMIT),
-        cost_estimate=pl.CostEstimate(
-            flops=4 * rows * cols * depth,
-            bytes_accessed=rows * cols * 10 + 4 * depth * cols,
-            transcendentals=0,
-        ),
+        cost_estimate=QUICK,
     )(half, own, received, low, slot, up_own, up_other)
 
 
-def output_kernel(places, own, other, *refs):
-    count = places.shape[0]
+def output_kernel(places, count, own, other, *refs):
     for w_own, w_other, out in zip(refs[:count], refs[count : 2 * count], refs[2 * count :]):
         total = jnp.dot(own[...], w_own[...], preferred_element_type=jnp.float32)
         total += jnp.dot(other[...], w_other[...], preferred_element_type=jnp.float32)
         out[...] = total.astype(out.dtype)
 
 
-def output_partial(chips, core, own, other, weight, weight_other, width):
+def output_partial(places, first, count, own, other, weight, weight_other, width):
     rows, depth = own.shape
-    count = len(chips)
     tile = width // 2 if width % 256 == 0 else width
     steps = width // tile
-    places = jnp.stack([2 * chip + core for chip in chips]).astype(jnp.int32)
     whole = pl.BlockSpec((rows, depth), lambda j, p: (0, 0))
     weights = [
-        pl.BlockSpec((depth, tile), lambda j, p, i=i: (0, p[i] * steps + j)) for i in range(count)
+        pl.BlockSpec((depth, tile), lambda j, p, i=i: (0, p[first + i] * steps + j))
+        for i in range(count)
     ]
+
+    def kernel(places, *refs):
+        output_kernel(places, count, *refs)
+
     return pl.pallas_call(
-        output_kernel,
+        kernel,
         grid_spec=pltpu.PrefetchScalarGridSpec(
             num_scalar_prefetch=1,
             grid=(steps,),
@@ -151,11 +162,7 @@
         ),
         out_shape=[jax.ShapeDtypeStruct((rows, width), jnp.bfloat16)] * count,
         compiler_params=pltpu.CompilerParams(vmem_limit_bytes=VMEM_LIMIT),
-        cost_estimate=pl.CostEstimate(
-            flops=4 * count * rows * width * depth,
-            bytes_accessed=2 * count * width * (rows + 2 * depth) + 4 * rows * depth,
-            transcendentals=0,
-        ),
+        cost_estimate=QUICK,
     )(places, own, other, *[weight] * count, *[weight_other] * count)
 
 
@@ -190,7 +197,7 @@
     return lax.optimization_barrier((value, *others))[0]
 
 
-def gather_features(tokens):
+def gather_features(tokens, down_other, up):
     layers, sides = lax.axis_size("z"), lax.axis_size("y")
     z = lax.axis_index("z")
     if layers != 4 or sides != 2:
@@ -198,22 +205,23 @@
         for k in range(layers):
             block = shift(tokens, "z", k) if k else tokens
             entries.append(((z - k) % layers, [block, shift(block, "y", 1)][:sides]))
-        return entries
+        return entries, down_other
     side = shift(tokens, "y", 1)
     below, above = shift(tokens, "z", 1), shift(tokens, "z", 3)
+    below, side, down_other = lax.optimization_barrier((below, side, down_other))
+    below_side = shift(below, "y", 1)
     from_below = lax.ppermute(below, "z", [(1, 2), (2, 3)])
+    above_side = shift(above, "y", 1)
     from_above = lax.ppermute(above, "z", [(2, 1), (1, 0)])
-    below_side = shift(after(below, side), "y", 1)
-    above_side = shift(after(above, side), "y", 1)
     two = jnp.where(z >= 2, from_below, from_above)
-    two = after(two, below_side, above_side)
+    two = after(two, below_side, up)
     two_side = shift(two, "y", 1)
     return [
         (z, [tokens, side]),
         ((z - 1) % 4, [below, below_side]),
         ((z + 1) % 4, [above, above_side]),
         ((z + 2) % 4, [two, two_side]),
-    ]
+    ], down_other
 
 
 def scatter_layers(parts):
@@ -257,7 +265,6 @@
     down = jnp.swapaxes(adapter_down_maps, 1, 2)
     down_other = shift(down, "core", 1)
     query_weight_other = shift(query_weight, "core", 1)
-    output_weight_other = shift(output_weight, "core", 1)
 
     ids = request_adapter[:, 0]
     numbers = jnp.arange(total_adapters, dtype=jnp.int32)
@@ -265,40 +272,32 @@
         jnp.where(ids[:, None] == numbers[None, :], adapter_storage_slot[None, :], 0), axis=1
     )[:, None]
 
-    entries = gather_features(tokens)
-
-    sums = []
-    for group in (entries[:-1], entries[-1:]):
-        chips = [chip for layer, _ in group for chip in chips_of(layer)]
-        places = jnp.stack([2 * chip + core for chip in chips]).astype(jnp.int32)
-        blocks = [block for _, pair in group for block in pair]
-        sums = project(
-            places, blocks, query_weight, query_weight_other, down, down_other, sums
-        )
-        first_sums = sums if len(group) > 1 else first_sums
-
-    reps = lax.axis_size("rep")
     half = lax.axis_index("rep") % 2
     up = jnp.swapaxes(adapter_up_maps, 1, 2)[0]
     up = lax.dynamic_slice_in_dim(up, half * (rank // 2), rank // 2, 0)
-    up = after(up, first_sums[2])
     up = lax.all_to_all(up, ADP, split_axis=1, concat_axis=0, tiled=True)
-    up_other = lax.ppermute(up, "rep", [(i, i ^ 1) for i in range(reps)])
-
-    own, sent, low = sums
-    low_other = shift(low, "core", 1)
+    up_other = lax.ppermute(up, "rep", [(i, i ^ 1) for i in range(lax.axis_size("rep"))])
+
+    entries, down_other = gather_features(tokens, down_other, up)
+    out_order = [2, 1, 3, 0] if layers == 4 else list(range(1, layers)) + [0]
+    out_keys = [(k, side) for k in out_order for side in reversed(range(sides))]
+    chips = [chip for layer, _ in entries for chip in chips_of(layer)]
+    chips += [chips_of(z + k)[side] for k, side in out_keys]
+    places = jnp.stack([2 * chip + core for chip in chips]).astype(jnp.int32)
+    out_first = len(chips) - len(out_keys)
+
+    blocks = [block for _, pair in entries for block in pair]
+    last = len(blocks) - sides
+    weights = query_weight, query_weight_other, down, down_other
+    sums = project(places, 0, blocks[:last], *weights, ())
+    own, sent, low = project(places, last, blocks[last:], *weights, (*sums, slot))
+
+    low = (low + shift(low, "core", 1)).astype(jnp.bfloat16)
     received = shift(sent, "core", 1)
-
-    low = low + low_other
-    chip = z * sides + y
-    low = jnp.where(slot == 2 * chip, low[:, :rank], 0.0) + jnp.where(
-        slot == 2 * chip + 1, low[:, rank:], 0.0
-    )
-    low = low.astype(jnp.bfloat16)
-    low = jnp.concatenate([low[: rows // 2], low[rows // 2 :]], axis=1)
     if sides == 2:
         low = low + shift(low, "y", 1)
     low = sum([shift(low, "z", k) for k in range(1, layers)], low)
+    output_weight_other = shift(after(output_weight, low), "core", 1)
 
     query = make_query(half.astype(jnp.int32).reshape(1), own, received, low, slot, up, up_other)
     query_local = lax.all_to_all(query, ADP, split_axis=0, concat_axis=1, tiled=True)
@@ -311,24 +310,23 @@
     context = context.reshape(rows, depth)
     context_other = shift(context, "core", 1)
 
-    order = [2, 1, 3, 0] if layers == 4 else list(range(1, layers)) + [0]
-    keys = [(k, side) for k in order for side in reversed(range(sides))]
     made = {}
-    for group in (keys[:1], keys[1:]):
+    for first, count in ((0, 1), (1, len(out_keys) - 1)):
         outs = output_partial(
-            [chips_of(z + k)[side] for k, side in group],
-            core,
+            places,
+            out_first + first,
+            count,
             context,
             context_other,
             output_weight,
             output_weight_other,
             width,
         )
-        made.update(zip(group, outs))
-    other_side = {k: shift(made[k, 1], "y", 1) for k in order if sides == 2}
+        made.update(zip(out_keys[first : first + count], outs))
+    other_side = {k: shift(made[k, 1], "y", 1) for k in out_order if sides == 2}
     parts = [None] * layers
-    for k in order:
-        parts[k] = after(made[k, 0], made[keys[-1]]).astype(jnp.float32)
+    for k in out_order:
+        parts[k] = after(made[k, 0], made[out_keys[-1]]).astype(jnp.float32)
         if sides == 2:
             parts[k] = parts[k] + other_side[k].astype(jnp.float32)
     return scatter_layers(parts).astype(jnp.bfloat16)

time: 197 us -> 196 us (level)
  waiting for transfers between devices: 77.5 us -> 82.4 us
  starting transfers between devices: 46.5 us -> 41.9 us
    ppermute x1, waiting for transfers between devices: 1.57 us -> 12.2 us  [shards(): lax.ppermute(up, 'rep', [(i, i ^ 1) for i in range(lax.axis_size('rep'))])]
    all_to_all x1, starting transfers between devices: 8.96 us -> 3.57 us  [shards(): up = lax.all_to_all(up, ADP, split_axis=1, concat_axis=0, tiled=True)]
    ppermute x22, waiting for transfers between devices: 48.9 us -> 44.3 us  [shift(): lax.ppermute(value, axis, [(i, (i + by) % size) for i in range(size)])]
    all_to_all x1, waiting for transfers between devices: 3.55 us -> 0.01 us  [shards(): up = lax.all_to_all(up, ADP, split_axis=1, concat_axis=0, tiled=True)]
  transfers between devices with their start and end apart: 29 -> 29, of which waited for: 19 -> 17; matrix products, arithmetic and copies ran while one was open for 12% -> 11% of each run, Pallas kernels for 13% -> 10%
where the time goes in v5:
time: 196 us; the launch traced here: 195 us
  waiting for transfers between devices  82.4 us (42%)
  starting transfers between devices  41.9 us (21%)
  Pallas kernels  28.6 us (15%)
  blocking collectives  15.5 us (8%)
  matrix products  10.4 us (5%)
  other arithmetic  10 us (5%)
  local copies, waits for them, and re-layouts  6.23 us (3%)
    ppermute x22, waiting for transfers between devices, shift(): lax.ppermute(value, axis, [(i, (i + by) % size) for i in range(size)])  44.3 us
    ppermute x22, starting transfers between devices, shift(): lax.ppermute(value, axis, [(i, (i + by) % size) for i in range(size)])  24.8 us
    all_to_all x1, blocking collectives, shards(): lax.all_to_all(context, ADP, split_axis=0, concat_axis=0, tiled=True)  15.5 us
    pallas_call x2, Pallas kernels, project(): pl.pallas_call(kernel, grid_spec=pltpu.PrefetchScalarGridSpec(num_scalar_...  14.1 us
    ppermute x1, waiting for transfers between devices, shards(): lax.ppermute(up, 'rep', [(i, i ^ 1) for i in range(lax.axis_size('rep'))])  12.2 us
    all_to_all x1, waiting for transfers between devices, shards(): lax.all_to_all(query, ADP, split_axis=0, concat_axis=1, tiled=True)  12 us
    pallas_call x2, Pallas kernels, output_partial(): pl.pallas_call(kernel, grid_spec=pltpu.PrefetchScalarGridSpec(num_scalar_...  10.9 us
    ppermute x1, waiting for transfers between devices, gather_features(): from_above = lax.ppermute(above, 'z', [(2, 1), (1, 0)])  10.5 us
  transfers between devices with their start and end apart: 29, of which 17 were waited for; matrix products, arithmetic and copies ran while one was open for 11% of the time, Pallas kernels for 10%

profile of v5, /device:TPU:0, one launch (start us, length us, event | category | flops | bytes accessed | tf_op | source)
XLA Modules:
  0.0 195.5 jit_solution(9382911196374865327)
XLA Ops:
  0.0 0.5 collective-permute-start.8
  0.5 2.6 %collective-permute-start = (bf16[384,512]{1,0:T(8,128)(2,1)}, bf16[384,512]{1,0:T(8,128)(2,1)S(1)}, u32[]{:S(2)}, u32[]{:S(2)}) collective-permute-start(bf16[384,512]{1,0:T(8,128)(2,1)} %refs_0_.1), channel_id=1, source_target_pairs={{0,4},{4,8},{8,12},{12,0},{1,5},{5,9},{9,13},{13,1},{2,6},{6,10},{... | collective-permute-start | bytes 1179656 | tf_op jit(solution)/shard_map/ppermute | solution.py:193
  3.1 1.5 collective-permute-start.1
  4.6 2.2 %collective-permute-start.4 = (bf16[384,512]{1,0:T(8,128)(2,1)}, bf16[384,512]{1,0:T(8,128)(2,1)S(1)}, u32[]{:S(2)}, u32[]{:S(2)}) collective-permute-start(bf16[384,512]{1,0:T(8,128)(2,1)} %refs_0_.1), channel_id=1, source_target_pairs={{0,12},{4,0},{8,4},{12,8},{1,13},{5,1},{9,5},{13,9},{2,14},{6,2},{... | collective-permute-start | bytes 1179656 | tf_op jit(solution)/shard_map/ppermute | solution.py:193
  7.1 1.1 copy.36
  8.1 3.6 %all-to-all-start = ((bf16[32,16,512]{2,0,1:T(8,128)(2,1)}), bf16[32,16,512]{2,0,1:T(8,128)(2,1)S(1)}, u32[]{:S(2)}, u32[]{:S(2)}) async-start(bf16[32,16,512]{2,0,1:T(8,128)(2,1)} %copy.36), calls=%async_computation | async-start | bytes 1048576 | tf_op jit(solution)/shard_map/all_to_all | solution.py:278
  11.7 13.2 %collective-permute-done.4.refs_4_ = bf16[384,512]{1,0:T(8,128)(2,1)S(1)} collective-permute-done((bf16[384,512]{1,0:T(8,128)(2,1)}, bf16[384,512]{1,0:T(8,128)(2,1)S(1)}, u32[]{:S(2)}, u32[]{:S(2)}) %collective-permute-start.4) | collective-permute-done | bytes 393248 | tf_op jit(solution)/shard_map/ppermute | solution.py:193
  25.0 1.3 collective-permute-start.5
  26.3 1.4 collective-permute-start.3
  27.8 0.7 collective-permute-start.6
  28.5 1.3 collective-permute-start.9
  29.8 10.5 %collective-permute-done.5 = bf16[384,512]{1,0:T(8,128)(2,1)S(1)} collective-permute-done((bf16[384,512]{1,0:T(8,128)(2,1)S(1)}, bf16[384,512]{1,0:T(8,128)(2,1)S(1)}, u32[]{:S(2)}, u32[]{:S(2)}) %collective-permute-start.5) | collective-permute-done | bytes 393248 | tf_op jit(solution)/shard_map/ppermute | solution.py:215
  40.3 0.7 copy-done.12
  41.1 1.0 broadcast_select_fusion.refs_0_
  42.2 1.2 collective-permute-start.7
  43.4 0.7 reduce
  44.1 0.7 select_reduce_fusion
  44.9 0.8 broadcast_in_dim.46.refs_13_.slot
  45.7 0.6 stack.61.places
  46.3 3.4 %collective-permute-done.9.refs_5_ = bf16[384,512]{1,0:T(8,128)(2,1)} collective-permute-done((bf16[384,512]{1,0:T(8,128)(2,1)S(1)}, bf16[384,512]{1,0:T(8,128)(2,1)}, u32[]{:S(2)}, u32[]{:S(2)}) %collective-permute-start.9) | collective-permute-done | bytes 393248 | tf_op jit(solution)/shard_map/ppermute | solution.py:193
  49.8 8.7 %shard_map.118 = (f32[384,512]{1,0:T(8,128)}, f32[384,512]{1,0:T(8,128)}, f32[384,128]{1,0:T(8,128)}) custom-call(s32[16]{0:T(128)} %stack.61.places, bf16[384,512]{1,0:T(8,128)(2,1)} %refs_0_.1, bf16[384,512]{1,0:T(8,128)(2,1)} %copy-done.10, bf16[384,512]{1,0:T(8,128)(2,1)} %copy-done.9, bf16[384,512]{1,0:T(8,128)(2,1)} %collective-permute-done.6.refs_3_, ...), custom_call_target="tpu_custom_call" | custom-call | flops 1 | bytes 1 | tf_op jit(solution)/shard_map/pallas_call | solution.py:63
  58.5 5.4 %shard_map.119 = (f32[384,512]{1,0:T(8,128)}, f32[384,512]{1,0:T(8,128)}, f32[192,128]{1,0:T(8,128)}) custom-call(s32[16]{0:T(128)} %stack.61.places, bf16[384,512]{1,0:T(8,128)(2,1)} %copy-done.5, bf16[384,512]{1,0:T(8,128)(2,1)} %collective-permute-done.7.refs_1_, bf16[8192,512]{1,0:T(8,128)(2,1)} %refs_3_.2, bf16[8192,512]{1,0:T(8,128)(2,1)} %refs_3_.2, ...), custom_call_target="tpu_custom_call" | custom-call | flops 1 | bytes 1 | tf_op jit(solution)/shard_map/pallas_call | solution.py:63
  63.9 1.5 collective-permute-done.11
  65.4 0.9 add_convert_fusion.4
  66.4 4.1 %collective-permute-done.12 = bf16[192,128]{1,0:T(8,128)(2,1)S(1)} collective-permute-done((bf16[192,128]{1,0:T(8,128)(2,1)S(1)}, bf16[192,128]{1,0:T(8,128)(2,1)S(1)}, u32[]{:S(2)}, u32[]{:S(2)}) %collective-permute-start.12) | collective-permute-done | bytes 49184 | tf_op jit(solution)/shard_map/ppermute | solution.py:193
  70.5 2.5 %collective-permute-start.13 = (bf16[192,128]{1,0:T(8,128)(2,1)S(1)}, bf16[192,128]{1,0:T(8,128)(2,1)S(1)}, u32[]{:S(2)}, u32[]{:S(2)}) collective-permute-start(bf16[192,128]{1,0:T(8,128)(2,1)S(1)} %add.265), channel_id=1, source_target_pairs={{0,4},{4,8},{8,12},{12,0},{1,5},{5,9},{9,13},{13,1},{2,6},{6,10},{... | collective-permute-start | bytes 147464 | tf_op jit(solution)/shard_map/ppermute | solution.py:193
  73.1 2.4 %collective-permute-start.15 = (bf16[192,128]{1,0:T(8,128)(2,1)S(1)}, bf16[192,128]{1,0:T(8,128)(2,1)S(1)}, u32[]{:S(2)}, u32[]{:S(2)}) collective-permute-start(bf16[192,128]{1,0:T(8,128)(2,1)S(1)} %add.265), channel_id=1, source_target_pairs={{0,12},{4,0},{8,4},{12,8},{1,13},{5,1},{9,5},{13,9},{2,14},{6,2},{... | collective-permute-start | bytes 147464 | tf_op jit(solution)/shard_map/ppermute | solution.py:193
  75.5 1.0 collective-permute-done.13
  76.5 1.8 collective-permute-done.14
  78.2 0.6 add_add_fusion.low
  78.9 0.5 collective-permute-start.10
  79.4 1.6 collective-permute-start.16
  81.0 12.2 %collective-permute-done.16.up_other = bf16[512,512]{1,0:T(8,128)(2,1)S(1)} collective-permute-done((bf16[512,512]{1,0:T(8,128)(2,1)S(1)}, bf16[512,512]{1,0:T(8,128)(2,1)S(1)}, u32[]{:S(2)}, u32[]{:S(2)}) %collective-permute-start.16) | collective-permute-done | bytes 524320 | tf_op jit(solution)/shard_map/ppermute | solution.py:279
  93.2 0.8 copy-done.8
  94.3 3.6 %shard_map.120 = bf16[384,512]{1,0:T(8,128)(2,1)} custom-call(s32[1]{0:T(128)} %bitcast.14.half, f32[384,512]{1,0:T(8,128)} %get-tuple-element.34.own, f32[384,512]{1,0:T(8,128)} %copy-done.7, bf16[192,128]{1,0:T(8,128)(2,1)} %add_add_fusion.low, s32[384,1]{1,0:T(8,128)} %broadcast_in_dim.46.refs_13_.slot, bf16[512,512]{1,0:T(8,128)(2,1)} %bitcast.58, ...), custom_call_target="tpu_custom_call" | custom-call | flops 1 | bytes 1 | tf_op jit(solution)/shard_map/pallas_call | solution.py:114
  97.9 5.5 %all-to-all-start.1 = ((bf16[16,24,512]{2,1,0:T(8,128)(2,1)}), bf16[16,24,512]{2,1,0:T(8,128)(2,1)S(1)}, u32[]{:S(2)}, u32[]{:S(2)}) async-start(bf16[16,24,512]{2,1,0:T(8,128)(2,1)} %bitcast.61), calls=%async_computation.1 | async-start | bytes 786432 | tf_op jit(solution)/shard_map/all_to_all | solution.py:303
  103.6 12.0 %all-to-all-done.1 = bf16[16,24,512]{2,1,0:T(8,128)(2,1)S(1)} async-done(((bf16[16,24,512]{2,1,0:T(8,128)(2,1)}), bf16[16,24,512]{2,1,0:T(8,128)(2,1)S(1)}, u32[]{:S(2)}, u32[]{:S(2)}) %all-to-all-start.1) | async-done | bytes 393248 | tf_op jit(solution)/shard_map/all_to_all | solution.py:303
  116.3 5.5 %fusion.15 = (f32[8,24,8]{2,1,0:T(8,128)S(1)}, f32[8,24,8,128]{3,2,1,0:T(8,128)S(1)}) fusion(bf16[8,24,128,128]{3,2,1,0:T(8,128)(2,1)} %param.19, bf16[24,8,8,128]{3,2,1,0:T(8,128)(2,1)S(1)} %reshape.48, pred[24,128]{1,0:T(8,128)(4,1)S(1)} %iota_compare_fusion.1), kind=kOutput, calls=%fused_computation.30 | convolution fusion | flops 50723328 | bytes 7480320 | tf_op jit(solution)/shard_map/rkge,krje->krgj/dot_general | solution.py:177
  121.9 0.5 fusion.8
  122.5 4.6 %fusion.5 = bf16[24,8,8,128]{3,2,1,0:T(8,128)(2,1)S(1)} fusion(bf16[8,24,128,128]{3,2,1,0:T(8,128)(2,1)} %param.20, f32[24,8,128]{2,1,0:T(8,128)S(1)} %bitcast.64, f32[24,8,8]{2,1,0:T(8,128)S(1)} %copy.43, f32[8,24,8,128]{3,2,1,0:T(8,128)S(1)} %get-tuple-element.52, f32[8,24,8]{2,1,0:T(8,128)S(1)} %get-tuple-element.50, f32[8,24,8]{2,1,0:T(8,128)S(1)} %max.3, ...), kind=kOutput, calls=%fused_computation.4 | convolution fusion | flops 51707904 | bytes 7590912 | tf_op jit(solution)/shard_map/krgj,krje->rkge/dot_general | solution.py:186
  127.6 15.5 %all_to_all.40 = bf16[16,24,512]{2,1,0:T(8,128)(2,1)S(1)} all-to-all(bf16[16,24,512]{2,1,0:T(8,128)(2,1)S(1)} %bitcast.60), channel_id=1, replica_groups=mesh['rep'=2,'z'=4,'y'=2,'core'=2] {'z','y','core'}, dimensions={0} | all-to-all | bytes 786432 | tf_op jit(solution)/shard_map/all_to_all | solution.py:309
  143.2 1.6 collective-permute-done.17.refs_1_
  144.8 0.7 copy-done.6
  145.6 3.4 %shard_map.122 = bf16[384,512]{1,0:T(8,128)(2,1)} custom-call(s32[16]{0:T(128)} %stack.61.places, bf16[384,512]{1,0:T(8,128)(2,1)} %bitcast.53, bf16[384,512]{1,0:T(8,128)(2,1)} %copy-done.6, bf16[512,8192]{1,0:T(8,128)(2,1)} %refs_2_.5, bf16[512,8192]{1,0:T(8,128)(2,1)} %collective-permute-done.18.refs_9_.refs_10_.refs_11_.refs_12_.refs_13_.refs_14_.refs_15_.refs_3_), custom_call_target="tpu_custom_call" | custom-call | flops 1 | bytes 1 | tf_op jit(solution)/shard_map/pallas_call | solution.py:155
  149.0 0.6 collective-permute-start.21
  149.6 7.5 %shard_map.121 = (bf16[384,512]{1,0:T(8,128)(2,1)}, bf16[384,512]{1,0:T(8,128)(2,1)}, bf16[384,512]{1,0:T(8,128)(2,1)}, bf16[384,512]{1,0:T(8,128)(2,1)}, bf16[3...) custom-call(s32[16]{0:T(128)} %stack.61.places, bf16[384,512]{1,0:T(8,128)(2,1)} %bitcast.54, ...), custom_call_target="tpu_custom_call" | custom-call | flops 1 | bytes 1 | tf_op jit(solution)/shard_map/pallas_call | solution.py:155
  157.1 1.5 collective-permute-start.20
  158.6 2.0 %collective-permute-done.21 = bf16[384,512]{1,0:T(8,128)(2,1)S(1)} collective-permute-done((bf16[384,512]{1,0:T(8,128)(2,1)}, bf16[384,512]{1,0:T(8,128)(2,1)S(1)}, u32[]{:S(2)}, u32[]{:S(2)}) %collective-permute-start.21) | collective-permute-done | bytes 393248 | tf_op jit(solution)/shard_map/ppermute | solution.py:193
  160.6 1.1 add_convert_fusion.3
  161.7 3.1 %collective-permute-start.22 = (bf16[384,512]{1,0:T(8,128)(2,1)S(1)}, bf16[384,512]{1,0:T(8,128)(2,1)S(1)}, u32[]{:S(2)}, u32[]{:S(2)}) collective-permute-start(bf16[384,512]{1,0:T(8,128)(2,1)S(1)} %add_convert_fusion.3), channel_id=1, source_target_pairs={{0,4},{4,8},{1,5},{5,9},{2,6},{6,10},{3,7},{7,11},{16,20},{20,24},... | collective-permute-start | bytes 1179656 | tf_op jit(solution)/shard_map/ppermute | solution.py:234
  164.8 0.6 collective-permute-start.24
  165.4 0.7 collective-permute-start.25
  166.1 1.5 collective-permute-start.19
  167.6 1.7 collective-permute-done.20
  169.3 3.3 %collective-permute-done.22 = bf16[384,512]{1,0:T(8,128)(2,1)S(1)} collective-permute-done((bf16[384,512]{1,0:T(8,128)(2,1)S(1)}, bf16[384,512]{1,0:T(8,128)(2,1)S(1)}, u32[]{:S(2)}, u32[]{:S(2)}) %collective-permute-start.22) | collective-permute-done | bytes 393248 | tf_op jit(solution)/shard_map/ppermute | solution.py:234
  172.6 1.1 add_convert_fusion.2
  173.7 2.5 %collective-permute-start.23 = (bf16[384,512]{1,0:T(8,128)(2,1)S(1)}, bf16[384,512]{1,0:T(8,128)(2,1)S(1)}, u32[]{:S(2)}, u32[]{:S(2)}) collective-permute-start(bf16[384,512]{1,0:T(8,128)(2,1)S(1)} %add_convert_fusion.2), channel_id=1, source_target_pairs={{0,4},{4,8},{8,12},{12,0},{1,5},{5,9},{9,13},{13,1},{2,6},{6,10},{... | collective-permute-start | bytes 1179656 | tf_op jit(solution)/shard_map/ppermute | solution.py:193
  176.3 1.5 collective-permute-done.24
  177.8 1.1 add_convert_fusion.1
  178.9 2.2 %collective-permute-start.26 = (bf16[384,512]{1,0:T(8,128)(2,1)S(1)}, bf16[384,512]{1,0:T(8,128)(2,1)S(1)}, u32[]{:S(2)}, u32[]{:S(2)}) collective-permute-start(bf16[384,512]{1,0:T(8,128)(2,1)S(1)} %add_convert_fusion.1), channel_id=1, source_target_pairs={{0,12},{4,0},{8,4},{12,8},{1,13},{5,1},{9,5},{13,9},{2,14},{6,2},{... | collective-permute-start | bytes 1179656 | tf_op jit(solution)/shard_map/ppermute | solution.py:193
  181.1 4.6 %collective-permute-done.19 = bf16[384,512]{1,0:T(8,128)(2,1)S(1)} collective-permute-done((bf16[384,512]{1,0:T(8,128)(2,1)}, bf16[384,512]{1,0:T(8,128)(2,1)S(1)}, u32[]{:S(2)}, u32[]{:S(2)}) %collective-permute-start.19) | collective-permute-done | bytes 393248 | tf_op jit(solution)/shard_map/ppermute | solution.py:193
  185.7 2.0 %collective-permute-done.23 = bf16[384,512]{1,0:T(8,128)(2,1)S(1)} collective-permute-done((bf16[384,512]{1,0:T(8,128)(2,1)S(1)}, bf16[384,512]{1,0:T(8,128)(2,1)S(1)}, u32[]{:S(2)}, u32[]{:S(2)}) %collective-permute-start.23) | collective-permute-done | bytes 393248 | tf_op jit(solution)/shard_map/ppermute | solution.py:193
  187.7 5.9 %collective-permute-done.26 = bf16[384,512]{1,0:T(8,128)(2,1)S(1)} collective-permute-done((bf16[384,512]{1,0:T(8,128)(2,1)S(1)}, bf16[384,512]{1,0:T(8,128)(2,1)S(1)}, u32[]{:S(2)}, u32[]{:S(2)}) %collective-permute-start.26) | collective-permute-done | bytes 393248 | tf_op jit(solution)/shard_map/ppermute | solution.py:193
  193.5 1.9 add_convert_fusion
  (62 shorter events, 2.2 us)
Async XLA Ops:
  0.0 6.9 %copy-start = (bf16[1,8192,64]{1,2,0:T(8,128)(2,1)S(1)}, bf16[1,8192,64]{1,2,0:T(8,128)(2,1)}, u32[]{:S(2)}) copy-start(bf16[1,8192,64]{1,2,0:T(8,128)(2,1)} %param.18) | copy-start | bytes 3145732
  0.0 49.8 %collective-permute-start.8 = (bf16[8192,512]{1,0:T(8,128)(2,1)}, bf16[8192,512]{1,0:T(8,128)(2,1)}, u32[]{:S(2)}, u32[]{:S(2)}) collective-permute-start(bf16[8192,512]{1,0:T(8,128)(2,1)} %refs_3_.2), channel_id=1, source_target_pairs={{0,1},{1,0},{2,3},{3,2},{4,5},{5,4},{6,7},{7,6},{8,9},{9,8},{10,11... | collective-permute-start | bytes 25165832 | tf_op jit(solution)/shard_map/ppermute | solution.py:193
  0.5 25.8 %collective-permute-start = (bf16[384,512]{1,0:T(8,128)(2,1)}, bf16[384,512]{1,0:T(8,128)(2,1)S(1)}, u32[]{:S(2)}, u32[]{:S(2)}) collective-permute-start(bf16[384,512]{1,0:T(8,128)(2,1)} %refs_0_.1), channel_id=1, source_target_pairs={{0,4},{4,8},{8,12},{12,0},{1,5},{5,9},{9,13},{13,1},{2,6},{6,10},{... | collective-permute-start | bytes 1179656 | tf_op jit(solution)/shard_map/ppermute | solution.py:193
  3.1 23.2 %collective-permute-start.1 = (bf16[384,512]{1,0:T(8,128)(2,1)}, bf16[384,512]{1,0:T(8,128)(2,1)S(1)}, u32[]{:S(2)}, u32[]{:S(2)}) collective-permute-start(bf16[384,512]{1,0:T(8,128)(2,1)} %refs_0_.1), channel_id=1, source_target_pairs={{0,2},{2,0},{1,3},{3,1},{4,6},{6,4},{5,7},{7,5},{8,10},{10,8},{9,1... | collective-permute-start | bytes 1179656 | tf_op jit(solution)/shard_map/ppermute | solution.py:193
  4.6 20.4 %collective-permute-start.4 = (bf16[384,512]{1,0:T(8,128)(2,1)}, bf16[384,512]{1,0:T(8,128)(2,1)S(1)}, u32[]{:S(2)}, u32[]{:S(2)}) collective-permute-start(bf16[384,512]{1,0:T(8,128)(2,1)} %refs_0_.1), channel_id=1, source_target_pairs={{0,12},{4,0},{8,4},{12,8},{1,13},{5,1},{9,5},{13,9},{2,14},{6,2},{... | collective-permute-start | bytes 1179656 | tf_op jit(solution)/shard_map/ppermute | solution.py:193
  6.9 19.4 %collective-permute-start.2 = (bf16[1,64,8192]{2,1,0:T(8,128)(2,1)}, bf16[1,64,8192]{2,1,0:T(8,128)(2,1)S(1)}, u32[]{:S(2)}, u32[]{:S(2)}) collective-permute-start(bf16[1,64,8192]{2,1,0:T(8,128)(2,1)} %bitcast.43), channel_id=1, source_target_pairs={{0,1},{1,0},{2,3},{3,2},{4,5},{5,4},{6,7},{7,6},{8,9},{9,8},{10,11... | collective-permute-start | bytes 3145736 | tf_op jit(solution)/shard_map/ppermute | solution.py:193
  8.1 34.0 %all-to-all-start = ((bf16[32,16,512]{2,0,1:T(8,128)(2,1)}), bf16[32,16,512]{2,0,1:T(8,128)(2,1)S(1)}, u32[]{:S(2)}, u32[]{:S(2)}) async-start(bf16[32,16,512]{2,0,1:T(8,128)(2,1)} %copy.36), calls=%async_computation | async-start | bytes 1048576 | tf_op jit(solution)/shard_map/all_to_all | solution.py:278
  25.0 24.8 %copy-start.11 = (bf16[384,512]{1,0:T(8,128)(2,1)}, bf16[384,512]{1,0:T(8,128)(2,1)S(1)}, u32[]{:S(2)}) copy-start(bf16[384,512]{1,0:T(8,128)(2,1)S(1)} %collective-permute-done.4.refs_4_) | copy-start | bytes 1179652
  25.0 15.4 %collective-permute-start.5 = (bf16[384,512]{1,0:T(8,128)(2,1)S(1)}, bf16[384,512]{1,0:T(8,128)(2,1)S(1)}, u32[]{:S(2)}, u32[]{:S(2)}) collective-permute-start(bf16[384,512]{1,0:T(8,128)(2,1)S(1)} %collective-permute-done.4.refs_4_), channel_id=1, source_target_pairs={{8,4},{4,0},{9,5},{5,1},{10,6},{6,2},{11,7},{7,3},{24,20},{20,16},... | collective-permute-start | bytes 1179656 | tf_op jit(solution)/shard_map/ppermute | solution.py:215
  26.3 23.5 %copy-start.9 = (bf16[384,512]{1,0:T(8,128)(2,1)}, bf16[384,512]{1,0:T(8,128)(2,1)S(1)}, u32[]{:S(2)}) copy-start(bf16[384,512]{1,0:T(8,128)(2,1)S(1)} %collective-permute-done.refs_2_) | copy-start | bytes 1179652
  26.3 23.5 %copy-start.10 = (bf16[384,512]{1,0:T(8,128)(2,1)}, bf16[384,512]{1,0:T(8,128)(2,1)S(1)}, u32[]{:S(2)}) copy-start(bf16[384,512]{1,0:T(8,128)(2,1)S(1)} %collective-permute-done.1.refs_1_) | copy-start | bytes 1179652
  26.3 23.5 %copy-start.2 = (bf16[1,64,8192]{2,1,0:T(8,128)(2,1)}, bf16[1,64,8192]{2,1,0:T(8,128)(2,1)S(1)}, u32[]{:S(2)}) copy-start(bf16[1,64,8192]{2,1,0:T(8,128)(2,1)S(1)} %collective-permute-done.2.refs_24_.refs_25_.refs_26_.refs_27_.refs_28_.refs_29_.refs_8_.refs_9_) | copy-start | bytes 3145732
  26.3 14.8 %collective-permute-start.3 = (bf16[384,512]{1,0:T(8,128)(2,1)S(1)}, bf16[384,512]{1,0:T(8,128)(2,1)}, u32[]{:S(2)}, u32[]{:S(2)}) collective-permute-start(bf16[384,512]{1,0:T(8,128)(2,1)S(1)} %collective-permute-done.refs_2_), channel_id=1, source_target_pairs={{4,8},{8,12},{5,9},{9,13},{6,10},{10,14},{7,11},{11,15},{20,24},{2... | collective-permute-start | bytes 1179656 | tf_op jit(solution)/shard_map/ppermute | solution.py:213
  27.8 14.4 %collective-permute-start.6 = (bf16[384,512]{1,0:T(8,128)(2,1)S(1)}, bf16[384,512]{1,0:T(8,128)(2,1)}, u32[]{:S(2)}, u32[]{:S(2)}) collective-permute-start(bf16[384,512]{1,0:T(8,128)(2,1)S(1)} %collective-permute-done.refs_2_), channel_id=1, source_target_pairs={{0,2},{2,0},{1,3},{3,1},{4,6},{6,4},{5,7},{7,5},{8,10},{10,8},{9,1... | collective-permute-start | bytes 1179656 | tf_op jit(solution)/shard_map/ppermute | solution.py:193
  28.5 21.3 %collective-permute-start.9 = (bf16[384,512]{1,0:T(8,128)(2,1)S(1)}, bf16[384,512]{1,0:T(8,128)(2,1)}, u32[]{:S(2)}, u32[]{:S(2)}) collective-permute-start(bf16[384,512]{1,0:T(8,128)(2,1)S(1)} %collective-permute-done.4.refs_4_), channel_id=1, source_target_pairs={{0,2},{2,0},{1,3},{3,1},{4,6},{6,4},{5,7},{7,5},{8,10},{10,8},{9,1... | collective-permute-start | bytes 1179656 | tf_op jit(solution)/shard_map/ppermute | solution.py:193
  40.3 0.7 copy-start.12
  42.1 16.3 %copy-start.5 = (bf16[384,512]{1,0:T(8,128)(2,1)}, bf16[384,512]{1,0:T(8,128)(2,1)S(1)}, u32[]{:S(2)}) copy-start(bf16[384,512]{1,0:T(8,128)(2,1)S(1)} %broadcast_select_fusion.refs_0_) | copy-start | bytes 1179652
  42.1 37.2 %copy-start.4 = (bf16[32,16,512]{2,0,1:T(8,128)(2,1)}, bf16[32,16,512]{2,0,1:T(8,128)(2,1)S(1)}, u32[]{:S(2)}) copy-start(bf16[32,16,512]{2,0,1:T(8,128)(2,1)S(1)} %all-to-all-done) | copy-start | bytes 1572868
  42.2 16.3 %collective-permute-start.7 = (bf16[384,512]{1,0:T(8,128)(2,1)S(1)}, bf16[384,512]{1,0:T(8,128)(2,1)}, u32[]{:S(2)}, u32[]{:S(2)}) collective-permute-start(bf16[384,512]{1,0:T(8,128)(2,1)S(1)} %broadcast_select_fusion.refs_0_), channel_id=1, source_target_pairs={{0,2},{2,0},{1,3},{3,1},{4,6},{6,4},{5,7},{7,5},{8,10},{10,8},{9,1... | collective-permute-start | bytes 1179656 | tf_op jit(solution)/shard_map/ppermute | solution.py:193
  58.5 44.9 %copy-start.13 = (bf16[24,1024]{1,0:T(8,128)(2,1)S(1)}, bf16[24,1024]{1,0:T(8,128)(2,1)}, u32[]{:S(2)}) copy-start(bf16[24,1024]{1,0:T(8,128)(2,1)} %param.21) | copy-start | bytes 147460
  58.5 44.9 %copy-start.14 = (bf16[24,1024]{1,0:T(8,128)(2,1)S(1)}, bf16[24,1024]{1,0:T(8,128)(2,1)}, u32[]{:S(2)}) copy-start(bf16[24,1024]{1,0:T(8,128)(2,1)} %param.22) | copy-start | bytes 147460
  58.5 45.0 %copy-start.15 = (s32[24]{0:T(128)S(1)}, s32[24]{0:T(128)}, u32[]{:S(2)}) copy-start(s32[24]{0:T(128)} %param.15) | copy-start | bytes 292
  63.9 1.5 collective-permute-start.11
  66.3 4.2 %collective-permute-start.12 = (bf16[192,128]{1,0:T(8,128)(2,1)S(1)}, bf16[192,128]{1,0:T(8,128)(2,1)S(1)}, u32[]{:S(2)}, u32[]{:S(2)}) collective-permute-start(bf16[192,128]{1,0:T(8,128)(2,1)S(1)} %add_convert_fusion.4), channel_id=1, source_target_pairs={{0,2},{2,0},{1,3},{3,1},{4,6},{6,4},{5,7},{7,5},{8,10},{10,8},{9,1... | collective-permute-start | bytes 147464 | tf_op jit(solution)/shard_map/ppermute | solution.py:193
  70.5 5.9 %collective-permute-start.13 = (bf16[192,128]{1,0:T(8,128)(2,1)S(1)}, bf16[192,128]{1,0:T(8,128)(2,1)S(1)}, u32[]{:S(2)}, u32[]{:S(2)}) collective-permute-start(bf16[192,128]{1,0:T(8,128)(2,1)S(1)} %add.265), channel_id=1, source_target_pairs={{0,4},{4,8},{8,12},{12,0},{1,5},{5,9},{9,13},{13,1},{2,6},{6,10},{... | collective-permute-start | bytes 147464 | tf_op jit(solution)/shard_map/ppermute | solution.py:193
  73.1 5.2 %collective-permute-start.14 = (bf16[192,128]{1,0:T(8,128)(2,1)S(1)}, bf16[192,128]{1,0:T(8,128)(2,1)S(1)}, u32[]{:S(2)}, u32[]{:S(2)}) collective-permute-start(bf16[192,128]{1,0:T(8,128)(2,1)S(1)} %add.265), channel_id=1, source_target_pairs={{0,8},{4,12},{8,0},{12,4},{1,9},{5,13},{9,1},{13,5},{2,10},{6,14},... | collective-permute-start | bytes 147464 | tf_op jit(solution)/shard_map/ppermute | solution.py:193
  73.1 5.2 %collective-permute-start.15 = (bf16[192,128]{1,0:T(8,128)(2,1)S(1)}, bf16[192,128]{1,0:T(8,128)(2,1)S(1)}, u32[]{:S(2)}, u32[]{:S(2)}) collective-permute-start(bf16[192,128]{1,0:T(8,128)(2,1)S(1)} %add.265), channel_id=1, source_target_pairs={{0,12},{4,0},{8,4},{12,8},{1,13},{5,1},{9,5},{13,9},{2,14},{6,2},{... | collective-permute-start | bytes 147464 | tf_op jit(solution)/shard_map/ppermute | solution.py:193
  78.9 66.0 %collective-permute-start.18 = (bf16[512,8192]{1,0:T(8,128)(2,1)}, bf16[512,8192]{1,0:T(8,128)(2,1)}, u32[]{:S(2)}, u32[]{:S(2)}) collective-permute-start(bf16[512,8192]{1,0:T(8,128)(2,1)} %refs_2_.5), channel_id=1, source_target_pairs={{0,1},{1,0},{2,3},{3,2},{4,5},{5,4},{6,7},{7,6},{8,9},{9,8},{10,11... | collective-permute-start | bytes 25165832 | tf_op jit(solution)/shard_map/ppermute | solution.py:193
  78.9 14.3 %collective-permute-start.10 = (f32[384,512]{1,0:T(8,128)}, f32[384,512]{1,0:T(8,128)S(1)}, u32[]{:S(2)}, u32[]{:S(2)}) collective-permute-start(f32[384,512]{1,0:T(8,128)} %get-tuple-element.35), channel_id=1, source_target_pairs={{0,1},{1,0},{2,3},{3,2},{4,5},{5,4},{6,7},{7,6},{8,9},{9,8},{10,11... | collective-permute-start | bytes 2359304 | tf_op jit(solution)/shard_map/ppermute | solution.py:193
  79.4 13.8 %collective-permute-start.16 = (bf16[512,512]{1,0:T(8,128)(2,1)S(1)}, bf16[512,512]{1,0:T(8,128)(2,1)S(1)}, u32[]{:S(2)}, u32[]{:S(2)}) collective-permute-start(bf16[512,512]{1,0:T(8,128)(2,1)S(1)} %bitcast.57), channel_id=1, source_target_pairs={{0,16},{16,0},{1,17},{17,1},{2,18},{18,2},{3,19},{19,3},{4,20},{20... | collective-permute-start | bytes 1572872 | tf_op jit(solution)/shard_map/ppermute | solution.py:279
  93.2 0.8 copy-start.8
  93.2 1.1 copy-start.7
  97.9 17.7 %all-to-all-start.1 = ((bf16[16,24,512]{2,1,0:T(8,128)(2,1)}), bf16[16,24,512]{2,1,0:T(8,128)(2,1)S(1)}, u32[]{:S(2)}, u32[]{:S(2)}) async-start(bf16[16,24,512]{2,1,0:T(8,128)(2,1)} %bitcast.61), calls=%async_computation.1 | async-start | bytes 786432 | tf_op jit(solution)/shard_map/all_to_all | solution.py:303
  143.1 1.7 copy-start.3
  143.1 1.7 collective-permute-start.17
  144.8 0.8 copy-start.6
  149.0 11.6 %collective-permute-start.21 = (bf16[384,512]{1,0:T(8,128)(2,1)}, bf16[384,512]{1,0:T(8,128)(2,1)S(1)}, u32[]{:S(2)}, u32[]{:S(2)}) collective-permute-start(bf16[384,512]{1,0:T(8,128)(2,1)} %shard_map.122), channel_id=1, source_target_pairs={{0,2},{2,0},{1,3},{3,1},{4,6},{6,4},{5,7},{7,5},{8,10},{10,8},{9,1... | collective-permute-start | bytes 1179656 | tf_op jit(solution)/shard_map/ppermute | solution.py:193
  149.6 45.9 %copy-start.1 = (bf16[1,8192,64]{1,2,0:T(8,128)(2,1)S(1)}, bf16[1,8192,64]{1,2,0:T(8,128)(2,1)}, u32[]{:S(2)}) copy-start(bf16[1,8192,64]{1,2,0:T(8,128)(2,1)} %param.18) | copy-start | bytes 3145732
  157.1 12.2 %collective-permute-start.20 = (bf16[384,512]{1,0:T(8,128)(2,1)}, bf16[384,512]{1,0:T(8,128)(2,1)S(1)}, u32[]{:S(2)}, u32[]{:S(2)}) collective-permute-start(bf16[384,512]{1,0:T(8,128)(2,1)} %get-tuple-element.43), channel_id=1, source_target_pairs={{0,2},{2,0},{1,3},{3,1},{4,6},{6,4},{5,7},{7,5},{8,10},{10,8},{9,1... | collective-permute-start | bytes 1179656 | tf_op jit(solution)/shard_map/ppermute | solution.py:193
  161.7 10.9 %collective-permute-start.22 = (bf16[384,512]{1,0:T(8,128)(2,1)S(1)}, bf16[384,512]{1,0:T(8,128)(2,1)S(1)}, u32[]{:S(2)}, u32[]{:S(2)}) collective-permute-start(bf16[384,512]{1,0:T(8,128)(2,1)S(1)} %add_convert_fusion.3), channel_id=1, source_target_pairs={{0,4},{4,8},{1,5},{5,9},{2,6},{6,10},{3,7},{7,11},{16,20},{20,24},... | collective-permute-start | bytes 1179656 | tf_op jit(solution)/shard_map/ppermute | solution.py:234
  164.8 13.0 %collective-permute-start.24 = (bf16[384,512]{1,0:T(8,128)(2,1)}, bf16[384,512]{1,0:T(8,128)(2,1)S(1)}, u32[]{:S(2)}, u32[]{:S(2)}) collective-permute-start(bf16[384,512]{1,0:T(8,128)(2,1)} %get-tuple-element.48), channel_id=1, source_target_pairs={{0,2},{2,0},{1,3},{3,1},{4,6},{6,4},{5,7},{7,5},{8,10},{10,8},{9,1... | collective-permute-start | bytes 1179656 | tf_op jit(solution)/shard_map/ppermute | solution.py:193
  165.4 12.3 %collective-permute-start.25 = (bf16[384,512]{1,0:T(8,128)(2,1)S(1)}, bf16[384,512]{1,0:T(8,128)(2,1)S(1)}, u32[]{:S(2)}, u32[]{:S(2)}) collective-permute-start(bf16[384,512]{1,0:T(8,128)(2,1)S(1)} %add_convert_fusion.3), channel_id=1, source_target_pairs={{12,8},{8,4},{13,9},{9,5},{14,10},{10,6},{15,11},{11,7},{28,24},{2... | collective-permute-start | bytes 1179656 | tf_op jit(solution)/shard_map/ppermute | solution.py:235
  166.1 19.5 %collective-permute-start.19 = (bf16[384,512]{1,0:T(8,128)(2,1)}, bf16[384,512]{1,0:T(8,128)(2,1)S(1)}, u32[]{:S(2)}, u32[]{:S(2)}) collective-permute-start(bf16[384,512]{1,0:T(8,128)(2,1)} %get-tuple-element.40), channel_id=1, source_target_pairs={{0,2},{2,0},{1,3},{3,1},{4,6},{6,4},{5,7},{7,5},{8,10},{10,8},{9,1... | collective-permute-start | bytes 1179656 | tf_op jit(solution)/shard_map/ppermute | solution.py:193
  173.7 13.9 %collective-permute-start.23 = (bf16[384,512]{1,0:T(8,128)(2,1)S(1)}, bf16[384,512]{1,0:T(8,128)(2,1)S(1)}, u32[]{:S(2)}, u32[]{:S(2)}) collective-permute-start(bf16[384,512]{1,0:T(8,128)(2,1)S(1)} %add_convert_fusion.2), channel_id=1, source_target_pairs={{0,4},{4,8},{8,12},{12,0},{1,5},{5,9},{9,13},{13,1},{2,6},{6,10},{... | collective-permute-start | bytes 1179656 | tf_op jit(solution)/shard_map/ppermute | solution.py:193
  178.9 14.6 %collective-permute-start.26 = (bf16[384,512]{1,0:T(8,128)(2,1)S(1)}, bf16[384,512]{1,0:T(8,128)(2,1)S(1)}, u32[]{:S(2)}, u32[]{:S(2)}) collective-permute-start(bf16[384,512]{1,0:T(8,128)(2,1)S(1)} %add_convert_fusion.1), channel_id=1, source_target_pairs={{0,12},{4,0},{8,4},{12,8},{1,13},{5,1},{9,5},{13,9},{2,14},{6,2},{... | collective-permute-start | bytes 1179656 | tf_op jit(solution)/shard_map/ppermute | solution.py:193

commit v6 on v5

--- a/solution.py
+++ b/solution.py
@@ -9,6 +9,7 @@
 HEADS = 64
 HEAD_DIM = 128
 ADP = ("z", "y", "core")
+GATHERED = ((0, 0), (0, 1), (3, 0), (1, 0), (3, 1), (1, 1), (2, 0), (2, 1))
 NT = (((1,), (1,)), ((), ()))
 VMEM_LIMIT = 56 << 20
 QUICK = pl.CostEstimate(flops=1, bytes_accessed=1, transcendentals=0)
@@ -197,31 +198,35 @@
     return lax.optimization_barrier((value, *others))[0]
 
 
-def gather_features(tokens, down_other, up):
+def gathered_chips():
+    layers, sides = lax.axis_size("z"), lax.axis_size("y")
+    z, y = lax.axis_index("z"), lax.axis_index("y")
+    steps = GATHERED
+    if layers != 4 or sides != 2:
+        steps = [(-k, side) for k in range(layers) for side in range(sides)]
+    return [((z + k) % layers) * sides + (y + side) % sides for k, side in steps]
+
+
+def gather_features(tokens, down_other, up, begin):
     layers, sides = lax.axis_size("z"), lax.axis_size("y")
     z = lax.axis_index("z")
     if layers != 4 or sides != 2:
-        entries = []
-        for k in range(layers):
-            block = shift(tokens, "z", k) if k else tokens
-            entries.append(((z - k) % layers, [block, shift(block, "y", 1)][:sides]))
-        return entries, down_other
+        blocks = [shift(tokens, "z", k) if k else tokens for k in range(layers)]
+        blocks = [[block, shift(block, "y", 1)][:sides] for block in blocks]
+        blocks = [block for pair in blocks for block in pair]
+        return begin(blocks[:-1]), blocks[-1:], up
     side = shift(tokens, "y", 1)
     below, above = shift(tokens, "z", 1), shift(tokens, "z", 3)
-    below, side, down_other = lax.optimization_barrier((below, side, down_other))
+    below, side, _ = lax.optimization_barrier((below, side, down_other))
     below_side = shift(below, "y", 1)
     from_below = lax.ppermute(below, "z", [(1, 2), (2, 3)])
+    above = after(above, below_side)
     above_side = shift(above, "y", 1)
     from_above = lax.ppermute(above, "z", [(2, 1), (1, 0)])
+    sums = begin([tokens, side, below, above])
+    from_above, from_below, up, sums = lax.optimization_barrier((from_above, from_below, up, sums))
     two = jnp.where(z >= 2, from_below, from_above)
-    two = after(two, below_side, up)
-    two_side = shift(two, "y", 1)
-    return [
-        (z, [tokens, side]),
-        ((z - 1) % 4, [below, below_side]),
-        ((z + 1) % 4, [above, above_side]),
-        ((z + 2) % 4, [two, two_side]),
-    ], down_other
+    return sums, [below_side, above_side, two, shift(two, "y", 1)], up
 
 
 def scatter_layers(parts):
@@ -276,21 +281,21 @@
     up = jnp.swapaxes(adapter_up_maps, 1, 2)[0]
     up = lax.dynamic_slice_in_dim(up, half * (rank // 2), rank // 2, 0)
     up = lax.all_to_all(up, ADP, split_axis=1, concat_axis=0, tiled=True)
-    up_other = lax.ppermute(up, "rep", [(i, i ^ 1) for i in range(lax.axis_size("rep"))])
-
-    entries, down_other = gather_features(tokens, down_other, up)
     out_order = [2, 1, 3, 0] if layers == 4 else list(range(1, layers)) + [0]
     out_keys = [(k, side) for k in out_order for side in reversed(range(sides))]
-    chips = [chip for layer, _ in entries for chip in chips_of(layer)]
+    chips = gathered_chips()
+    out_first = len(chips)
     chips += [chips_of(z + k)[side] for k, side in out_keys]
     places = jnp.stack([2 * chip + core for chip in chips]).astype(jnp.int32)
-    out_first = len(chips) - len(out_keys)
-
-    blocks = [block for _, pair in entries for block in pair]
-    last = len(blocks) - sides
+
     weights = query_weight, query_weight_other, down, down_other
-    sums = project(places, 0, blocks[:last], *weights, ())
-    own, sent, low = project(places, last, blocks[last:], *weights, (*sums, slot))
+    sums, blocks, up = gather_features(
+        tokens, down_other, up, lambda blocks: project(places, 0, blocks, *weights, ())
+    )
+    up_other = lax.ppermute(up, "rep", [(i, i ^ 1) for i in range(lax.axis_size("rep"))])
+    own, sent, low = project(
+        after(places, up_other), out_first - len(blocks), blocks, *weights, (*sums, slot)
+    )
 
     low = (low + shift(low, "core", 1)).astype(jnp.bfloat16)
     received = shift(sent, "core", 1)

time: 196 us -> 193 us (0.985)
  waiting for transfers between devices: 82.4 us -> 76.5 us
  starting transfers between devices: 41.9 us -> 46.6 us
    ppermute x1, waiting for transfers between devices: 10.5 us -> 4.73 us  [gather_features(): from_above = lax.ppermute(above, 'z', [(2, 1), (1, 0)])]
    ppermute x22, starting transfers between devices: 24.8 us -> 29.6 us  [shift(): lax.ppermute(value, axis, [(i, (i + by) % size) for i in range(size)])]
    ppermute x1, waiting for transfers between devices: 12.2 us -> 8.37 us  [shards(): lax.ppermute(up, 'rep', [(i, i ^ 1) for i in range(lax.axis_size('rep'))])]
    ppermute x22, waiting for transfers between devices: 44.3 us -> 48.1 us  [shift(): lax.ppermute(value, axis, [(i, (i + by) % size) for i in range(size)])]
  transfers between devices with their start and end apart: 29 -> 29, of which waited for: 17 -> 18; matrix products, arithmetic and copies ran while one was open for 11% -> 10% of each run, Pallas kernels for 10% -> 9%
where the time goes in v6:
time: 193 us; the launch traced here: 192 us
  waiting for transfers between devices  76.5 us (40%)
  starting transfers between devices  46.6 us (24%)
  Pallas kernels  28.3 us (15%)
  blocking collectives  15.5 us (8%)
  matrix products  10.4 us (5%)
  other arithmetic  8.71 us (5%)
  local copies, waits for them, and re-layouts  6.07 us (3%)
    ppermute x22, waiting for transfers between devices, shift(): lax.ppermute(value, axis, [(i, (i + by) % size) for i in range(size)])  48.1 us
    ppermute x22, starting transfers between devices, shift(): lax.ppermute(value, axis, [(i, (i + by) % size) for i in range(size)])  29.6 us
    all_to_all x1, blocking collectives, shards(): lax.all_to_all(context, ADP, split_axis=0, concat_axis=0, tiled=True)  15.5 us
    pallas_call x2, Pallas kernels, project(): pl.pallas_call(kernel, grid_spec=pltpu.PrefetchScalarGridSpec(num_scalar_...  13.8 us
    all_to_all x1, waiting for transfers between devices, shards(): lax.all_to_all(query, ADP, split_axis=0, concat_axis=1, tiled=True)  12 us
    pallas_call x2, Pallas kernels, output_partial(): pl.pallas_call(kernel, grid_spec=pltpu.PrefetchScalarGridSpec(num_scalar_...  10.9 us
    ppermute x1, waiting for transfers between devices, shards(): lax.ppermute(up, 'rep', [(i, i ^ 1) for i in range(lax.axis_size('rep'))])  8.37 us
    dot_general x1, matrix products, attention(): jnp.einsum('rkge,krje->krgj', query, key_cache, preferred_element_type=jn...  5.52 us
  transfers between devices with their start and end apart: 29, of which 18 were waited for; matrix products, arithmetic and copies ran while one was open for 10% of the time, Pallas kernels for 9%

profile of v6, /device:TPU:0, one launch (start us, length us, event | category | flops | bytes accessed | tf_op | source)
XLA Modules:
  0.0 192.5 jit_solution(4687261567662550921)
XLA Ops:
  0.0 0.5 collective-permute-start.7
  0.5 2.6 %collective-permute-start.1 = (bf16[384,512]{1,0:T(8,128)(2,1)}, bf16[384,512]{1,0:T(8,128)(2,1)S(1)}, u32[]{:S(2)}, u32[]{:S(2)}) collective-permute-start(bf16[384,512]{1,0:T(8,128)(2,1)} %refs_0_.1), channel_id=1, source_target_pairs={{0,4},{4,8},{8,12},{12,0},{1,5},{5,9},{9,13},{13,1},{2,6},{6,10},{... | collective-permute-start | bytes 1179656 | tf_op jit(solution)/shard_map/ppermute | solution.py:194
  3.1 1.5 collective-permute-start.2
  4.8 1.1 copy.36
  5.9 4.1 %all-to-all-start = ((bf16[32,16,512]{2,0,1:T(8,128)(2,1)}), bf16[32,16,512]{2,0,1:T(8,128)(2,1)S(1)}, u32[]{:S(2)}, u32[]{:S(2)}) async-start(bf16[32,16,512]{2,0,1:T(8,128)(2,1)} %copy.36), calls=%async_computation | async-start | bytes 1048576 | tf_op jit(solution)/shard_map/all_to_all | solution.py:283
  10.0 3.7 %collective-permute-start = (bf16[384,512]{1,0:T(8,128)(2,1)}, bf16[384,512]{1,0:T(8,128)(2,1)S(1)}, u32[]{:S(2)}, u32[]{:S(2)}) collective-permute-start(bf16[384,512]{1,0:T(8,128)(2,1)} %refs_0_.1), channel_id=1, source_target_pairs={{0,12},{4,0},{8,4},{12,8},{1,13},{5,1},{9,5},{13,9},{2,14},{6,2},{... | collective-permute-start | bytes 1179656 | tf_op jit(solution)/shard_map/ppermute | solution.py:194
  13.7 1.6 collective-permute-done.1.refs_2_
  15.3 2.5 %collective-permute-start.4 = (bf16[384,512]{1,0:T(8,128)(2,1)S(1)}, bf16[384,512]{1,0:T(8,128)(2,1)S(1)}, u32[]{:S(2)}, u32[]{:S(2)}) collective-permute-start(bf16[384,512]{1,0:T(8,128)(2,1)S(1)} %collective-permute-done.1.refs_2_), channel_id=1, source_target_pairs={{0,2},{2,0},{1,3},{3,1},{4,6},{6,4},{5,7},{7,5},{8,10},{10,8},{9,1... | collective-permute-start | bytes 1179656 | tf_op jit(solution)/shard_map/ppermute | solution.py:194
  17.8 1.4 collective-permute-start.6
  19.2 12.7 %collective-permute-done.refs_3_ = bf16[384,512]{1,0:T(8,128)(2,1)S(1)} collective-permute-done((bf16[384,512]{1,0:T(8,128)(2,1)}, bf16[384,512]{1,0:T(8,128)(2,1)S(1)}, u32[]{:S(2)}, u32[]{:S(2)}) %collective-permute-start) | collective-permute-done | bytes 393248 | tf_op jit(solution)/shard_map/ppermute | solution.py:194
  31.9 1.3 collective-permute-start.5
  33.3 0.6 stack.43.places
  33.9 1.5 collective-permute-start.9
  35.4 6.6 %shard_map.118 = (f32[384,512]{1,0:T(8,128)}, f32[384,512]{1,0:T(8,128)}, f32[384,128]{1,0:T(8,128)}) custom-call(s32[16]{0:T(128)} %stack.43.places, bf16[384,512]{1,0:T(8,128)(2,1)} %refs_0_.1, bf16[384,512]{1,0:T(8,128)(2,1)} %copy-done.10, bf16[384,512]{1,0:T(8,128)(2,1)} %copy-done.9, bf16[384,512]{1,0:T(8,128)(2,1)} %copy-done.11, ...), custom_call_target="tpu_custom_call" | custom-call | flops 1 | bytes 1 | tf_op jit(solution)/shard_map/pallas_call | solution.py:64
  42.0 4.7 %collective-permute-done.5 = bf16[384,512]{1,0:T(8,128)(2,1)} collective-permute-done((bf16[384,512]{1,0:T(8,128)(2,1)S(1)}, bf16[384,512]{1,0:T(8,128)(2,1)}, u32[]{:S(2)}, u32[]{:S(2)}) %collective-permute-start.5) | collective-permute-done | bytes 393248 | tf_op jit(solution)/shard_map/ppermute | solution.py:225
  46.8 1.5 collective-permute-start.8
  48.3 1.0 broadcast_select_fusion.refs_2_
  49.3 1.5 collective-permute-start.10
  51.0 0.8 broadcast_in_dim.46.refs_23_.slot
  51.8 8.4 %collective-permute-done.8.up_other = bf16[512,512]{1,0:T(8,128)(2,1)S(1)} collective-permute-done((bf16[512,512]{1,0:T(8,128)(2,1)S(1)}, bf16[512,512]{1,0:T(8,128)(2,1)S(1)}, u32[]{:S(2)}, u32[]{:S(2)}) %collective-permute-start.8) | collective-permute-done | bytes 524320 | tf_op jit(solution)/shard_map/ppermute | solution.py:295
  60.2 0.8 copy-done.13
  60.9 7.2 %shard_map.119 = (f32[384,512]{1,0:T(8,128)}, f32[384,512]{1,0:T(8,128)}, f32[192,128]{1,0:T(8,128)}) custom-call(s32[16]{0:T(128)} %stack.43.places, bf16[384,512]{1,0:T(8,128)(2,1)} %copy-done.12, bf16[384,512]{1,0:T(8,128)(2,1)} %collective-permute-done.9.refs_1_, bf16[384,512]{1,0:T(8,128)(2,1)} %copy-done.5, bf16[384,512]{1,0:T(8,128)(2,1)} %copy-done.13, ...), custom_call_target="tpu_custom_call" | custom-call | flops 1 | bytes 1 | tf_op jit(solution)/shard_map/pallas_call | solution.py:64
  68.3 1.5 collective-permute-done.12
  69.8 0.9 add_convert_fusion.4
  70.7 1.5 collective-permute-start.13
  72.2 2.6 %collective-permute-done.13 = bf16[192,128]{1,0:T(8,128)(2,1)S(1)} collective-permute-done((bf16[192,128]{1,0:T(8,128)(2,1)S(1)}, bf16[192,128]{1,0:T(8,128)(2,1)S(1)}, u32[]{:S(2)}, u32[]{:S(2)}) %collective-permute-start.13) | collective-permute-done | bytes 49184 | tf_op jit(solution)/shard_map/ppermute | solution.py:194
  74.9 1.5 collective-permute-start.14
  76.5 2.8 %collective-permute-start.16 = (bf16[192,128]{1,0:T(8,128)(2,1)S(1)}, bf16[192,128]{1,0:T(8,128)(2,1)S(1)}, u32[]{:S(2)}, u32[]{:S(2)}) collective-permute-start(bf16[192,128]{1,0:T(8,128)(2,1)S(1)} %add.217), channel_id=1, source_target_pairs={{0,12},{4,0},{8,4},{12,8},{1,13},{5,1},{9,5},{13,9},{2,14},{6,2},{... | collective-permute-start | bytes 147464 | tf_op jit(solution)/shard_map/ppermute | solution.py:194
  79.4 1.5 collective-permute-done.14
  80.9 1.1 collective-permute-done.15
  82.0 0.6 add_add_fusion.low
  82.6 0.5 collective-permute-start.11
  83.1 7.8 %collective-permute-done.11.received = f32[384,512]{1,0:T(8,128)S(1)} collective-permute-done((f32[384,512]{1,0:T(8,128)}, f32[384,512]{1,0:T(8,128)S(1)}, u32[]{:S(2)}, u32[]{:S(2)}) %collective-permute-start.11) | collective-permute-done | bytes 786464 | tf_op jit(solution)/shard_map/ppermute | solution.py:194
  91.0 0.9 copy-done.7
  91.9 3.6 %shard_map.120 = bf16[384,512]{1,0:T(8,128)(2,1)} custom-call(s32[1]{0:T(128)} %bitcast.8.half, f32[384,512]{1,0:T(8,128)} %get-tuple-element.46.own, f32[384,512]{1,0:T(8,128)} %copy-done.7, bf16[192,128]{1,0:T(8,128)(2,1)} %add_add_fusion.low, s32[384,1]{1,0:T(8,128)} %broadcast_in_dim.46.refs_23_.slot, bf16[512,512]{1,0:T(8,128)(2,1)} %bitcast.52, ...), custom_call_target="tpu_custom_call" | custom-call | flops 1 | bytes 1 | tf_op jit(solution)/shard_map/pallas_call | solution.py:115
  95.5 5.0 %all-to-all-start.1 = ((bf16[16,24,512]{2,1,0:T(8,128)(2,1)}), bf16[16,24,512]{2,1,0:T(8,128)(2,1)S(1)}, u32[]{:S(2)}, u32[]{:S(2)}) async-start(bf16[16,24,512]{2,1,0:T(8,128)(2,1)} %bitcast.55), calls=%async_computation.1 | async-start | bytes 786432 | tf_op jit(solution)/shard_map/all_to_all | solution.py:308
  100.6 12.0 %all-to-all-done.1 = bf16[16,24,512]{2,1,0:T(8,128)(2,1)S(1)} async-done(((bf16[16,24,512]{2,1,0:T(8,128)(2,1)}), bf16[16,24,512]{2,1,0:T(8,128)(2,1)S(1)}, u32[]{:S(2)}, u32[]{:S(2)}) %all-to-all-start.1) | async-done | bytes 393248 | tf_op jit(solution)/shard_map/all_to_all | solution.py:308
  113.3 5.5 %fusion.15 = (f32[8,24,8]{2,1,0:T(8,128)S(1)}, f32[8,24,8,128]{3,2,1,0:T(8,128)S(1)}) fusion(bf16[8,24,128,128]{3,2,1,0:T(8,128)(2,1)} %param.19, bf16[24,8,8,128]{3,2,1,0:T(8,128)(2,1)S(1)} %reshape.48, pred[24,128]{1,0:T(8,128)(4,1)S(1)} %iota_compare_fusion.1), kind=kOutput, calls=%fused_computation.30 | convolution fusion | flops 50723328 | bytes 7480320 | tf_op jit(solution)/shard_map/rkge,krje->krgj/dot_general | solution.py:178
  118.9 0.5 fusion.8
  119.5 4.6 %fusion.5 = bf16[24,8,8,128]{3,2,1,0:T(8,128)(2,1)S(1)} fusion(bf16[8,24,128,128]{3,2,1,0:T(8,128)(2,1)} %param.20, f32[24,8,128]{2,1,0:T(8,128)S(1)} %bitcast.58, f32[24,8,8]{2,1,0:T(8,128)S(1)} %copy.43, f32[8,24,8,128]{3,2,1,0:T(8,128)S(1)} %get-tuple-element.64, f32[8,24,8]{2,1,0:T(8,128)S(1)} %get-tuple-element.62, f32[8,24,8]{2,1,0:T(8,128)S(1)} %max.3, ...), kind=kOutput, calls=%fused_computation.4 | convolution fusion | flops 51707904 | bytes 7590912 | tf_op jit(solution)/shard_map/krgj,krje->rkge/dot_general | solution.py:187
  124.6 15.5 %all_to_all.40 = bf16[16,24,512]{2,1,0:T(8,128)(2,1)S(1)} all-to-all(bf16[16,24,512]{2,1,0:T(8,128)(2,1)S(1)} %bitcast.54), channel_id=1, replica_groups=mesh['rep'=2,'z'=4,'y'=2,'core'=2] {'z','y','core'}, dimensions={0} | all-to-all | bytes 786432 | tf_op jit(solution)/shard_map/all_to_all | solution.py:314
  140.2 1.6 collective-permute-done.17.refs_1_
  141.8 0.8 copy-done.6
  142.6 3.4 %shard_map.122 = bf16[384,512]{1,0:T(8,128)(2,1)} custom-call(s32[16]{0:T(128)} %stack.43.places, bf16[384,512]{1,0:T(8,128)(2,1)} %bitcast.47, bf16[384,512]{1,0:T(8,128)(2,1)} %copy-done.6, bf16[512,8192]{1,0:T(8,128)(2,1)} %refs_2_.3, bf16[512,8192]{1,0:T(8,128)(2,1)} %collective-permute-done.18.refs_9_.refs_10_.refs_11_.refs_12_.refs_13_.refs_14_.refs_15_.refs_3_), custom_call_target="tpu_custom_call" | custom-call | flops 1 | bytes 1 | tf_op jit(solution)/shard_map/pallas_call | solution.py:156
  146.1 0.6 collective-permute-start.21
  146.7 7.5 %shard_map.121 = (bf16[384,512]{1,0:T(8,128)(2,1)}, bf16[384,512]{1,0:T(8,128)(2,1)}, bf16[384,512]{1,0:T(8,128)(2,1)}, bf16[384,512]{1,0:T(8,128)(2,1)}, bf16[3...) custom-call(s32[16]{0:T(128)} %stack.43.places, bf16[384,512]{1,0:T(8,128)(2,1)} %bitcast.48, ...), custom_call_target="tpu_custom_call" | custom-call | flops 1 | bytes 1 | tf_op jit(solution)/shard_map/pallas_call | solution.py:156
  154.1 1.5 collective-permute-start.20
  155.6 2.1 %collective-permute-done.21 = bf16[384,512]{1,0:T(8,128)(2,1)S(1)} collective-permute-done((bf16[384,512]{1,0:T(8,128)(2,1)}, bf16[384,512]{1,0:T(8,128)(2,1)S(1)}, u32[]{:S(2)}, u32[]{:S(2)}) %collective-permute-start.21) | collective-permute-done | bytes 393248 | tf_op jit(solution)/shard_map/ppermute | solution.py:194
  157.7 1.1 add_convert_fusion.3
  158.8 3.1 %collective-permute-start.22 = (bf16[384,512]{1,0:T(8,128)(2,1)S(1)}, bf16[384,512]{1,0:T(8,128)(2,1)S(1)}, u32[]{:S(2)}, u32[]{:S(2)}) collective-permute-start(bf16[384,512]{1,0:T(8,128)(2,1)S(1)} %add_convert_fusion.3), channel_id=1, source_target_pairs={{0,4},{4,8},{1,5},{5,9},{2,6},{6,10},{3,7},{7,11},{16,20},{20,24},... | collective-permute-start | bytes 1179656 | tf_op jit(solution)/shard_map/ppermute | solution.py:239
  161.9 0.6 collective-permute-start.24
  162.5 0.7 collective-permute-start.25
  163.2 1.5 collective-permute-start.19
  164.7 1.7 collective-permute-done.20
  166.4 3.3 %collective-permute-done.22 = bf16[384,512]{1,0:T(8,128)(2,1)S(1)} collective-permute-done((bf16[384,512]{1,0:T(8,128)(2,1)S(1)}, bf16[384,512]{1,0:T(8,128)(2,1)S(1)}, u32[]{:S(2)}, u32[]{:S(2)}) %collective-permute-start.22) | collective-permute-done | bytes 393248 | tf_op jit(solution)/shard_map/ppermute | solution.py:239
  169.6 1.1 add_convert_fusion.2
  170.8 2.5 %collective-permute-start.23 = (bf16[384,512]{1,0:T(8,128)(2,1)S(1)}, bf16[384,512]{1,0:T(8,128)(2,1)S(1)}, u32[]{:S(2)}, u32[]{:S(2)}) collective-permute-start(bf16[384,512]{1,0:T(8,128)(2,1)S(1)} %add_convert_fusion.2), channel_id=1, source_target_pairs={{0,4},{4,8},{8,12},{12,0},{1,5},{5,9},{9,13},{13,1},{2,6},{6,10},{... | collective-permute-start | bytes 1179656 | tf_op jit(solution)/shard_map/ppermute | solution.py:194
  173.3 1.5 collective-permute-done.24
  174.8 1.1 add_convert_fusion.1
  175.9 2.2 %collective-permute-start.26 = (bf16[384,512]{1,0:T(8,128)(2,1)S(1)}, bf16[384,512]{1,0:T(8,128)(2,1)S(1)}, u32[]{:S(2)}, u32[]{:S(2)}) collective-permute-start(bf16[384,512]{1,0:T(8,128)(2,1)S(1)} %add_convert_fusion.1), channel_id=1, source_target_pairs={{0,12},{4,0},{8,4},{12,8},{1,13},{5,1},{9,5},{13,9},{2,14},{6,2},{... | collective-permute-start | bytes 1179656 | tf_op jit(solution)/shard_map/ppermute | solution.py:194
  178.1 4.6 %collective-permute-done.19 = bf16[384,512]{1,0:T(8,128)(2,1)S(1)} collective-permute-done((bf16[384,512]{1,0:T(8,128)(2,1)}, bf16[384,512]{1,0:T(8,128)(2,1)S(1)}, u32[]{:S(2)}, u32[]{:S(2)}) %collective-permute-start.19) | collective-permute-done | bytes 393248 | tf_op jit(solution)/shard_map/ppermute | solution.py:194
  182.7 2.0 %collective-permute-done.23 = bf16[384,512]{1,0:T(8,128)(2,1)S(1)} collective-permute-done((bf16[384,512]{1,0:T(8,128)(2,1)S(1)}, bf16[384,512]{1,0:T(8,128)(2,1)S(1)}, u32[]{:S(2)}, u32[]{:S(2)}) %collective-permute-start.23) | collective-permute-done | bytes 393248 | tf_op jit(solution)/shard_map/ppermute | solution.py:194
  184.7 5.8 %collective-permute-done.26 = bf16[384,512]{1,0:T(8,128)(2,1)S(1)} collective-permute-done((bf16[384,512]{1,0:T(8,128)(2,1)S(1)}, bf16[384,512]{1,0:T(8,128)(2,1)S(1)}, u32[]{:S(2)}, u32[]{:S(2)}) %collective-permute-start.26) | collective-permute-done | bytes 393248 | tf_op jit(solution)/shard_map/ppermute | solution.py:194
  190.5 1.9 %add_convert_fusion = bf16[384,512]{1,0:T(8,128)(2,1)} fusion(bf16[384,512]{1,0:T(8,128)(2,1)S(1)} %collective-permute-done.26, bf16[384,512]{1,0:T(8,128)(2,1)S(1)} %collective-permute-done.23, bf16[384,512]{1,0:T(8,128)(2,1)S(1)} %collective-permute-done.19, bf16[384,512]{1,0:T(8,128)(2,1)} %get-tuple-element.51), kind=kLoop, calls=%fused_computation.5 | loop fusion | flops 1572864 | bytes 1966080 | tf_op jit(solution)/shard_map/convert_element_type | solution.py:337
  (68 shorter events, 2.2 us)
Async XLA Ops:
  0.0 4.6 %copy-start = (bf16[1,8192,64]{1,2,0:T(8,128)(2,1)S(1)}, bf16[1,8192,64]{1,2,0:T(8,128)(2,1)}, u32[]{:S(2)}) copy-start(bf16[1,8192,64]{1,2,0:T(8,128)(2,1)} %param.18) | copy-start | bytes 3145732
  0.0 35.4 %collective-permute-start.7 = (bf16[8192,512]{1,0:T(8,128)(2,1)}, bf16[8192,512]{1,0:T(8,128)(2,1)}, u32[]{:S(2)}, u32[]{:S(2)}) collective-permute-start(bf16[8192,512]{1,0:T(8,128)(2,1)} %refs_7_.4), channel_id=1, source_target_pairs={{0,1},{1,0},{2,3},{3,2},{4,5},{5,4},{6,7},{7,6},{8,9},{9,8},{10,11... | collective-permute-start | bytes 25165832 | tf_op jit(solution)/shard_map/ppermute | solution.py:194
  0.5 14.8 %collective-permute-start.1 = (bf16[384,512]{1,0:T(8,128)(2,1)}, bf16[384,512]{1,0:T(8,128)(2,1)S(1)}, u32[]{:S(2)}, u32[]{:S(2)}) collective-permute-start(bf16[384,512]{1,0:T(8,128)(2,1)} %refs_0_.1), channel_id=1, source_target_pairs={{0,4},{4,8},{8,12},{12,0},{1,5},{5,9},{9,13},{13,1},{2,6},{6,10},{... | collective-permute-start | bytes 1179656 | tf_op jit(solution)/shard_map/ppermute | solution.py:194
  3.1 12.2 %collective-permute-start.2 = (bf16[384,512]{1,0:T(8,128)(2,1)}, bf16[384,512]{1,0:T(8,128)(2,1)S(1)}, u32[]{:S(2)}, u32[]{:S(2)}) collective-permute-start(bf16[384,512]{1,0:T(8,128)(2,1)} %refs_0_.1), channel_id=1, source_target_pairs={{0,2},{2,0},{1,3},{3,1},{4,6},{6,4},{5,7},{7,5},{8,10},{10,8},{9,1... | collective-permute-start | bytes 1179656 | tf_op jit(solution)/shard_map/ppermute | solution.py:194
  4.6 10.7 %collective-permute-start.3 = (bf16[1,64,8192]{2,1,0:T(8,128)(2,1)}, bf16[1,64,8192]{2,1,0:T(8,128)(2,1)S(1)}, u32[]{:S(2)}, u32[]{:S(2)}) collective-permute-start(bf16[1,64,8192]{2,1,0:T(8,128)(2,1)} %bitcast.37), channel_id=1, source_target_pairs={{0,1},{1,0},{2,3},{3,2},{4,5},{5,4},{6,7},{7,6},{8,9},{9,8},{10,11... | collective-permute-start | bytes 3145736 | tf_op jit(solution)/shard_map/ppermute | solution.py:194
  5.9 36.1 %all-to-all-start = ((bf16[32,16,512]{2,0,1:T(8,128)(2,1)}), bf16[32,16,512]{2,0,1:T(8,128)(2,1)S(1)}, u32[]{:S(2)}, u32[]{:S(2)}) async-start(bf16[32,16,512]{2,0,1:T(8,128)(2,1)} %copy.36), calls=%async_computation | async-start | bytes 1048576 | tf_op jit(solution)/shard_map/all_to_all | solution.py:283
  10.0 21.9 %collective-permute-start = (bf16[384,512]{1,0:T(8,128)(2,1)}, bf16[384,512]{1,0:T(8,128)(2,1)S(1)}, u32[]{:S(2)}, u32[]{:S(2)}) collective-permute-start(bf16[384,512]{1,0:T(8,128)(2,1)} %refs_0_.1), channel_id=1, source_target_pairs={{0,12},{4,0},{8,4},{12,8},{1,13},{5,1},{9,5},{13,9},{2,14},{6,2},{... | collective-permute-start | bytes 1179656 | tf_op jit(solution)/shard_map/ppermute | solution.py:194
  15.3 20.1 %copy-start.9 = (bf16[384,512]{1,0:T(8,128)(2,1)}, bf16[384,512]{1,0:T(8,128)(2,1)S(1)}, u32[]{:S(2)}) copy-start(bf16[384,512]{1,0:T(8,128)(2,1)S(1)} %collective-permute-done.1.refs_2_) | copy-start | bytes 1179652
  15.3 20.1 %copy-start.10 = (bf16[384,512]{1,0:T(8,128)(2,1)}, bf16[384,512]{1,0:T(8,128)(2,1)S(1)}, u32[]{:S(2)}) copy-start(bf16[384,512]{1,0:T(8,128)(2,1)S(1)} %collective-permute-done.2.refs_1_) | copy-start | bytes 1179652
  15.3 20.1 %copy-start.2 = (bf16[1,64,8192]{2,1,0:T(8,128)(2,1)}, bf16[1,64,8192]{2,1,0:T(8,128)(2,1)S(1)}, u32[]{:S(2)}) copy-start(bf16[1,64,8192]{2,1,0:T(8,128)(2,1)S(1)} %collective-permute-done.3.refs_16_.refs_17_.refs_18_.refs_19_) | copy-start | bytes 3145732
  15.3 16.6 %collective-permute-start.4 = (bf16[384,512]{1,0:T(8,128)(2,1)S(1)}, bf16[384,512]{1,0:T(8,128)(2,1)S(1)}, u32[]{:S(2)}, u32[]{:S(2)}) collective-permute-start(bf16[384,512]{1,0:T(8,128)(2,1)S(1)} %collective-permute-done.1.refs_2_), channel_id=1, source_target_pairs={{0,2},{2,0},{1,3},{3,1},{4,6},{6,4},{5,7},{7,5},{8,10},{10,8},{9,1... | collective-permute-start | bytes 1179656 | tf_op jit(solution)/shard_map/ppermute | solution.py:194
  17.8 24.2 %collective-permute-start.6 = (bf16[384,512]{1,0:T(8,128)(2,1)S(1)}, bf16[384,512]{1,0:T(8,128)(2,1)}, u32[]{:S(2)}, u32[]{:S(2)}) collective-permute-start(bf16[384,512]{1,0:T(8,128)(2,1)S(1)} %collective-permute-done.1.refs_2_), channel_id=1, source_target_pairs={{4,8},{8,12},{5,9},{9,13},{6,10},{10,14},{7,11},{11,15},{20,24},{2... | collective-permute-start | bytes 1179656 | tf_op jit(solution)/shard_map/ppermute | solution.py:222
  31.9 3.5 %copy-start.11 = (bf16[384,512]{1,0:T(8,128)(2,1)}, bf16[384,512]{1,0:T(8,128)(2,1)S(1)}, u32[]{:S(2)}) copy-start(bf16[384,512]{1,0:T(8,128)(2,1)S(1)} %collective-permute-done.refs_3_) | copy-start | bytes 1179652
  31.9 10.1 %copy-start.12 = (bf16[384,512]{1,0:T(8,128)(2,1)}, bf16[384,512]{1,0:T(8,128)(2,1)S(1)}, u32[]{:S(2)}) copy-start(bf16[384,512]{1,0:T(8,128)(2,1)S(1)} %collective-permute-done.4.refs_0_) | copy-start | bytes 1179652
  31.9 14.9 %collective-permute-start.5 = (bf16[384,512]{1,0:T(8,128)(2,1)S(1)}, bf16[384,512]{1,0:T(8,128)(2,1)}, u32[]{:S(2)}, u32[]{:S(2)}) collective-permute-start(bf16[384,512]{1,0:T(8,128)(2,1)S(1)} %collective-permute-done.refs_3_), channel_id=1, source_target_pairs={{8,4},{4,0},{9,5},{5,1},{10,6},{6,2},{11,7},{7,3},{24,20},{20,16},... | collective-permute-start | bytes 1179656 | tf_op jit(solution)/shard_map/ppermute | solution.py:225
  33.9 17.0 %copy-start.16 = (s32[384,1]{0,1:T(1,128)S(1)}, s32[384,1]{0,1:T(1,128)}, u32[]{:S(2)}) copy-start(s32[384,1]{0,1:T(1,128)} %param.13) | copy-start | bytes 4612
  33.9 17.0 %copy-start.17 = (s32[16]{0:T(128)S(1)}, s32[16]{0:T(128)}, u32[]{:S(2)}) copy-start(s32[16]{0:T(128)} %param.14) | copy-start | bytes 196
  33.9 26.3 %collective-permute-start.9 = (bf16[384,512]{1,0:T(8,128)(2,1)S(1)}, bf16[384,512]{1,0:T(8,128)(2,1)}, u32[]{:S(2)}, u32[]{:S(2)}) collective-permute-start(bf16[384,512]{1,0:T(8,128)(2,1)S(1)} %collective-permute-done.refs_3_), channel_id=1, source_target_pairs={{0,2},{2,0},{1,3},{3,1},{4,6},{6,4},{5,7},{7,5},{8,10},{10,8},{9,1... | collective-permute-start | bytes 1179656 | tf_op jit(solution)/shard_map/ppermute | solution.py:194
  42.0 26.2 %copy-start.4 = (bf16[32,16,512]{2,0,1:T(8,128)(2,1)}, bf16[32,16,512]{2,0,1:T(8,128)(2,1)S(1)}, u32[]{:S(2)}) copy-start(bf16[32,16,512]{2,0,1:T(8,128)(2,1)S(1)} %all-to-all-done) | copy-start | bytes 1572868
  46.8 13.4 %collective-permute-start.8 = (bf16[512,512]{1,0:T(8,128)(2,1)S(1)}, bf16[512,512]{1,0:T(8,128)(2,1)S(1)}, u32[]{:S(2)}, u32[]{:S(2)}) collective-permute-start(bf16[512,512]{1,0:T(8,128)(2,1)S(1)} %bitcast.51), channel_id=1, source_target_pairs={{0,16},{16,0},{1,17},{17,1},{2,18},{18,2},{3,19},{19,3},{4,20},{20... | collective-permute-start | bytes 1572872 | tf_op jit(solution)/shard_map/ppermute | solution.py:295
  49.3 10.9 %copy-start.5 = (bf16[384,512]{1,0:T(8,128)(2,1)}, bf16[384,512]{1,0:T(8,128)(2,1)S(1)}, u32[]{:S(2)}) copy-start(bf16[384,512]{1,0:T(8,128)(2,1)S(1)} %broadcast_select_fusion.refs_2_) | copy-start | bytes 1179652
  49.3 10.8 %collective-permute-start.10 = (bf16[384,512]{1,0:T(8,128)(2,1)S(1)}, bf16[384,512]{1,0:T(8,128)(2,1)S(1)}, u32[]{:S(2)}, u32[]{:S(2)}) collective-permute-start(bf16[384,512]{1,0:T(8,128)(2,1)S(1)} %broadcast_select_fusion.refs_2_), channel_id=1, source_target_pairs={{0,2},{2,0},{1,3},{3,1},{4,6},{6,4},{5,7},{7,5},{8,10},{10,8},{9,1... | collective-permute-start | bytes 1179656 | tf_op jit(solution)/shard_map/ppermute | solution.py:194
  51.8 48.7 %copy-start.14 = (bf16[24,1024]{1,0:T(8,128)(2,1)S(1)}, bf16[24,1024]{1,0:T(8,128)(2,1)}, u32[]{:S(2)}) copy-start(bf16[24,1024]{1,0:T(8,128)(2,1)} %param.21) | copy-start | bytes 147460
  51.8 48.7 %copy-start.15 = (bf16[24,1024]{1,0:T(8,128)(2,1)S(1)}, bf16[24,1024]{1,0:T(8,128)(2,1)}, u32[]{:S(2)}) copy-start(bf16[24,1024]{1,0:T(8,128)(2,1)} %param.22) | copy-start | bytes 147460
  51.8 48.8 %copy-start.18 = (s32[24]{0:T(128)S(1)}, s32[24]{0:T(128)}, u32[]{:S(2)}) copy-start(s32[24]{0:T(128)} %param.15) | copy-start | bytes 292
  60.1 8.0 %copy-start.8 = (bf16[512,512]{1,0:T(8,128)(2,1)}, bf16[512,512]{1,0:T(8,128)(2,1)S(1)}, u32[]{:S(2)}) copy-start(bf16[512,512]{1,0:T(8,128)(2,1)S(1)} %collective-permute-done.8.up_other) | copy-start | bytes 1572868
  60.2 0.8 copy-start.13
  68.2 1.6 collective-permute-start.12
  70.7 4.2 %collective-permute-start.13 = (bf16[192,128]{1,0:T(8,128)(2,1)S(1)}, bf16[192,128]{1,0:T(8,128)(2,1)S(1)}, u32[]{:S(2)}, u32[]{:S(2)}) collective-permute-start(bf16[192,128]{1,0:T(8,128)(2,1)S(1)} %add_convert_fusion.4), channel_id=1, source_target_pairs={{0,2},{2,0},{1,3},{3,1},{4,6},{6,4},{5,7},{7,5},{8,10},{10,8},{9,1... | collective-permute-start | bytes 147464 | tf_op jit(solution)/shard_map/ppermute | solution.py:194
  74.9 6.0 %collective-permute-start.14 = (bf16[192,128]{1,0:T(8,128)(2,1)S(1)}, bf16[192,128]{1,0:T(8,128)(2,1)S(1)}, u32[]{:S(2)}, u32[]{:S(2)}) collective-permute-start(bf16[192,128]{1,0:T(8,128)(2,1)S(1)} %add.217), channel_id=1, source_target_pairs={{0,4},{4,8},{8,12},{12,0},{1,5},{5,9},{9,13},{13,1},{2,6},{6,10},{... | collective-permute-start | bytes 147464 | tf_op jit(solution)/shard_map/ppermute | solution.py:194
  76.3 5.7 %collective-permute-start.15 = (bf16[192,128]{1,0:T(8,128)(2,1)S(1)}, bf16[192,128]{1,0:T(8,128)(2,1)S(1)}, u32[]{:S(2)}, u32[]{:S(2)}) collective-permute-start(bf16[192,128]{1,0:T(8,128)(2,1)S(1)} %add.217), channel_id=1, source_target_pairs={{0,8},{4,12},{8,0},{12,4},{1,9},{5,13},{9,1},{13,5},{2,10},{6,14},... | collective-permute-start | bytes 147464 | tf_op jit(solution)/shard_map/ppermute | solution.py:194
  76.5 5.5 %collective-permute-start.16 = (bf16[192,128]{1,0:T(8,128)(2,1)S(1)}, bf16[192,128]{1,0:T(8,128)(2,1)S(1)}, u32[]{:S(2)}, u32[]{:S(2)}) collective-permute-start(bf16[192,128]{1,0:T(8,128)(2,1)S(1)} %add.217), channel_id=1, source_target_pairs={{0,12},{4,0},{8,4},{12,8},{1,13},{5,1},{9,5},{13,9},{2,14},{6,2},{... | collective-permute-start | bytes 147464 | tf_op jit(solution)/shard_map/ppermute | solution.py:194
  82.6 59.2 %collective-permute-start.18 = (bf16[512,8192]{1,0:T(8,128)(2,1)}, bf16[512,8192]{1,0:T(8,128)(2,1)}, u32[]{:S(2)}, u32[]{:S(2)}) collective-permute-start(bf16[512,8192]{1,0:T(8,128)(2,1)} %refs_2_.3), channel_id=1, source_target_pairs={{0,1},{1,0},{2,3},{3,2},{4,5},{5,4},{6,7},{7,6},{8,9},{9,8},{10,11... | collective-permute-start | bytes 25165832 | tf_op jit(solution)/shard_map/ppermute | solution.py:194
  82.6 8.3 %collective-permute-start.11 = (f32[384,512]{1,0:T(8,128)}, f32[384,512]{1,0:T(8,128)S(1)}, u32[]{:S(2)}, u32[]{:S(2)}) collective-permute-start(f32[384,512]{1,0:T(8,128)} %get-tuple-element.47), channel_id=1, source_target_pairs={{0,1},{1,0},{2,3},{3,2},{4,5},{5,4},{6,7},{7,6},{8,9},{9,8},{10,11... | collective-permute-start | bytes 2359304 | tf_op jit(solution)/shard_map/ppermute | solution.py:194
  91.0 0.9 copy-start.7
  95.5 17.2 %all-to-all-start.1 = ((bf16[16,24,512]{2,1,0:T(8,128)(2,1)}), bf16[16,24,512]{2,1,0:T(8,128)(2,1)S(1)}, u32[]{:S(2)}, u32[]{:S(2)}) async-start(bf16[16,24,512]{2,1,0:T(8,128)(2,1)} %bitcast.55), calls=%async_computation.1 | async-start | bytes 786432 | tf_op jit(solution)/shard_map/all_to_all | solution.py:308
  140.1 1.7 copy-start.3
  140.1 1.7 collective-permute-start.17
  141.8 0.8 copy-start.6
  146.1 11.6 %collective-permute-start.21 = (bf16[384,512]{1,0:T(8,128)(2,1)}, bf16[384,512]{1,0:T(8,128)(2,1)S(1)}, u32[]{:S(2)}, u32[]{:S(2)}) collective-permute-start(bf16[384,512]{1,0:T(8,128)(2,1)} %shard_map.122), channel_id=1, source_target_pairs={{0,2},{2,0},{1,3},{3,1},{4,6},{6,4},{5,7},{7,5},{8,10},{10,8},{9,1... | collective-permute-start | bytes 1179656 | tf_op jit(solution)/shard_map/ppermute | solution.py:194
  146.7 45.8 %copy-start.1 = (bf16[1,8192,64]{1,2,0:T(8,128)(2,1)S(1)}, bf16[1,8192,64]{1,2,0:T(8,128)(2,1)}, u32[]{:S(2)}) copy-start(bf16[1,8192,64]{1,2,0:T(8,128)(2,1)} %param.18) | copy-start | bytes 3145732
  154.1 12.2 %collective-permute-start.20 = (bf16[384,512]{1,0:T(8,128)(2,1)}, bf16[384,512]{1,0:T(8,128)(2,1)S(1)}, u32[]{:S(2)}, u32[]{:S(2)}) collective-permute-start(bf16[384,512]{1,0:T(8,128)(2,1)} %get-tuple-element.55), channel_id=1, source_target_pairs={{0,2},{2,0},{1,3},{3,1},{4,6},{6,4},{5,7},{7,5},{8,10},{10,8},{9,1... | collective-permute-start | bytes 1179656 | tf_op jit(solution)/shard_map/ppermute | solution.py:194
  158.8 10.8 %collective-permute-start.22 = (bf16[384,512]{1,0:T(8,128)(2,1)S(1)}, bf16[384,512]{1,0:T(8,128)(2,1)S(1)}, u32[]{:S(2)}, u32[]{:S(2)}) collective-permute-start(bf16[384,512]{1,0:T(8,128)(2,1)S(1)} %add_convert_fusion.3), channel_id=1, source_target_pairs={{0,4},{4,8},{1,5},{5,9},{2,6},{6,10},{3,7},{7,11},{16,20},{20,24},... | collective-permute-start | bytes 1179656 | tf_op jit(solution)/shard_map/ppermute | solution.py:239
  161.9 12.9 %collective-permute-start.24 = (bf16[384,512]{1,0:T(8,128)(2,1)}, bf16[384,512]{1,0:T(8,128)(2,1)S(1)}, u32[]{:S(2)}, u32[]{:S(2)}) collective-permute-start(bf16[384,512]{1,0:T(8,128)(2,1)} %get-tuple-element.60), channel_id=1, source_target_pairs={{0,2},{2,0},{1,3},{3,1},{4,6},{6,4},{5,7},{7,5},{8,10},{10,8},{9,1... | collective-permute-start | bytes 1179656 | tf_op jit(solution)/shard_map/ppermute | solution.py:194
  162.5 12.3 %collective-permute-start.25 = (bf16[384,512]{1,0:T(8,128)(2,1)S(1)}, bf16[384,512]{1,0:T(8,128)(2,1)S(1)}, u32[]{:S(2)}, u32[]{:S(2)}) collective-permute-start(bf16[384,512]{1,0:T(8,128)(2,1)S(1)} %add_convert_fusion.3), channel_id=1, source_target_pairs={{12,8},{8,4},{13,9},{9,5},{14,10},{10,6},{15,11},{11,7},{28,24},{2... | collective-permute-start | bytes 1179656 | tf_op jit(solution)/shard_map/ppermute | solution.py:240
  163.2 19.5 %collective-permute-start.19 = (bf16[384,512]{1,0:T(8,128)(2,1)}, bf16[384,512]{1,0:T(8,128)(2,1)S(1)}, u32[]{:S(2)}, u32[]{:S(2)}) collective-permute-start(bf16[384,512]{1,0:T(8,128)(2,1)} %get-tuple-element.52), channel_id=1, source_target_pairs={{0,2},{2,0},{1,3},{3,1},{4,6},{6,4},{5,7},{7,5},{8,10},{10,8},{9,1... | collective-permute-start | bytes 1179656 | tf_op jit(solution)/shard_map/ppermute | solution.py:194
  170.8 13.9 %collective-permute-start.23 = (bf16[384,512]{1,0:T(8,128)(2,1)S(1)}, bf16[384,512]{1,0:T(8,128)(2,1)S(1)}, u32[]{:S(2)}, u32[]{:S(2)}) collective-permute-start(bf16[384,512]{1,0:T(8,128)(2,1)S(1)} %add_convert_fusion.2), channel_id=1, source_target_pairs={{0,4},{4,8},{8,12},{12,0},{1,5},{5,9},{9,13},{13,1},{2,6},{6,10},{... | collective-permute-start | bytes 1179656 | tf_op jit(solution)/shard_map/ppermute | solution.py:194
  175.9 14.6 %collective-permute-start.26 = (bf16[384,512]{1,0:T(8,128)(2,1)S(1)}, bf16[384,512]{1,0:T(8,128)(2,1)S(1)}, u32[]{:S(2)}, u32[]{:S(2)}) collective-permute-start(bf16[384,512]{1,0:T(8,128)(2,1)S(1)} %add_convert_fusion.1), channel_id=1, source_target_pairs={{0,12},{4,0},{8,4},{12,8},{1,13},{5,1},{9,5},{13,9},{2,14},{6,2},{... | collective-permute-start | bytes 1179656 | tf_op jit(solution)/shard_map/ppermute | solution.py:194
